TPU v7x, 128 devices: a whole 4x4x4 slice. The times are simulated.
128 devices in a mesh: grp: 8 (over x, core), mem: 16 (over z, y).
Axes of the slice: x: 4, y: 4, z: 4, core: 2. Of those that a mesh axis runs over, the one named last changes fastest.
Arguments:
- embeddings: bfloat16 [65536, 768], P(('grp', 'mem')), may hold values from -1500 to 1500
- cluster_id: int32 [65536], P(('grp', 'mem')), may hold values from 0 to 7, as said below
- row_order: int32 [65536], P(('grp', 'mem')), may hold values from 0 to 65535, each once
- assignment: int32 [8], replicated, may hold values from 0 to 7, as said below
- placement: int32 [65536], P(('grp', 'mem')), may hold values from 0 to 15
Outputs:
- owner_best: float32 [131072], P(('grp', 'mem'))
Inputs may be any that keep to these rules, and one draw needn't show every extreme that they name: `cluster_id`: owner = assignment * 16 + placement; at most 8 rows of one device share an owner, and in every draw some owner gets exactly 8 rows from every device. `assignment`: each group owns exactly 1 cluster.
All inputs are finite; a program needn't handle non-finite values.
Results may differ from a plain program's by a relative error of at most 0.00034.
Values may be sent and summed in bfloat16 or wider, within the bound.
No kernel may reach another device: no remote copies, remote signals or barrier semaphores. Data moves between devices by JAX's collectives and lax.ppermute only.
A program may use at most 128 MiB of HBM per device.

v0:
```python
import math

import jax
import jax.numpy as jnp
from jax import lax
from jax.sharding import PartitionSpec as P


def pair_tile(own_rows, piece_rows):
    own_units, own_cluster, own_order = own_rows
    piece_units, piece_cluster, piece_order = piece_rows
    own_count = own_units.shape[0]
    block_rows = 512
    blocks = own_count // block_rows

    def block_max(packed):
        block_units, block_cluster, block_order = packed
        scores = jnp.einsum(
            "ik,jk->ij", block_units, piece_units, preferred_element_type=jnp.float32
        )
        same_cluster = (block_cluster[:, None] == piece_cluster[None, :]) & (
            block_cluster[:, None] >= 0
        )
        row_best = jnp.max(
            jnp.where(same_cluster & (piece_order[None, :] < block_order[:, None]), scores, -2.0),
            axis=1,
        )
        return row_best

    packed = (
        own_units.reshape(blocks, block_rows, own_units.shape[1]),
        own_cluster.reshape(blocks, block_rows),
        own_order.reshape(blocks, block_rows),
    )
    return lax.map(block_max, packed).reshape(own_count)


def local(embeddings, cluster_id, row_order, assignment, placement):
    members = lax.axis_size("mem")
    groups = lax.axis_size("grp")
    owners = groups * members
    row_count = embeddings.shape[0]
    feature_count = embeddings.shape[1]
    capacity = max(2, 2 * row_count // owners)
    slot_count = owners * capacity
    widened = embeddings.astype(jnp.float32)
    unit_rows = (
        widened
        * lax.rsqrt(jnp.mean(widened * widened, axis=1, keepdims=True) + 1e-06)
        * (1.0 / math.sqrt(feature_count))
    ).astype(jnp.bfloat16)
    table_hits = cluster_id[:, None] == jnp.arange(assignment.shape[0], dtype=jnp.int32)[None, :]
    group_of = jnp.sum(jnp.where(table_hits, assignment[None, :], 0), axis=1)
    owner_id = group_of * members + placement
    owner_hits = (owner_id[:, None] == jnp.arange(owners, dtype=jnp.int32)[None, :]).astype(
        jnp.int32
    )
    rank_in_source = jnp.sum((jnp.cumsum(owner_hits, axis=0) - 1) * owner_hits, axis=1)
    target = owner_id * capacity + rank_in_source
    send_units = jnp.zeros((slot_count, feature_count), jnp.bfloat16).at[target].set(unit_rows)
    send_cluster = jnp.full((slot_count,), -1, jnp.int32).at[target].set(cluster_id)
    send_order = jnp.zeros((slot_count,), jnp.int32).at[target].set(row_order)
    got_units, got_cluster, got_order = (
        lax.all_to_all(send_units, ("grp", "mem"), split_axis=0, concat_axis=0, tiled=True),
        lax.all_to_all(send_cluster, ("grp", "mem"), split_axis=0, concat_axis=0, tiled=True),
        lax.all_to_all(send_order, ("grp", "mem"), split_axis=0, concat_axis=0, tiled=True),
    )
    own_rows = (got_units, got_cluster, got_order)
    piece = (
        lax.all_gather(own_rows[0], "mem", axis=0, tiled=True),
        lax.all_gather(own_rows[1], "mem", axis=0, tiled=True),
        lax.all_gather(own_rows[2], "mem", axis=0, tiled=True),
    )
    piece_count = piece[0].shape[0]
    shards = piece_count // slot_count
    split_piece = (
        piece[0].reshape(shards, slot_count, feature_count),
        piece[1].reshape(shards, slot_count),
        piece[2].reshape(shards, slot_count),
    )

    def through(carried, shard_rows):
        return (jnp.maximum(carried, pair_tile(own_rows, shard_rows)), None)

    best = lax.scan(through, jnp.full((slot_count,), -2.0, jnp.float32), split_piece)[0]
    return jnp.maximum(best, -1.0)


def solution(mesh):
    return jax.shard_map(
        local,
        mesh=mesh,
        in_specs=(
            P(("grp", "mem"), None),
            P(("grp", "mem")),
            P(("grp", "mem")),
            P(),
            P(("grp", "mem")),
        ),
        out_specs=P(("grp", "mem")),
        check_vma=False,
    )
```

profile of v0, /device:TPU:0, one launch (start us, length us, event | category | flops | bytes accessed | tf_op | source)
XLA Modules:
  0.0 275.7 jit_solution(13633355521372279465)
XLA Ops:
  9.0 3.1 %scatter_custom_fusion = bf16[1024,768]{1,0:T(8,128)(2,1)S(1)} fusion(s32[512]{0:T(512)S(1)} %compare_select_fusion, bf16[512,768]{1,0:T(8,128)(2,1)S(1)} %copy-done.1, f32[]{:T(128)} %constant.61.clone.1, f32[512]{0:T(512)S(1)} %add_rsqrt_fusion, bf16[]{:T(256)} %constant.32.clone.1), kind=kCustom, calls=%fused_computation.19 | custom fusion | flops 1572864 | bytes 2361350 | tf_op jit(solution)/shard_map/scatter | solution.py:60
  12.1 35.5 %all_to_all.36 = bf16[128,8,768]{2,1,0:T(8,128)(2,1)} all-to-all(bf16[128,8,768]{2,1,0:T(8,128)(2,1)S(1)} %bitcast.62), channel_id=1, replica_groups=mesh['grp'=8,'mem'=16] {'grp','mem'}, dimensions={0} | all-to-all | bytes 3145728 | tf_op jit(solution)/shard_map/all_to_all | solution.py:64
  47.7 2.7 scatter_custom_fusion.1
  51.1 4.5 %all-to-all-start.1 = ((s32[128,8,1]{1,2,0:T(1,128)}), s32[128,8,1]{1,2,0:T(1,128)S(1)}, u32[]{:S(2)}, u32[]{:S(2)}) async-start(s32[128,8,1]{1,2,0:T(1,128)} %bitcast.10), calls=%async_computation.1 | async-start | bytes 131072 | tf_op jit(solution)/shard_map/all_to_all | solution.py:65
  55.7 2.6 scatter_custom_fusion.2
  59.0 6.2 %all-to-all-done.1 = s32[128,8,1]{1,2,0:T(1,128)S(1)} async-done(((s32[128,8,1]{1,2,0:T(1,128)}), s32[128,8,1]{1,2,0:T(1,128)S(1)}, u32[]{:S(2)}, u32[]{:S(2)}) %all-to-all-start.1) | async-done | bytes 4128 | tf_op jit(solution)/shard_map/all_to_all | solution.py:65
  65.2 4.6 %all-to-all-start.2 = ((s32[128,8,1]{1,2,0:T(1,128)}), s32[128,8,1]{1,2,0:T(1,128)S(1)}, u32[]{:S(2)}, u32[]{:S(2)}) async-start(s32[128,8,1]{1,2,0:T(1,128)} %bitcast.11), calls=%async_computation.2 | async-start | bytes 131072 | tf_op jit(solution)/shard_map/all_to_all | solution.py:66
  71.1 23.8 %all_gather.10 = s32[16384]{0:T(1024)S(1)} all-gather(s32[1024]{0:T(1024)S(1)} %all_to_all.29), channel_id=1, replica_groups=mesh['grp'=8,'mem'=16] {'mem'}, dimensions={0}, use_global_device_ids=true | all-gather | bytes 69632 | tf_op jit(solution)/shard_map/all_gather | solution.py:71
  95.9 23.2 %all_gather.11 = s32[16384]{0:T(1024)S(1)} all-gather(s32[1024]{0:T(1024)S(1)} %all_to_all.32), channel_id=1, replica_groups=mesh['grp'=8,'mem'=16] {'mem'}, dimensions={0}, use_global_device_ids=true | all-gather | bytes 69632 | tf_op jit(solution)/shard_map/all_gather | solution.py:72
  119.1 80.4 %all-gather.2.cloned.1.call-done = bf16[16384,768]{1,0:T(8,128)(2,1)} async-done(((bf16[1024,768]{1,0:T(8,128)(2,1)}), bf16[16384,768]{1,0:T(8,128)(2,1)}) %all-gather.2.cloned.1.call-update) | async-done | bytes 25165840 | tf_op jit(solution)/shard_map/all_gather | solution.py:70
  199.5 68.7 %while.25 = (s32[]{:T(128)}, f32[1024]{0:T(1024)S(1)}, bf16[1024,768]{1,0:T(8,128)(2,1)S(1)}, s32[1024]{0:T(1024)}, s32[1024]{0:T(1024)}, /*index=5*/bf16[16,102...) while((s32[]{:T(128)}, f32[1024]{0:T(1024)S(1)}, ...), condition=%wide.wide.region_12.13_spmd.clone, body=%wide.wide.region_8.12_spmd.clone.sunk | while | flops 808454144 | bytes 5571944 | solution.py:85
  199.5 1.5 dynamic-slice_bitcast_fusion.3
  201.1 2.7 while.26
  201.1 1.3 select_reduce_fusion.3
  202.5 1.3 select_reduce_fusion.3
  203.8 1.5 dynamic-slice_bitcast_fusion.3
  205.4 2.7 while.26
  205.4 1.3 select_reduce_fusion.3
  206.8 1.3 select_reduce_fusion.3
  208.1 1.5 dynamic-slice_bitcast_fusion.3
  209.7 2.7 while.26
  211.1 1.3 select_reduce_fusion.3
  212.4 1.5 dynamic-slice_bitcast_fusion.3
  214.0 2.7 while.26
  215.3 1.3 select_reduce_fusion.3
  216.7 1.5 dynamic-slice_bitcast_fusion.3
  218.3 2.7 while.26
  219.6 1.3 select_reduce_fusion.3
  221.0 1.5 dynamic-slice_bitcast_fusion.3
  222.6 2.7 while.26
  223.9 1.3 select_reduce_fusion.3
  225.3 1.5 dynamic-slice_bitcast_fusion.3
  226.8 2.7 while.26
  228.2 1.3 select_reduce_fusion.3
  229.6 1.5 dynamic-slice_bitcast_fusion.3
  231.1 2.7 while.26
  231.2 1.3 select_reduce_fusion.3
  232.5 1.3 select_reduce_fusion.3
  233.9 1.5 dynamic-slice_bitcast_fusion.3
  235.4 2.7 while.26
  236.8 1.3 select_reduce_fusion.3
  238.2 1.5 dynamic-slice_bitcast_fusion.3
  239.7 2.7 while.26
  241.1 1.3 select_reduce_fusion.3
  242.5 1.5 dynamic-slice_bitcast_fusion.3
  244.0 2.7 while.26
  245.4 1.3 select_reduce_fusion.3
  246.8 1.5 dynamic-slice_bitcast_fusion.3
  248.3 2.7 while.26
  249.7 1.3 select_reduce_fusion.3
  251.1 1.5 dynamic-slice_bitcast_fusion.3
  252.6 2.7 while.26
  254.0 1.3 select_reduce_fusion.3
  255.4 1.5 dynamic-slice_bitcast_fusion.3
  256.9 2.7 while.26
  257.0 1.3 select_reduce_fusion.3
  258.3 1.3 select_reduce_fusion.3
  259.7 1.5 dynamic-slice_bitcast_fusion.3
  261.2 2.7 while.26
  261.2 1.3 select_reduce_fusion.3
  262.6 1.3 select_reduce_fusion.3
  264.0 1.5 dynamic-slice_bitcast_fusion.3
  265.5 2.7 while.26
  266.9 1.3 select_reduce_fusion.3
  (208 shorter events, 22.8 us)
Async XLA Ops:
  6.5 2.3 copy-start.1
  6.5 193.0 %all-gather.2.cloned.1.call-start = ((), (), s32[]{:S(2)}) async-start(), calls=%async_computation.3 | async-start | bytes 26738688 | tf_op jit(solution)/shard_map/all_gather | solution.py:70
  47.6 151.9 %copy-start = (bf16[128,8,768]{2,1,0:T(8,128)(2,1)S(1)}, bf16[128,8,768]{2,1,0:T(8,128)(2,1)}, u32[]{:S(2)}) copy-start(bf16[128,8,768]{2,1,0:T(8,128)(2,1)} %all_to_all.36) | copy-start | bytes 4718596
  51.1 14.0 %all-to-all-start.1 = ((s32[128,8,1]{1,2,0:T(1,128)}), s32[128,8,1]{1,2,0:T(1,128)S(1)}, u32[]{:S(2)}, u32[]{:S(2)}) async-start(s32[128,8,1]{1,2,0:T(1,128)} %bitcast.10), calls=%async_computation.1 | async-start | bytes 131072 | tf_op jit(solution)/shard_map/all_to_all | solution.py:65
  65.2 29.8 %all-to-all-start.2 = ((s32[128,8,1]{1,2,0:T(1,128)}), s32[128,8,1]{1,2,0:T(1,128)S(1)}, u32[]{:S(2)}, u32[]{:S(2)}) async-start(s32[128,8,1]{1,2,0:T(1,128)} %bitcast.11), calls=%async_computation.2 | async-start | bytes 131072 | tf_op jit(solution)/shard_map/all_to_all | solution.py:66
  71.1 128.4 %copy-start.2 = (s32[1024]{0:T(1024)}, s32[1024]{0:T(1024)S(1)}, u32[]{:S(2)}) copy-start(s32[1024]{0:T(1024)S(1)} %all_to_all.29) | copy-start | bytes 12292
  95.8 103.7 %copy-start.3 = (s32[1024]{0:T(1024)}, s32[1024]{0:T(1024)S(1)}, u32[]{:S(2)}) copy-start(s32[1024]{0:T(1024)S(1)} %all_to_all.32) | copy-start | bytes 12292
Sparse Core Ops, SparseCore 0:
  47.8 151.6 all-gather.1
where the time goes:
time: 277 us; the launch traced here: 276 us
  waiting for transfers between devices  86.6 us (31%)
  blocking collectives  82.5 us (30%)
  matrix products  40.4 us (15%)
  local copies, waits for them, and re-layouts  33.8 us (12%)
  between operations  13.5 us (5%)
  starting transfers between devices  9.14 us (3%)
  other arithmetic  7.79 us (3%)
    all_gather x1, waiting for transfers between devices, local(): lax.all_gather(own_rows[0], 'mem', axis=0, tiled=True)  80.4 us
    dot_general x32, matrix products, block_max(): jnp.einsum('ik,jk->ij', block_units, piece_units, preferred_element_type=...  40.4 us
    all_to_all x1, blocking collectives, local(): lax.all_to_all(send_units, ('grp', 'mem'), split_axis=0, concat_axis=0, t...  35.5 us
    squeeze x16, local copies, waits for them, and re-layouts, local(): lax.scan(through, jnp.full((slot_count,), -2.0, jnp.float32), split_piece)  24.3 us
    all_gather x1, blocking collectives, local(): lax.all_gather(own_rows[1], 'mem', axis=0, tiled=True)  23.8 us
    all_gather x1, blocking collectives, local(): lax.all_gather(own_rows[2], 'mem', axis=0, tiled=True)  23.2 us
    all_to_all x1, waiting for transfers between devices, local(): lax.all_to_all(send_cluster, ('grp', 'mem'), split_axis=0, concat_axis=0,...  6.17 us
  transfers between devices with their start and end apart: 3, of which 2 were waited for; matrix products, arithmetic and copies ran while one was open for 3% of the time, Pallas kernels for 0%

commit v1 on v0

v1 whole, which is shorter than its diff:
```python
import math

import jax
import jax.numpy as jnp
from jax import lax
from jax.experimental import pallas as pl
from jax.experimental.pallas import tpu as pltpu
from jax.sharding import Mesh
from jax.sharding import PartitionSpec as P

F32, BF16, I32 = jnp.float32, jnp.bfloat16, jnp.int32
AXES = ("x", "core", "z", "y")
WIDTH = 768
ROWS = 512
KINDS = 8
MEMBERS = 16
CAP = 8
SEND = 96
BLOCK = SEND + 8
PACKED = 640
HELD = PACKED - 16
FAR = 256.0
VMEM = 56 * 2**20


def iota(shape, axis):
    return lax.broadcasted_iota(I32, shape, axis)


def iota_f(shape, axis):
    return iota(shape, axis).astype(F32)


def hot(hits):
    return jnp.where(hits, 1.0, 0.0).astype(BF16)


def mul(a, b):
    return jnp.dot(a, b, preferred_element_type=F32)


def mul_nt(a, b):
    return lax.dot_general(a, b, (((1,), (1,)), ((), ())), preferred_element_type=F32)


def rows_of(*rows):
    n = next(r.shape[1] for r in rows if r is not None)
    at = iota((8, n), 0)
    out = jnp.zeros((8, n), F32)
    for i, row in enumerate(rows):
        if row is not None:
            out = jnp.where(at == i, jnp.broadcast_to(row, (8, n)), out)
    return out


def prep_kernel(assign_ref, emb_ref, cid_ref, order_ref, place_ref, out_ref):
    wide = emb_ref[...].astype(F32)
    mean = jnp.mean(wide * wide, axis=1, keepdims=True)
    unit = (wide * lax.rsqrt(mean + 1e-06) * (1.0 / math.sqrt(WIDTH))).astype(BF16)
    cid = cid_ref[...]
    group = jnp.zeros_like(cid)
    for c in range(KINDS):
        group = jnp.where(cid == c, assign_ref[c], group)
    group = group.astype(F32)
    place = place_ref[...].astype(F32)
    owner = group * MEMBERS + place
    columns = jnp.transpose(rows_of(group, owner))
    before = iota((ROWS, ROWS), 0) < iota((ROWS, ROWS), 1)

    def rank(column, row):
        return jnp.sum(jnp.where(before & (column == row), 1.0, 0.0), axis=0, keepdims=True)

    in_group = rank(columns[:, 0:1], group)
    in_owner = rank(columns[:, 1:2], owner)
    fits = in_group < SEND
    order = order_ref[...]
    high = (order // 256).astype(F32)
    low = (order % 256).astype(F32)
    numbers = rows_of(high, low, place * CAP + in_owner + 1.0).astype(BF16)
    slot = jnp.where(fits, group * 128 + in_group, -1.0)
    spread = mul_nt(numbers, hot(iota_f((KINDS * 128, ROWS), 0) == slot))
    lane = iota((8, 128), 1)
    line = iota((8, 128), 0)
    counts = jnp.zeros((8, 128), F32)
    for g in range(KINDS):
        count = jnp.sum(jnp.where(group == g, 1.0, 0.0), axis=1, keepdims=True)
        counts = jnp.where((lane == g) & (line == 3), count, counts)
    numbers = jnp.concatenate(
        [spread[:, g * 128 : (g + 1) * 128] + counts for g in range(KINDS)]
        + [jnp.zeros((64, 128), F32)],
        axis=0,
    )
    numbers = jnp.concatenate([numbers, jnp.zeros((128, WIDTH - 128), F32)], axis=1).astype(BF16)
    at = iota((1, 128), 1)
    at = jnp.where(at < 64, (at // 8) * BLOCK + SEND + at % 8, -1).astype(F32)
    target = jnp.concatenate([jnp.where(fits, group * BLOCK + in_group, -1.0), at], axis=1)
    placing = hot(iota_f((KINDS * BLOCK, ROWS + 128), 0) == target)
    out_ref[...] = mul(placing, jnp.concatenate([unit, numbers], axis=0)).astype(BF16)


def pack_kernel(in_ref, out_ref):
    count = KINDS * BLOCK
    at = iota((64, count), 0)
    pick = hot(iota((64, count), 1) == (at // 8) * BLOCK + SEND + at % 8)
    numbers = mul(pick, in_ref[:, 0:128])
    lane = iota_f((1, count), 1)
    position = jnp.full((1, count), -1.0, F32)
    slot = iota_f((128, PACKED), 0)
    shift = iota_f((128, PACKED), 1) - slot
    base = jnp.zeros((1, 1), F32)
    gathered = jnp.zeros((8, PACKED), F32)
    line = iota((8, 128), 0)
    over = jnp.zeros((1, 128), F32)
    total = jnp.zeros((1, 128), F32)
    for s in range(KINDS):
        mine = numbers[s * 8 : s * 8 + 8, :]
        n = jnp.sum(jnp.where(mine[2:3, :] > 0.0, 1.0, 0.0), axis=1, keepdims=True)
        step = lane - s * BLOCK
        position = jnp.where((step >= 0.0) & (step < n), base + step, position)
        move = hot((shift == base) & (slot < n))
        mine = jnp.where(line == 4, float(s), mine)
        gathered = gathered + mul(mine.astype(BF16), move)
        base = base + n
        counts = mine[3:4, :]
        over = jnp.maximum(over, jnp.where(counts > SEND, 1.0, 0.0))
        total = total + counts
    over = jnp.maximum(over, jnp.where(total > HELD, 1.0, 0.0))
    over = jnp.max(over, axis=1, keepdims=True)
    position = jnp.where(position < HELD, position, -1.0)
    placing = hot(iota_f((HELD, count), 0) == position)
    out_ref[0:HELD, :] = mul(placing, in_ref[...]).astype(BF16)
    code = gathered[2:3, :]
    valid = (code > 0.0) & (iota((1, PACKED), 1) < HELD)
    final = rows_of(
        jnp.where(valid, gathered[0:1, :], FAR),
        jnp.where(valid, gathered[1:2, :], 0.0),
        jnp.where(valid, code, 0.0),
        jnp.where(valid, gathered[4:5, :], 0.0),
        jnp.broadcast_to(over, (1, PACKED)),
    )
    final = jnp.concatenate([final, jnp.zeros((8, WIDTH - PACKED), F32)], axis=1)
    final = jnp.concatenate([final, jnp.zeros((8, WIDTH), F32)], axis=0)
    out_ref[HELD:PACKED, :] = final.astype(BF16)


TILE = 160


def numbers_of(ref):
    return ref[HELD:PACKED, :].astype(F32)[0:8, 0:PACKED]


def orders_of(numbers):
    return numbers[0:1, :] * 256.0 + numbers[1:2, :]


def pair_max(row_refs, col_refs, best_ref, first, order_ref, init):
    col_orders = [orders_of(numbers_of(c)) for c in col_refs]
    for i, row_ref in enumerate(row_refs):
        order_ref[...] = jnp.transpose(rows_of(orders_of(numbers_of(row_ref))))

        def tile(t, _, row_ref=row_ref, start=(first + i) * PACKED):
            here = pl.ds(pl.multiple_of(t * TILE, TILE), TILE)
            there = pl.ds(pl.multiple_of(start + t * TILE, TILE), TILE)
            rows = row_ref[here, :]
            order = order_ref[here, 0:1]
            best = jnp.full((TILE, 128), -2.0, F32) if init else best_ref[there, :]
            for col_ref, col_order in zip(col_refs, col_orders):
                scores = mul_nt(rows, col_ref[...])
                scores = jnp.where(col_order < order, scores, -2.0)
                for j in range(PACKED // 128):
                    best = jnp.maximum(best, scores[:, j * 128 : (j + 1) * 128])
            best_ref[there, :] = best
            return 0

        lax.fori_loop(0, PACKED // TILE, tile, 0)


def near_kernel(own, y1, y3, z1, z3, best_ref, order_ref):
    pair_max((own, y1, y3), (own, z1, z3), best_ref, 0, order_ref, True)


def far_kernel(own, y1, y3, y2a, y2b, z1, z3, z2a, z2b, near_ref, out_ref, y2, z2, best_ref, order_ref, sent):
    half = PACKED // 2
    y2[0:half, :] = y2a[...]
    y2[half:PACKED, :] = y2b[...]
    z2[0:half, :] = z2a[...]
    z2[half:PACKED, :] = z2b[...]
    best_ref[0 : 3 * PACKED, :] = near_ref[...]
    pair_max((own, y1, y3), (z2,), best_ref, 0, order_ref, False)
    pair_max((y2,), (own, z1, z3, z2), best_ref, 3, order_ref, True)
    over = jnp.zeros((1, 128), F32)
    for ref in (own, y1, y3, y2, z1, z3, z2):
        over = jnp.maximum(over, numbers_of(ref)[4:5, 0:128])
    sent[...] = jnp.zeros((128, 128), F32)
    sent[4 * KINDS : 4 * KINDS + 8, :] = jnp.broadcast_to(over, (8, 128))
    lane = iota_f((1, 128), 1)
    for q, ref in enumerate((own, y1, y3, y2)):
        best = jnp.max(best_ref[q * PACKED : (q + 1) * PACKED, :], axis=1, keepdims=True)
        best = jnp.maximum(best, -1.0)
        numbers = numbers_of(ref)
        code = jnp.transpose(rows_of(numbers[3:4, :] * 128.0 + numbers[2:3, :] - 1.0, numbers[2:3, :]))
        code = jnp.where(code[:, 1:2] > 0.0, code[:, 0:1], -1.0)
        lines = [
            jnp.max(jnp.where(code == lane + 128.0 * s, best, -1.0), axis=0, keepdims=True)
            for s in range(KINDS)
        ]
        sent[q * KINDS : (q + 1) * KINDS, :] = rows_of(*lines)
    out_ref[...] = jnp.transpose(sent[...])


def final_kernel(in_ref, out_ref, over_ref):
    got = jnp.transpose(in_ref[...])
    over_ref[0, 0] = (jnp.max(got[4 * KINDS : 4 * KINDS + 1, :]) > 0.5).astype(I32)
    lane = iota((KINDS, 128), 1) % 32
    best = got[0:KINDS, :]
    for q, away in ((1, 3), (2, 1), (3, 2)):
        part = got[q * KINDS : (q + 1) * KINDS, :]
        moved = jnp.where(
            lane >= 8 * away,
            pltpu.roll(part, 8 * away, 1),
            pltpu.roll(part, 128 + 8 * away - 32, 1),
        )
        best = jnp.maximum(best, moved)
    out_ref[...] = best


def call(kernel, out, scratch=(), ins=None, outs=None, cost=None):
    more = {}
    if ins is not None:
        more["in_specs"] = ins
    if outs is not None:
        more["out_specs"] = outs
    return pl.pallas_call(
        kernel,
        out_shape=out,
        scratch_shapes=list(scratch),
        cost_estimate=cost,
        compiler_params=pltpu.CompilerParams(vmem_limit_bytes=VMEM),
        **more,
    )


def ring(x, axis, step):
    return lax.ppermute(x, axis, [(i, (i + step) % 4) for i in range(4)])


def fast(embeddings, cluster_id, row_order, assignment, placement):
    vmem = pl.BlockSpec(memory_space=pltpu.VMEM)
    smem = pl.BlockSpec(memory_space=pltpu.SMEM)
    line = lambda a: a.reshape(1, ROWS)
    sent = call(
        prep_kernel,
        jax.ShapeDtypeStruct((KINDS * BLOCK, WIDTH), BF16),
        ins=[smem] + [vmem] * 4,
        cost=pl.CostEstimate(flops=10**9, bytes_accessed=2 * 10**6, transcendentals=0),
    )(assignment, embeddings, line(cluster_id), line(row_order), line(placement))
    got = lax.all_to_all(
        sent.reshape(KINDS, BLOCK, WIDTH), ("x", "core"), split_axis=0, concat_axis=0, tiled=True
    )
    own = call(
        pack_kernel,
        jax.ShapeDtypeStruct((PACKED, WIDTH), BF16),
        cost=pl.CostEstimate(flops=10**9, bytes_accessed=2 * 10**6, transcendentals=0),
    )(got.reshape(KINDS * BLOCK, WIDTH))
    half = PACKED // 2
    y1, y3, z1, z3 = ring(own, "y", 1), ring(own, "y", -1), ring(own, "z", 1), ring(own, "z", -1)
    y2a, y2b = ring(y1[:half], "y", 1), ring(y3[half:], "y", -1)
    z2a, z2b = ring(z1[:half], "z", 1), ring(z3[half:], "z", -1)
    pair = 2 * PACKED * PACKED * WIDTH
    near = call(
        near_kernel,
        jax.ShapeDtypeStruct((3 * PACKED, 128), F32),
        [pltpu.VMEM((PACKED, 8), F32)],
        cost=pl.CostEstimate(flops=9 * pair, bytes_accessed=6 * 10**6, transcendentals=0),
    )(own, y1, y3, z1, z3)
    part = pltpu.VMEM((PACKED, WIDTH), BF16)
    back = call(
        far_kernel,
        jax.ShapeDtypeStruct((128, 128), F32),
        [part, part, pltpu.VMEM((4 * PACKED, 128), F32), pltpu.VMEM((PACKED, 8), F32), pltpu.VMEM((128, 128), F32)],
        cost=pl.CostEstimate(flops=7 * pair, bytes_accessed=8 * 10**6, transcendentals=0),
    )(own, y1, y3, y2a, y2b, z1, z3, z2a, z2b, near)
    back = lax.all_to_all(back, ("z", "y"), split_axis=0, concat_axis=0, tiled=True)
    best, over = call(
        final_kernel,
        (jax.ShapeDtypeStruct((KINDS, 128), F32), jax.ShapeDtypeStruct((1, 1), I32)),
        ins=[vmem],
        outs=(vmem, smem),
    )(back)
    return best.reshape(KINDS * 128), over[0, 0] > 0


def slow(embeddings, cluster_id, row_order, assignment, placement):
    owners = KINDS * MEMBERS
    slots = owners * CAP
    wide = embeddings.astype(F32)
    mean = jnp.mean(wide * wide, axis=1, keepdims=True)
    unit = (wide * lax.rsqrt(mean + 1e-06) * (1.0 / math.sqrt(WIDTH))).astype(BF16)
    owner = jnp.sum(
        jnp.where(cluster_id[:, None] == jnp.arange(KINDS, dtype=I32)[None, :], assignment[None, :], 0), axis=1
    ) * MEMBERS + placement
    ids = jnp.arange(ROWS, dtype=I32)
    rank = jnp.sum(((owner[:, None] == owner[None, :]) & (ids[None, :] < ids[:, None])).astype(I32), axis=1)
    target = owner * CAP + rank
    units = jnp.zeros((slots, WIDTH), BF16).at[target].set(unit)
    orders = jnp.full((slots,), ROWS * owners, I32).at[target].set(row_order)
    swap = lambda a: lax.all_to_all(a, AXES, split_axis=0, concat_axis=0, tiled=True)
    units, orders = swap(units), swap(orders)

    def step(_, carried):
        best, piece, piece_orders = carried

        def block(packed):
            block_units, block_orders = packed
            scores = jnp.einsum("ik,jk->ij", block_units, piece, preferred_element_type=F32)
            fit = piece_orders[None, :] < block_orders[:, None]
            return jnp.max(jnp.where(fit, scores, -2.0), axis=1)

        here = lax.map(block, (units.reshape(2, slots // 2, WIDTH), orders.reshape(2, slots // 2)))
        best = jnp.maximum(best, here.reshape(slots))
        turn = [(i, (i + 1) % MEMBERS) for i in range(MEMBERS)]
        return best, lax.ppermute(piece, ("z", "y"), turn), lax.ppermute(piece_orders, ("z", "y"), turn)

    best = lax.fori_loop(0, MEMBERS, step, (jnp.full((slots,), -2.0, F32), units, orders))[0]
    return jnp.where(orders < ROWS * owners, jnp.maximum(best, -1.0), -1.0)


def local(*args):
    best, over = fast(*args)
    return lax.cond(over, lambda args, best: slow(*args), lambda args, best: best, args, best)


def solution(mesh):
    fine = Mesh(mesh.devices.reshape(4, 2, 4, 4), AXES)
    return jax.shard_map(
        local,
        mesh=fine,
        in_specs=(P(AXES, None), P(AXES), P(AXES), P(), P(AXES)),
        out_specs=P(AXES),
        check_vma=False,
    )
```

time: 277 us -> 116 us (0.42)
  waiting for transfers between devices: 86.6 us -> 25.4 us
  blocking collectives: 82.5 us -> 23.1 us
  Pallas kernels: 0 us -> 44.8 us
  matrix products: 40.4 us -> 0 us
  local copies, waits for them, and re-layouts: 33.8 us -> 3.24 us
  between operations: 13.5 us -> 0.82 us
  starting transfers between devices: 9.14 us -> 18.3 us
  other arithmetic: 7.79 us -> 0 us
    all_gather x1 -> x0, waiting for transfers between devices: 80.4 us -> none  [local(): lax.all_gather(own_rows[0], 'mem', axis=0, tiled=True)]
    all_gather x2 -> x0, blocking collectives: 47 us -> none  [the longest x1 23.8 us: local(): lax.all_gather(own_rows[1], 'mem', axis=0, tiled=True)]
    pallas_call x0 -> x5, Pallas kernels: none -> 44.8 us  [the longest x1 18.5 us: fast(): call(far_kernel, jax.ShapeDtypeStruct((128, 128), F32), [part, part, pltp...]
    dot_general x32 -> x0, matrix products: 40.4 us -> none  [block_max(): jnp.einsum('ik,jk->ij', block_units, piece_units, preferred_element_type=...]
    squeeze x16 -> x0, local copies, waits for them, and re-layouts: 24.3 us -> none  [local(): lax.scan(through, jnp.full((slot_count,), -2.0, jnp.float32), split_piece)]
    ppermute x0 -> x8, waiting for transfers between devices: none -> 17.7 us  [ring(): return lax.ppermute(x, axis, [(i, (i + step) % 4) for i in range(4)])]
    ppermute x0 -> x8, starting transfers between devices: none -> 14.7 us  [ring(): return lax.ppermute(x, axis, [(i, (i + step) % 4) for i in range(4)])]
    all_to_all x1, blocking collectives: 35.5 us -> 23.1 us  [fast(): lax.all_to_all(sent.reshape(KINDS, BLOCK, WIDTH), ('x', 'core'), split_ax...]
  transfers between devices with their start and end apart: 3 -> 9, of which waited for: 2 -> 3; matrix products, arithmetic and copies ran while one was open for 3% -> 0% of each run, Pallas kernels for 0% -> 15%
where the time goes in v1:
time: 116 us
  Pallas kernels  44.8 us (39%)
  waiting for transfers between devices  25.4 us (22%)
  blocking collectives  23.1 us (20%)
  starting transfers between devices  18.3 us (16%)
  local copies, waits for them, and re-layouts  3.24 us (3%)
    all_to_all x1, blocking collectives, fast(): lax.all_to_all(sent.reshape(KINDS, BLOCK, WIDTH), ('x', 'core'), split_ax...  23.1 us
    pallas_call x1, Pallas kernels, fast(): call(far_kernel, jax.ShapeDtypeStruct((128, 128), F32), [part, part, pltp...  18.5 us
    ppermute x8, waiting for transfers between devices, ring(): return lax.ppermute(x, axis, [(i, (i + step) % 4) for i in range(4)])  17.7 us
    pallas_call x1, Pallas kernels, fast(): call(near_kernel, jax.ShapeDtypeStruct((3 * PACKED, 128), F32), [pltpu.VM...  16.8 us
    ppermute x8, starting transfers between devices, ring(): return lax.ppermute(x, axis, [(i, (i + step) % 4) for i in range(4)])  14.7 us
    all_to_all x1, waiting for transfers between devices, fast(): lax.all_to_all(back, ('z', 'y'), split_axis=0, concat_axis=0, tiled=True)  7.67 us
    pallas_call x1, Pallas kernels, fast(): call(prep_kernel, jax.ShapeDtypeStruct((KINDS * BLOCK, WIDTH), BF16), ins...  4.07 us
    pallas_call x1, Pallas kernels, fast(): call(pack_kernel, jax.ShapeDtypeStruct((PACKED, WIDTH), BF16), cost=pl.Co...  3.92 us
  transfers between devices with their start and end apart: 9, of which 3 were waited for; matrix products, arithmetic and copies ran while one was open for 0% of the time, Pallas kernels for 15%

profile of v1, /device:TPU:0, one launch (start us, length us, event | category | flops | bytes accessed | tf_op | source)
XLA Modules:
  0.0 115.7 jit_solution(5256406330962049565)
XLA Ops:
  0.0 4.1 %shard_map.57 = bf16[832,768]{1,0:T(8,128)(2,1)} custom-call(s32[8]{0:T(128)} %assign_ref.1, bf16[512,768]{1,0:T(8,128)(2,1)} %emb_ref.1, s32[1,512]{1,0:T(1,128)} %bitcast.52, s32[1,512]{1,0:T(1,128)} %bitcast.54, s32[1,512]{1,0:T(1,128)} %bitcast.51), custom_call_target="tpu_custom_call" | custom-call | flops 1000000000 | bytes 2000000 | tf_op jit(solution)/shard_map/pallas_call | solution.py:252
  4.1 23.1 %all_to_all.34 = bf16[8,104,768]{2,1,0:T(8,128)(2,1)} all-to-all(bf16[8,104,768]{2,1,0:T(8,128)(2,1)} %bitcast.46), channel_id=1, replica_groups=mesh['x'=4,'core'=2,'z'=4,'y'=4] {'x','core'}, dimensions={0} | all-to-all | bytes 2555904 | tf_op jit(solution)/shard_map/all_to_all | solution.py:258
  27.2 3.9 %shard_map.58.own = bf16[640,768]{1,0:T(8,128)(2,1)} custom-call(bf16[832,768]{1,0:T(8,128)(2,1)} %bitcast.45), custom_call_target="tpu_custom_call" | custom-call | flops 1000000000 | bytes 2000000 | tf_op jit(solution)/shard_map/pallas_call | solution.py:261
  31.1 1.6 %collective-permute-start.2 = (bf16[640,768]{1,0:T(8,128)(2,1)}, bf16[640,768]{1,0:T(8,128)(2,1)S(1)}, u32[]{:S(2)}, u32[]{:S(2)}) collective-permute-start(bf16[640,768]{1,0:T(8,128)(2,1)} %shard_map.58.own), channel_id=1, source_target_pairs={{0,1},{1,2},{2,3},{3,0},{4,5},{5,6},{6,7},{7,4},{8,9},{9,10},{10,1... | collective-permute-start | bytes 2949128 | tf_op jit(solution)/shard_map/ppermute | solution.py:245
  32.7 1.7 %collective-permute-start.3 = (bf16[640,768]{1,0:T(8,128)(2,1)}, bf16[640,768]{1,0:T(8,128)(2,1)S(1)}, u32[]{:S(2)}, u32[]{:S(2)}) collective-permute-start(bf16[640,768]{1,0:T(8,128)(2,1)} %shard_map.58.own), channel_id=1, source_target_pairs={{0,3},{1,0},{2,1},{3,2},{4,7},{5,4},{6,5},{7,6},{8,11},{9,8},{10,9... | collective-permute-start | bytes 2949128 | tf_op jit(solution)/shard_map/ppermute | solution.py:245
  34.3 1.9 %collective-permute-start.6 = (bf16[640,768]{1,0:T(8,128)(2,1)}, bf16[640,768]{1,0:T(8,128)(2,1)S(1)}, u32[]{:S(2)}, u32[]{:S(2)}) collective-permute-start(bf16[640,768]{1,0:T(8,128)(2,1)} %shard_map.58.own), channel_id=1, source_target_pairs={{0,4},{4,8},{8,12},{12,0},{1,5},{5,9},{9,13},{13,1},{2,6},{6,10},{... | collective-permute-start | bytes 2949128 | tf_op jit(solution)/shard_map/ppermute | solution.py:245
  36.2 2.1 %collective-permute-start.7 = (bf16[640,768]{1,0:T(8,128)(2,1)}, bf16[640,768]{1,0:T(8,128)(2,1)S(1)}, u32[]{:S(2)}, u32[]{:S(2)}) collective-permute-start(bf16[640,768]{1,0:T(8,128)(2,1)} %shard_map.58.own), channel_id=1, source_target_pairs={{0,12},{4,0},{8,4},{12,8},{1,13},{5,1},{9,5},{13,9},{2,14},{6,2},{... | collective-permute-start | bytes 2949128 | tf_op jit(solution)/shard_map/ppermute | solution.py:245
  38.4 17.4 %collective-permute-done.2.y1 = bf16[640,768]{1,0:T(8,128)(2,1)S(1)} collective-permute-done((bf16[640,768]{1,0:T(8,128)(2,1)}, bf16[640,768]{1,0:T(8,128)(2,1)S(1)}, u32[]{:S(2)}, u32[]{:S(2)}) %collective-permute-start.2) | collective-permute-done | bytes 983072 | tf_op jit(solution)/shard_map/ppermute | solution.py:245
  55.7 0.0 copy-start.2
  55.8 0.4 collective-permute-start.4
  56.2 0.0 collective-permute-done.3.y3
  56.2 0.0 copy-start.3
  56.2 3.0 %collective-permute-start.5 = (bf16[320,768]{1,0:T(8,128)(2,1)S(1)}, bf16[320,768]{1,0:T(8,128)(2,1)S(1)}, u32[]{:S(2)}, u32[]{:S(2)}) collective-permute-start(bf16[320,768]{1,0:T(8,128)(2,1)S(1)} %slice.17), channel_id=1, source_target_pairs={{0,3},{1,0},{2,1},{3,2},{4,7},{5,4},{6,5},{7,6},{8,11},{9,8},{10,9... | collective-permute-start | bytes 1474568 | tf_op jit(solution)/shard_map/ppermute | solution.py:245
  59.2 0.3 collective-permute-done.6.z1
  59.5 0.0 copy-start.4
  59.6 1.7 %collective-permute-start.8 = (bf16[320,768]{1,0:T(8,128)(2,1)S(1)}, bf16[320,768]{1,0:T(8,128)(2,1)S(1)}, u32[]{:S(2)}, u32[]{:S(2)}) collective-permute-start(bf16[320,768]{1,0:T(8,128)(2,1)S(1)} %slice.18), channel_id=1, source_target_pairs={{0,4},{4,8},{8,12},{12,0},{1,5},{5,9},{9,13},{13,1},{2,6},{6,10},{... | collective-permute-start | bytes 1474568 | tf_op jit(solution)/shard_map/ppermute | solution.py:245
  61.2 0.0 collective-permute-done.7.z3
  61.2 0.0 copy-start.5
  61.3 0.0 copy-done.2
  61.3 2.4 %collective-permute-start.9 = (bf16[320,768]{1,0:T(8,128)(2,1)S(1)}, bf16[320,768]{1,0:T(8,128)(2,1)S(1)}, u32[]{:S(2)}, u32[]{:S(2)}) collective-permute-start(bf16[320,768]{1,0:T(8,128)(2,1)S(1)} %slice.19), channel_id=1, source_target_pairs={{0,12},{4,0},{8,4},{12,8},{1,13},{5,1},{9,5},{13,9},{2,14},{6,2},{... | collective-permute-start | bytes 1474568 | tf_op jit(solution)/shard_map/ppermute | solution.py:245
  63.7 0.0 copy-done.3
  63.7 0.0 copy-done.4
  63.7 0.0 copy-done.5
  63.7 16.8 %shard_map.59.near_ref = f32[1920,128]{1,0:T(8,128)} custom-call(bf16[640,768]{1,0:T(8,128)(2,1)} %shard_map.58.own, bf16[640,768]{1,0:T(8,128)(2,1)} %copy-done.2, bf16[640,768]{1,0:T(8,128)(2,1)} %copy-done.3, bf16[640,768]{1,0:T(8,128)(2,1)} %copy-done.4, bf16[640,768]{1,0:T(8,128)(2,1)} %copy-done.5), custom_call_target="tpu_custom_call" | custom-call | flops 5662310400 | bytes 6000000 | tf_op jit(solution)/shard_map/pallas_call | solution.py:271
  80.5 0.0 copy-start
  80.5 0.0 copy-start.7
  80.5 0.0 copy-start.8
  80.5 0.0 copy-start.9
  80.5 0.0 collective-permute-done.4.y2a
  80.5 0.0 copy-start.10
  80.5 0.0 collective-permute-done.5.y2b
  80.5 0.0 copy-start.11
  80.6 0.0 collective-permute-done.8.z2a
  80.6 0.0 copy-start.12
  80.6 0.0 collective-permute-done.9.z2b
  80.6 0.7 copy-done.10
  81.3 0.1 copy-done.11
  81.5 0.2 copy-done.12
  81.7 0.0 copy-start.13
  81.7 0.8 copy-done.13
  82.4 18.5 %shard_map.60 = f32[128,128]{1,0:T(8,128)} custom-call(bf16[640,768]{1,0:T(8,128)(2,1)} %shard_map.58.own, bf16[640,768]{1,0:T(8,128)(2,1)} %copy-done.2, bf16[640,768]{1,0:T(8,128)(2,1)} %copy-done.3, bf16[320,768]{1,0:T(8,128)(2,1)} %copy-done.10, bf16[320,768]{1,0:T(8,128)(2,1)} %copy-done.11, bf16[640,768]{1,0:T(8,128)(2,1)} %copy-done.4, ...), custom_call_target="tpu_custom_call" | custom-call | flops 4404019200 | bytes 8000000 | tf_op jit(solution)/shard_map/pallas_call | solution.py:278
  100.9 3.6 %all-to-all-start.3 = ((f32[16,8,128]{2,1,0:T(8,128)}), f32[16,8,128]{2,1,0:T(8,128)S(1)}, u32[]{:S(2)}, u32[]{:S(2)}) async-start(f32[16,8,128]{2,1,0:T(8,128)} %bitcast.50), calls=%async_computation.3 | async-start | bytes 131072 | tf_op jit(solution)/shard_map/all_to_all | solution.py:284
  104.5 7.7 %all-to-all-done.3 = f32[16,8,128]{2,1,0:T(8,128)S(1)} async-done(((f32[16,8,128]{2,1,0:T(8,128)}), f32[16,8,128]{2,1,0:T(8,128)S(1)}, u32[]{:S(2)}, u32[]{:S(2)}) %all-to-all-start.3) | async-done | bytes 65568 | tf_op jit(solution)/shard_map/all_to_all | solution.py:284
  112.2 0.0 copy-start.1
  112.2 0.6 copy-done.1
  112.8 1.5 %shard_map.61 = (f32[8,128]{1,0:T(8,128)S(1)}, s32[1,1]{1,0:T(1,128)}) custom-call(f32[128,128]{1,0:T(8,128)} %bitcast.48), custom_call_target="tpu_custom_call" | custom-call | tf_op jit(solution)/shard_map/pallas_call | solution.py:285
  115.0 0.0 copy-done
  115.0 0.0 copy-done.7
  115.1 0.0 copy-done.8
  115.1 0.0 copy-done.9
  115.1 0.0 copy-start.14
  115.1 0.6 copy-done.14
  (5 shorter events, 0.1 us)
Async XLA Ops:
  31.1 24.7 %collective-permute-start.2 = (bf16[640,768]{1,0:T(8,128)(2,1)}, bf16[640,768]{1,0:T(8,128)(2,1)S(1)}, u32[]{:S(2)}, u32[]{:S(2)}) collective-permute-start(bf16[640,768]{1,0:T(8,128)(2,1)} %shard_map.58.own), channel_id=1, source_target_pairs={{0,1},{1,2},{2,3},{3,0},{4,5},{5,6},{6,7},{7,4},{8,9},{9,10},{10,1... | collective-permute-start | bytes 2949128 | tf_op jit(solution)/shard_map/ppermute | solution.py:245
  32.7 23.5 %collective-permute-start.3 = (bf16[640,768]{1,0:T(8,128)(2,1)}, bf16[640,768]{1,0:T(8,128)(2,1)S(1)}, u32[]{:S(2)}, u32[]{:S(2)}) collective-permute-start(bf16[640,768]{1,0:T(8,128)(2,1)} %shard_map.58.own), channel_id=1, source_target_pairs={{0,3},{1,0},{2,1},{3,2},{4,7},{5,4},{6,5},{7,6},{8,11},{9,8},{10,9... | collective-permute-start | bytes 2949128 | tf_op jit(solution)/shard_map/ppermute | solution.py:245
  34.3 25.2 %collective-permute-start.6 = (bf16[640,768]{1,0:T(8,128)(2,1)}, bf16[640,768]{1,0:T(8,128)(2,1)S(1)}, u32[]{:S(2)}, u32[]{:S(2)}) collective-permute-start(bf16[640,768]{1,0:T(8,128)(2,1)} %shard_map.58.own), channel_id=1, source_target_pairs={{0,4},{4,8},{8,12},{12,0},{1,5},{5,9},{9,13},{13,1},{2,6},{6,10},{... | collective-permute-start | bytes 2949128 | tf_op jit(solution)/shard_map/ppermute | solution.py:245
  36.2 25.0 %collective-permute-start.7 = (bf16[640,768]{1,0:T(8,128)(2,1)}, bf16[640,768]{1,0:T(8,128)(2,1)S(1)}, u32[]{:S(2)}, u32[]{:S(2)}) collective-permute-start(bf16[640,768]{1,0:T(8,128)(2,1)} %shard_map.58.own), channel_id=1, source_target_pairs={{0,12},{4,0},{8,4},{12,8},{1,13},{5,1},{9,5},{13,9},{2,14},{6,2},{... | collective-permute-start | bytes 2949128 | tf_op jit(solution)/shard_map/ppermute | solution.py:245
  55.7 5.5 %copy-start.2 = (bf16[640,768]{1,0:T(8,128)(2,1)}, bf16[640,768]{1,0:T(8,128)(2,1)S(1)}, u32[]{:S(2)}) copy-start(bf16[640,768]{1,0:T(8,128)(2,1)S(1)} %collective-permute-done.2.y1) | copy-start | bytes 2949124
  55.8 24.7 %collective-permute-start.4 = (bf16[320,768]{1,0:T(8,128)(2,1)S(1)}, bf16[320,768]{1,0:T(8,128)(2,1)S(1)}, u32[]{:S(2)}, u32[]{:S(2)}) collective-permute-start(bf16[320,768]{1,0:T(8,128)(2,1)S(1)} %slice.16), channel_id=1, source_target_pairs={{0,1},{1,2},{2,3},{3,0},{4,5},{5,6},{6,7},{7,4},{8,9},{9,10},{10,1... | collective-permute-start | bytes 1474568 | tf_op jit(solution)/shard_map/ppermute | solution.py:245
  56.2 7.5 %copy-start.3 = (bf16[640,768]{1,0:T(8,128)(2,1)}, bf16[640,768]{1,0:T(8,128)(2,1)S(1)}, u32[]{:S(2)}) copy-start(bf16[640,768]{1,0:T(8,128)(2,1)S(1)} %collective-permute-done.3.y3) | copy-start | bytes 2949124
  56.2 24.3 %collective-permute-start.5 = (bf16[320,768]{1,0:T(8,128)(2,1)S(1)}, bf16[320,768]{1,0:T(8,128)(2,1)S(1)}, u32[]{:S(2)}, u32[]{:S(2)}) collective-permute-start(bf16[320,768]{1,0:T(8,128)(2,1)S(1)} %slice.17), channel_id=1, source_target_pairs={{0,3},{1,0},{2,1},{3,2},{4,7},{5,4},{6,5},{7,6},{8,11},{9,8},{10,9... | collective-permute-start | bytes 1474568 | tf_op jit(solution)/shard_map/ppermute | solution.py:245
  59.5 4.1 %copy-start.4 = (bf16[640,768]{1,0:T(8,128)(2,1)}, bf16[640,768]{1,0:T(8,128)(2,1)S(1)}, u32[]{:S(2)}) copy-start(bf16[640,768]{1,0:T(8,128)(2,1)S(1)} %collective-permute-done.6.z1) | copy-start | bytes 2949124
  59.6 21.0 %collective-permute-start.8 = (bf16[320,768]{1,0:T(8,128)(2,1)S(1)}, bf16[320,768]{1,0:T(8,128)(2,1)S(1)}, u32[]{:S(2)}, u32[]{:S(2)}) collective-permute-start(bf16[320,768]{1,0:T(8,128)(2,1)S(1)} %slice.18), channel_id=1, source_target_pairs={{0,4},{4,8},{8,12},{12,0},{1,5},{5,9},{9,13},{13,1},{2,6},{6,10},{... | collective-permute-start | bytes 1474568 | tf_op jit(solution)/shard_map/ppermute | solution.py:245
  61.2 2.5 %copy-start.5 = (bf16[640,768]{1,0:T(8,128)(2,1)}, bf16[640,768]{1,0:T(8,128)(2,1)S(1)}, u32[]{:S(2)}) copy-start(bf16[640,768]{1,0:T(8,128)(2,1)S(1)} %collective-permute-done.7.z3) | copy-start | bytes 2949124
  61.3 19.3 %collective-permute-start.9 = (bf16[320,768]{1,0:T(8,128)(2,1)S(1)}, bf16[320,768]{1,0:T(8,128)(2,1)S(1)}, u32[]{:S(2)}, u32[]{:S(2)}) collective-permute-start(bf16[320,768]{1,0:T(8,128)(2,1)S(1)} %slice.19), channel_id=1, source_target_pairs={{0,12},{4,0},{8,4},{12,8},{1,13},{5,1},{9,5},{13,9},{2,14},{6,2},{... | collective-permute-start | bytes 1474568 | tf_op jit(solution)/shard_map/ppermute | solution.py:245
  80.5 34.5 %copy-start = (bf16[512,768]{1,0:T(8,128)(2,1)S(1)}, bf16[512,768]{1,0:T(8,128)(2,1)}, u32[]{:S(2)}) copy-start(bf16[512,768]{1,0:T(8,128)(2,1)} %emb_ref.1) | copy-start | bytes 2359300
  80.5 34.5 %copy-start.7 = (s32[512]{0:T(512)S(1)}, s32[512]{0:T(512)}, u32[]{:S(2)}) copy-start(s32[512]{0:T(512)} %param.15) | copy-start | bytes 6148
  80.5 34.6 %copy-start.8 = (s32[512]{0:T(512)S(1)}, s32[512]{0:T(512)}, u32[]{:S(2)}) copy-start(s32[512]{0:T(512)} %param.12) | copy-start | bytes 6148
  80.5 34.6 %copy-start.9 = (s32[8]{0:T(128)S(1)}, s32[8]{0:T(128)}, u32[]{:S(2)}) copy-start(s32[8]{0:T(128)} %assign_ref.1) | copy-start | bytes 100
  80.5 0.8 copy-start.10
  80.5 0.9 copy-start.11
  80.6 1.1 copy-start.12
  81.7 0.8 copy-start.13
  100.9 11.3 %all-to-all-start.3 = ((f32[16,8,128]{2,1,0:T(8,128)}), f32[16,8,128]{2,1,0:T(8,128)S(1)}, u32[]{:S(2)}, u32[]{:S(2)}) async-start(f32[16,8,128]{2,1,0:T(8,128)} %bitcast.50), calls=%async_computation.3 | async-start | bytes 131072 | tf_op jit(solution)/shard_map/all_to_all | solution.py:284
  112.2 0.6 copy-start.1
  115.1 0.6 copy-start.14

commit v2 on v1

v2 whole, which is shorter than its diff:
```python
import math

import jax
import jax.numpy as jnp
from jax import lax
from jax.experimental import pallas as pl
from jax.experimental.pallas import tpu as pltpu
from jax.sharding import Mesh
from jax.sharding import PartitionSpec as P

F32, BF16, I32 = jnp.float32, jnp.bfloat16, jnp.int32
AXES = ("x", "core", "z", "y")
WIDTH = 768
ROWS = 512
KINDS = 8
MEMBERS = 16
CAP = 8
SEND = 96
BLOCK = SEND + 8
PACKED = 640
HELD = PACKED - 16
FAR = 256.0
VMEM = 56 * 2**20


def iota(shape, axis):
    return lax.broadcasted_iota(I32, shape, axis)


def iota_f(shape, axis):
    return iota(shape, axis).astype(F32)


def hot(hits):
    return jnp.where(hits, 1.0, 0.0).astype(BF16)


def mul(a, b):
    return jnp.dot(a, b, preferred_element_type=F32)


def mul_nt(a, b):
    return lax.dot_general(a, b, (((1,), (1,)), ((), ())), preferred_element_type=F32)


def rows_of(*rows):
    n = next(r.shape[1] for r in rows if r is not None)
    at = iota((8, n), 0)
    out = jnp.zeros((8, n), F32)
    for i, row in enumerate(rows):
        if row is not None:
            out = jnp.where(at == i, jnp.broadcast_to(row, (8, n)), out)
    return out


def prep_kernel(assign_ref, emb_ref, cid_ref, order_ref, place_ref, same_ref, other_ref):
    wide = emb_ref[...].astype(F32)
    mean = jnp.mean(wide * wide, axis=1, keepdims=True)
    unit = (wide * lax.rsqrt(mean + 1e-06) * (1.0 / math.sqrt(WIDTH))).astype(BF16)
    my_x, my_core = lax.axis_index("x"), lax.axis_index("core")
    cid = cid_ref[...]
    group = jnp.zeros_like(cid)
    for c in range(KINDS):
        away = lax.rem(assign_ref[c] // 2 - my_x + 4, 4)
        away += 4 * lax.rem(assign_ref[c] + my_core, 2)
        group = jnp.where(cid == c, away, group)
    group = group.astype(F32)
    place = place_ref[...].astype(F32)
    owner = group * MEMBERS + place
    columns = jnp.transpose(rows_of(group, owner))
    before = iota((ROWS, ROWS), 0) < iota((ROWS, ROWS), 1)

    def rank(column, row):
        return jnp.sum(jnp.where(before & (column == row), 1.0, 0.0), axis=0, keepdims=True)

    in_group = rank(columns[:, 0:1], group)
    in_owner = rank(columns[:, 1:2], owner)
    fits = in_group < SEND
    order = order_ref[...]
    high = (order // 256).astype(F32)
    low = (order % 256).astype(F32)
    kind = jnp.where(iota_f((KINDS, ROWS), 0) == group, 1.0, 0.0)
    numbers = jnp.concatenate([kind * high, kind * low, kind * (place * CAP + in_owner + 1.0)], axis=0)
    slot = jnp.transpose(rows_of(in_group))[:, 0:1]
    spread = mul(numbers.astype(BF16), hot(iota_f((ROWS, 128), 1) == slot))
    spread = jnp.where(iota((24, 128), 1) < SEND, spread, 0.0)
    counts = jnp.zeros((KINDS, 128), F32)
    for c in range(KINDS):
        count = jnp.sum(jnp.where(cid == c, 1.0, 0.0), axis=1, keepdims=True)
        counts = jnp.where(iota((KINDS, 128), 1) == assign_ref[c], count, counts)
    numbers = jnp.concatenate([spread, counts, jnp.zeros((96, 128), F32)], axis=0)
    numbers = jnp.concatenate([numbers, jnp.zeros((128, WIDTH - 128), F32)], axis=1).astype(BF16)
    at = iota((1, 128), 1)
    at = jnp.where(at < 32, (at % 8) * BLOCK + SEND + at // 8, -1).astype(F32)
    target = jnp.concatenate([jnp.where(fits, group * BLOCK + in_group, -1.0), at], axis=1)
    both = jnp.concatenate([unit, numbers], axis=0)
    half = 4 * BLOCK
    for ref, first in ((other_ref, half), (same_ref, 0)):
        placing = hot(iota_f((half, ROWS + 128), 0) == target - first)
        ref[...] = mul(placing, both).astype(BF16)


def pack_kernel(here_ref, from1_ref, from2_ref, from3_ref, out_ref, in_ref):
    count = KINDS * BLOCK
    for k, ref in enumerate((here_ref, from1_ref, from2_ref, from3_ref)):
        in_ref[k * 2 * BLOCK : (k + 1) * 2 * BLOCK, :] = ref[...]
    my_x, my_core = lax.axis_index("x"), lax.axis_index("core")
    at = iota((32, count), 0)
    pick = hot(iota((32, count), 1) == (at % 8) * BLOCK + SEND + at // 8)
    numbers = mul(pick, in_ref[:, 0:128])
    n = jnp.sum(jnp.where(numbers[16:24, :] > 0.0, 1.0, 0.0), axis=1, keepdims=True)
    line = iota((KINDS, 1), 0)
    base = jnp.zeros((KINDS, 1), F32)
    source = jnp.zeros((KINDS, 1), F32)
    lane = iota_f((1, count), 1)
    position = jnp.full((1, count), -1.0, F32)
    start = jnp.zeros((1, 1), F32)
    for b in range(KINDS):
        step = lane - b * BLOCK
        mine = n[b : b + 1, :]
        position = jnp.where((step >= 0.0) & (step < mine), start + step, position)
        base = jnp.where(line == b, start, base)
        from_device = 2 * lax.rem(my_x - b // 2 + 4, 4) + lax.rem(my_core + b % 2, 2)
        source = jnp.where(line == b, from_device.astype(F32), source)
        start = start + mine
    position = jnp.where(position < HELD, position, -1.0)
    placing = hot(iota_f((HELD, count), 0) == position)
    out_ref[0:HELD, :] = mul(placing, in_ref[...]).astype(BF16)
    step = iota_f((KINDS, PACKED), 1) - base
    mine = jnp.where((step >= 0.0) & (step < n), 1.0, 0.0)
    slot = jnp.sum(mine * step, axis=0, keepdims=True)
    found = mul(numbers[0:24, :].astype(BF16), hot(iota_f((128, PACKED), 0) == slot))
    high, low, code = (
        jnp.sum(mine * found[i * 8 : i * 8 + 8, :], axis=0, keepdims=True) for i in range(3)
    )
    source = jnp.sum(mine * source, axis=0, keepdims=True)
    counts = numbers[24:32, :]
    over = jnp.max(jnp.where(counts > SEND, 1.0, 0.0), axis=0, keepdims=True)
    over = jnp.maximum(over, jnp.where(jnp.sum(counts, axis=0, keepdims=True) > HELD, 1.0, 0.0))
    over = jnp.max(over, axis=1, keepdims=True)
    valid = (code > 0.0) & (iota((1, PACKED), 1) < HELD)
    final = rows_of(
        jnp.where(valid, high, FAR),
        jnp.where(valid, low, 0.0),
        jnp.where(valid, code, 0.0),
        jnp.where(valid, source, 0.0),
        jnp.broadcast_to(over, (1, PACKED)),
    )
    final = jnp.concatenate([final, jnp.zeros((8, WIDTH - PACKED), F32)], axis=1)
    final = jnp.concatenate([final, jnp.zeros((8, WIDTH), F32)], axis=0)
    out_ref[HELD:PACKED, :] = final.astype(BF16)


def numbers_of(ref):
    n = ref.shape[0]
    return ref[n - 16 : n, :].astype(F32)[0:8, 0:PACKED]


def orders_of(numbers):
    return numbers[0:1, :] * 256.0 + numbers[1:2, :]


def earlier_max(best, rows_ref, row_order, cols_ref, col_order):
    scores = mul_nt(cols_ref[...], rows_ref[...])
    scores = jnp.where(col_order < row_order, scores, -2.0)
    count, n = scores.shape
    return jnp.maximum(best, jnp.max(scores.reshape(count // 8, 8, n), axis=0))


def near_kernel(own, y1, y3, z1, z3, best_ref, order_ref):
    cols = (own, z1, z3)
    order_ref[...] = jnp.transpose(rows_of(*[orders_of(numbers_of(c)) for c in cols]))
    for i, rows in enumerate((own, y1, y3)):
        order = orders_of(numbers_of(rows))
        best = jnp.full((8, PACKED), -2.0, F32)
        for k, col in enumerate(cols):
            best = earlier_max(best, rows, order, col, order_ref[:, k : k + 1])
        best_ref[:, i * PACKED : (i + 1) * PACKED] = best


def far_kernel(own, y1, y3, y2a, y2b, z1, z3, z2a, z2b, near_ref, out_ref, y2, order_ref, sent):
    half = PACKED // 2
    y2[0:half, :] = y2a[...]
    y2[half:PACKED, :] = y2b[...]
    order_ref[...] = jnp.transpose(rows_of(*[orders_of(numbers_of(c)) for c in (own, z1, z3, z2b)]))
    over = jnp.zeros((1, 128), F32)
    for ref in (own, y1, y3, y2b, z1, z3, z2b):
        over = jnp.maximum(over, numbers_of(ref)[4:5, 0:128])
    sent[...] = jnp.zeros((128, 128), F32)
    sent[4 * KINDS : 4 * KINDS + 8, :] = jnp.broadcast_to(over, (8, 128))
    for q, rows in enumerate((own, y1, y3, y2)):
        numbers = numbers_of(rows)
        order = orders_of(numbers)
        if q < 3:
            best = near_ref[:, q * PACKED : (q + 1) * PACKED]
        else:
            best = jnp.full((8, PACKED), -2.0, F32)
            for k, col in enumerate((own, z1, z3)):
                best = earlier_max(best, rows, order, col, order_ref[:, k : k + 1])
        best = earlier_max(best, rows, order, z2a, order_ref[0:half, 3:4])
        best = earlier_max(best, rows, order, z2b, order_ref[half:PACKED, 3:4])
        best = jnp.maximum(jnp.max(best, axis=0, keepdims=True), -1.0)
        high = best.astype(BF16).astype(F32)
        low = best - high
        middle = low.astype(BF16).astype(F32)
        low = low - middle
        lines = jnp.where(
            (iota_f((KINDS, PACKED), 0) == numbers[3:4, :]) & (numbers[2:3, :] > 0.0), 1.0, 0.0
        )
        pieces = jnp.concatenate([lines, lines * high, lines * middle, lines * low], axis=0)
        code = jnp.transpose(rows_of(numbers[2:3, :]))[:, 0:1]
        put = mul(pieces.astype(BF16), hot(iota_f((PACKED, 128), 1) == code - 1.0))
        sent[q * KINDS : (q + 1) * KINDS, :] = (
            (put[0:8, :] - 1.0) + (put[8:16, :] + put[16:24, :] + put[24:32, :])
        )
    out_ref[...] = jnp.transpose(sent[...])


def final_kernel(in_ref, out_ref, over_ref):
    got = jnp.transpose(in_ref[...])
    over_ref[0, 0] = (jnp.max(got[4 * KINDS : 4 * KINDS + 1, :]) > 0.5).astype(I32)
    lane = iota((KINDS, 128), 1) % 32
    best = got[0:KINDS, :]
    for q, away in ((1, 3), (2, 1), (3, 2)):
        part = got[q * KINDS : (q + 1) * KINDS, :]
        moved = jnp.where(
            lane >= 8 * away,
            pltpu.roll(part, 8 * away, 1),
            pltpu.roll(part, 128 + 8 * away - 32, 1),
        )
        best = jnp.maximum(best, moved)
    out_ref[...] = best


def call(kernel, out, scratch=(), ins=None, outs=None, cost=None):
    more = {}
    if ins is not None:
        more["in_specs"] = ins
    if outs is not None:
        more["out_specs"] = outs
    return pl.pallas_call(
        kernel,
        out_shape=out,
        scratch_shapes=list(scratch),
        cost_estimate=cost,
        compiler_params=pltpu.CompilerParams(vmem_limit_bytes=VMEM),
        **more,
    )


def ring(x, axis, step):
    return lax.ppermute(x, axis, [(i, (i + step) % 4) for i in range(4)])


def fast(embeddings, cluster_id, row_order, assignment, placement):
    vmem = pl.BlockSpec(memory_space=pltpu.VMEM)
    smem = pl.BlockSpec(memory_space=pltpu.SMEM)
    line = lambda a: a.reshape(1, ROWS)
    cheap = pl.CostEstimate(flops=10**9, bytes_accessed=2 * 10**6, transcendentals=0)
    blocks = jax.ShapeDtypeStruct((4 * BLOCK, WIDTH), BF16)
    same, other = call(
        prep_kernel,
        (blocks, blocks),
        ins=[smem] + [vmem] * 4,
        cost=cheap,
    )(assignment, embeddings, line(cluster_id), line(row_order), line(placement))
    other = lax.ppermute(other, "core", [(0, 1), (1, 0)])
    shape = (4, 1, BLOCK, WIDTH)
    both = jnp.concatenate([same.reshape(shape), other.reshape(shape)], axis=1).reshape(4, 2 * BLOCK, WIDTH)
    own = call(
        pack_kernel,
        jax.ShapeDtypeStruct((PACKED, WIDTH), BF16),
        [pltpu.VMEM((KINDS * BLOCK, WIDTH), BF16)],
        cost=cheap,
    )(both[0], *[ring(both[k], "x", k) for k in (1, 2, 3)])
    half = PACKED // 2
    y1, y3, z1, z3 = ring(own, "y", 1), ring(own, "y", -1), ring(own, "z", 1), ring(own, "z", -1)
    y2a, y2b = ring(y1[:half], "y", 1), ring(y3[half:], "y", -1)
    z2a, z2b = ring(z1[:half], "z", 1), ring(z3[half:], "z", -1)
    pair = 2 * PACKED * PACKED * WIDTH
    near = call(
        near_kernel,
        jax.ShapeDtypeStruct((8, 3 * PACKED), F32),
        [pltpu.VMEM((PACKED, 8), F32)],
        cost=pl.CostEstimate(flops=9 * pair, bytes_accessed=6 * 10**6, transcendentals=0),
    )(own, y1, y3, z1, z3)
    back = call(
        far_kernel,
        jax.ShapeDtypeStruct((128, 128), F32),
        [pltpu.VMEM((PACKED, WIDTH), BF16), pltpu.VMEM((PACKED, 8), F32), pltpu.VMEM((128, 128), F32)],
        cost=pl.CostEstimate(flops=7 * pair, bytes_accessed=8 * 10**6, transcendentals=0),
    )(own, y1, y3, y2a, y2b, z1, z3, z2a, z2b, near)
    back = lax.all_to_all(back, ("z", "y"), split_axis=0, concat_axis=0, tiled=True)
    best, over = call(
        final_kernel,
        (jax.ShapeDtypeStruct((KINDS, 128), F32), jax.ShapeDtypeStruct((1, 1), I32)),
        ins=[vmem],
        outs=(vmem, smem),
    )(back)
    return best.reshape(KINDS * 128), over[0, 0] > 0


def slow(embeddings, cluster_id, row_order, assignment, placement):
    owners = KINDS * MEMBERS
    slots = owners * CAP
    wide = embeddings.astype(F32)
    mean = jnp.mean(wide * wide, axis=1, keepdims=True)
    unit = (wide * lax.rsqrt(mean + 1e-06) * (1.0 / math.sqrt(WIDTH))).astype(BF16)
    owner = jnp.sum(
        jnp.where(cluster_id[:, None] == jnp.arange(KINDS, dtype=I32)[None, :], assignment[None, :], 0), axis=1
    ) * MEMBERS + placement
    ids = jnp.arange(ROWS, dtype=I32)
    rank = jnp.sum(((owner[:, None] == owner[None, :]) & (ids[None, :] < ids[:, None])).astype(I32), axis=1)
    target = owner * CAP + rank
    units = jnp.zeros((slots, WIDTH), BF16).at[target].set(unit)
    orders = jnp.full((slots,), ROWS * owners, I32).at[target].set(row_order)
    swap = lambda a: lax.all_to_all(a, AXES, split_axis=0, concat_axis=0, tiled=True)
    units, orders = swap(units), swap(orders)

    def step(_, carried):
        best, piece, piece_orders = carried

        def block(packed):
            block_units, block_orders = packed
            scores = jnp.einsum("ik,jk->ij", block_units, piece, preferred_element_type=F32)
            fit = piece_orders[None, :] < block_orders[:, None]
            return jnp.max(jnp.where(fit, scores, -2.0), axis=1)

        here = lax.map(block, (units.reshape(2, slots // 2, WIDTH), orders.reshape(2, slots // 2)))
        best = jnp.maximum(best, here.reshape(slots))
        turn = [(i, (i + 1) % MEMBERS) for i in range(MEMBERS)]
        return best, lax.ppermute(piece, ("z", "y"), turn), lax.ppermute(piece_orders, ("z", "y"), turn)

    best = lax.fori_loop(0, MEMBERS, step, (jnp.full((slots,), -2.0, F32), units, orders))[0]
    return jnp.where(orders < ROWS * owners, jnp.maximum(best, -1.0), -1.0)


def local(*args):
    best, over = fast(*args)
    return lax.cond(over, lambda args, best: slow(*args), lambda args, best: best, args, best)


def solution(mesh):
    fine = Mesh(mesh.devices.reshape(4, 2, 4, 4), AXES)
    return jax.shard_map(
        local,
        mesh=fine,
        in_specs=(P(AXES, None), P(AXES), P(AXES), P(), P(AXES)),
        out_specs=P(AXES),
        check_vma=False,
    )
```

time: 116 us -> 102 us (0.88)
  blocking collectives: 23.1 us -> 0 us
  Pallas kernels: 44.8 us -> 29.7 us
  waiting for transfers between devices: 25.4 us -> 40.4 us
  starting transfers between devices: 18.3 us -> 24.1 us
  other arithmetic: 0 us -> 1.97 us
    all_to_all x1 -> x0, blocking collectives: 23.1 us -> none  [fast(): lax.all_to_all(sent.reshape(KINDS, BLOCK, WIDTH), ('x', 'core'), split_ax...]
    pallas_call x4, Pallas kernels: 43.3 us -> 28.1 us  [the longest x1 10.2 us: fast(): call(far_kernel, jax.ShapeDtypeStruct((128, 128), F32), [pltpu.VMEM((PACK...]
    ppermute x8 -> x11, waiting for transfers between devices: 17.7 us -> 30.5 us  [ring(): return lax.ppermute(x, axis, [(i, (i + step) % 4) for i in range(4)])]
    ppermute x8 -> x11, starting transfers between devices: 14.7 us -> 20.4 us  [ring(): return lax.ppermute(x, axis, [(i, (i + step) % 4) for i in range(4)])]
    ppermute x0 -> x1, waiting for transfers between devices: none -> 2.28 us  [fast(): other = lax.ppermute(other, 'core', [(0, 1), (1, 0)])]
    concatenate x0 -> x1, other arithmetic: none -> 1.97 us  [fast(): jnp.concatenate([same.reshape(shape), other.reshape(shape)], axis=1)]
    unnamed x28 -> x34, local copies, waits for them, and re-layouts: 3.11 us -> 3.99 us
  transfers between devices with their start and end apart: 9 -> 13, of which waited for: 3 -> 6; matrix products, arithmetic and copies ran while one was open for 0% -> 0% of each run, Pallas kernels for 15% -> 10%
where the time goes in v2:
time: 102 us; the launch traced here: 101 us
  waiting for transfers between devices  40.4 us (40%)
  Pallas kernels  29.7 us (29%)
  starting transfers between devices  24.1 us (24%)
  local copies, waits for them, and re-layouts  4.13 us (4%)
  other arithmetic  1.97 us (2%)
    ppermute x11, waiting for transfers between devices, ring(): return lax.ppermute(x, axis, [(i, (i + step) % 4) for i in range(4)])  30.5 us
    ppermute x11, starting transfers between devices, ring(): return lax.ppermute(x, axis, [(i, (i + step) % 4) for i in range(4)])  20.4 us
    pallas_call x1, Pallas kernels, fast(): call(far_kernel, jax.ShapeDtypeStruct((128, 128), F32), [pltpu.VMEM((PACK...  10.2 us
    pallas_call x1, Pallas kernels, fast(): call(near_kernel, jax.ShapeDtypeStruct((8, 3 * PACKED), F32), [pltpu.VMEM...  10.1 us
    all_to_all x1, waiting for transfers between devices, fast(): lax.all_to_all(back, ('z', 'y'), split_axis=0, concat_axis=0, tiled=True)  7.67 us
    pallas_call x1, Pallas kernels, fast(): call(prep_kernel, (blocks, blocks), ins=[smem] + [vmem] * 4, cost=cheap)  4 us
    unnamed x34, local copies, waits for them, and re-layouts  3.99 us
    pallas_call x1, Pallas kernels, fast(): call(pack_kernel, jax.ShapeDtypeStruct((PACKED, WIDTH), BF16), [pltpu.VME...  3.79 us
  transfers between devices with their start and end apart: 13, of which 6 were waited for; matrix products, arithmetic and copies ran while one was open for 0% of the time, Pallas kernels for 10%

profile of v2, /device:TPU:0, one launch (start us, length us, event | category | flops | bytes accessed | tf_op | source)
XLA Modules:
  0.0 101.1 jit_solution(18270399930926029293)
XLA Ops:
  0.0 4.0 %shard_map.57 = (bf16[416,768]{1,0:T(8,128)(2,1)}, bf16[416,768]{1,0:T(8,128)(2,1)}) custom-call(s32[8]{0:T(128)} %assign_ref.1, bf16[512,768]{1,0:T(8,128)(2,1)} %emb_ref.1, s32[1,512]{1,0:T(1,128)} %bitcast.64, s32[1,512]{1,0:T(1,128)} %bitcast.66, s32[1,512]{1,0:T(1,128)} %bitcast.63), custom_call_target="tpu_custom_call" | custom-call | flops 1000000000 | bytes 2000000 | tf_op jit(solution)/shard_map/pallas_call | solution.py:261
  4.0 0.0 collective-permute-start.2
  4.0 2.3 %collective-permute-done.2 = bf16[416,768]{1,0:T(8,128)(2,1)S(1)} collective-permute-done((bf16[416,768]{1,0:T(8,128)(2,1)}, bf16[416,768]{1,0:T(8,128)(2,1)S(1)}, u32[]{:S(2)}, u32[]{:S(2)}) %collective-permute-start.2) | collective-permute-done | bytes 639008 | tf_op jit(solution)/shard_map/ppermute | solution.py:267
  6.3 2.0 %pad_maximum_fusion = (bf16[1,2,104,768]{3,2,1,0:T(8,128)(2,1)S(1)}, bf16[1,2,104,768]{3,2,1,0:T(8,128)(2,1)}, bf16[1,2,104,768]{3,2,1,0:T(8,128)(2,1)S(1)}, bf16[1,2,104,768]{3,2,1,0:T(8,128)(2,1)S(1)}) fusion(bf16[4,1,104,768]{3,2,1,0:T(8,128)(2,1)S(1)} %bitcast.54, bf16[4,1,104,768]{3,2,1,0:T(8,128)(2,1)} %bitcast.53), kind=kLoop, calls=%fused_computation.37 | loop fusion | flops 638976 | bytes 2555904 | tf_op jit(solution)/shard_map/concatenate | solution.py:269
  8.3 1.6 %collective-permute-start.3 = (bf16[208,768]{1,0:T(8,128)(2,1)S(1)}, bf16[208,768]{1,0:T(8,128)(2,1)S(1)}, u32[]{:S(2)}, u32[]{:S(2)}) collective-permute-start(bf16[208,768]{1,0:T(8,128)(2,1)S(1)} %bitcast.59), channel_id=1, source_target_pairs={{0,32},{32,64},{64,96},{96,0},{1,33},{33,65},{65,97},{97,1},{2,34}... | collective-permute-start | bytes 958472 | tf_op jit(solution)/shard_map/ppermute | solution.py:252
  9.8 2.7 %collective-permute-start.4 = (bf16[208,768]{1,0:T(8,128)(2,1)S(1)}, bf16[208,768]{1,0:T(8,128)(2,1)S(1)}, u32[]{:S(2)}, u32[]{:S(2)}) collective-permute-start(bf16[208,768]{1,0:T(8,128)(2,1)S(1)} %bitcast.58), channel_id=1, source_target_pairs={{0,64},{32,96},{64,0},{96,32},{1,65},{33,97},{65,1},{97,33},{2,66}... | collective-permute-start | bytes 958472 | tf_op jit(solution)/shard_map/ppermute | solution.py:252
  12.6 1.4 %collective-permute-start.5 = (bf16[208,768]{1,0:T(8,128)(2,1)S(1)}, bf16[208,768]{1,0:T(8,128)(2,1)S(1)}, u32[]{:S(2)}, u32[]{:S(2)}) collective-permute-start(bf16[208,768]{1,0:T(8,128)(2,1)S(1)} %bitcast.57), channel_id=1, source_target_pairs={{0,96},{32,0},{64,32},{96,64},{1,97},{33,1},{65,33},{97,65},{2,98}... | collective-permute-start | bytes 958472 | tf_op jit(solution)/shard_map/ppermute | solution.py:252
  14.0 5.0 %collective-permute-done.3.from1_ref = bf16[208,768]{1,0:T(8,128)(2,1)S(1)} collective-permute-done((bf16[208,768]{1,0:T(8,128)(2,1)S(1)}, bf16[208,768]{1,0:T(8,128)(2,1)S(1)}, u32[]{:S(2)}, u32[]{:S(2)}) %collective-permute-start.3) | collective-permute-done | bytes 319520 | tf_op jit(solution)/shard_map/ppermute | solution.py:252
  19.1 0.0 copy-start.14
  19.1 7.9 %collective-permute-done.4.from2_ref = bf16[208,768]{1,0:T(8,128)(2,1)S(1)} collective-permute-done((bf16[208,768]{1,0:T(8,128)(2,1)S(1)}, bf16[208,768]{1,0:T(8,128)(2,1)S(1)}, u32[]{:S(2)}, u32[]{:S(2)}) %collective-permute-start.4) | collective-permute-done | bytes 319520 | tf_op jit(solution)/shard_map/ppermute | solution.py:252
  27.0 0.0 collective-permute-done.5.from3_ref
  27.0 0.0 copy-start.16
  27.0 0.0 copy-done.14
  27.0 0.7 copy-done.15
  27.7 0.1 copy-done.16
  27.8 3.8 %shard_map.58.own = bf16[640,768]{1,0:T(8,128)(2,1)} custom-call(bf16[208,768]{1,0:T(8,128)(2,1)} %bitcast.56, bf16[208,768]{1,0:T(8,128)(2,1)} %copy-done.14, bf16[208,768]{1,0:T(8,128)(2,1)} %copy-done.15, bf16[208,768]{1,0:T(8,128)(2,1)} %copy-done.16), custom_call_target="tpu_custom_call" | custom-call | flops 1000000000 | bytes 2000000 | tf_op jit(solution)/shard_map/pallas_call | solution.py:270
  31.6 1.6 %collective-permute-start.6 = (bf16[640,768]{1,0:T(8,128)(2,1)}, bf16[640,768]{1,0:T(8,128)(2,1)S(1)}, u32[]{:S(2)}, u32[]{:S(2)}) collective-permute-start(bf16[640,768]{1,0:T(8,128)(2,1)} %shard_map.58.own), channel_id=1, source_target_pairs={{0,1},{1,2},{2,3},{3,0},{4,5},{5,6},{6,7},{7,4},{8,9},{9,10},{10,1... | collective-permute-start | bytes 2949128 | tf_op jit(solution)/shard_map/ppermute | solution.py:252
  33.2 1.7 %collective-permute-start.7 = (bf16[640,768]{1,0:T(8,128)(2,1)}, bf16[640,768]{1,0:T(8,128)(2,1)S(1)}, u32[]{:S(2)}, u32[]{:S(2)}) collective-permute-start(bf16[640,768]{1,0:T(8,128)(2,1)} %shard_map.58.own), channel_id=1, source_target_pairs={{0,3},{1,0},{2,1},{3,2},{4,7},{5,4},{6,5},{7,6},{8,11},{9,8},{10,9... | collective-permute-start | bytes 2949128 | tf_op jit(solution)/shard_map/ppermute | solution.py:252
  34.8 1.9 %collective-permute-start.10 = (bf16[640,768]{1,0:T(8,128)(2,1)}, bf16[640,768]{1,0:T(8,128)(2,1)S(1)}, u32[]{:S(2)}, u32[]{:S(2)}) collective-permute-start(bf16[640,768]{1,0:T(8,128)(2,1)} %shard_map.58.own), channel_id=1, source_target_pairs={{0,4},{4,8},{8,12},{12,0},{1,5},{5,9},{9,13},{13,1},{2,6},{6,10},{... | collective-permute-start | bytes 2949128 | tf_op jit(solution)/shard_map/ppermute | solution.py:252
  36.8 2.1 %collective-permute-start.11 = (bf16[640,768]{1,0:T(8,128)(2,1)}, bf16[640,768]{1,0:T(8,128)(2,1)S(1)}, u32[]{:S(2)}, u32[]{:S(2)}) collective-permute-start(bf16[640,768]{1,0:T(8,128)(2,1)} %shard_map.58.own), channel_id=1, source_target_pairs={{0,12},{4,0},{8,4},{12,8},{1,13},{5,1},{9,5},{13,9},{2,14},{6,2},{... | collective-permute-start | bytes 2949128 | tf_op jit(solution)/shard_map/ppermute | solution.py:252
  38.9 17.2 %collective-permute-done.6.y1 = bf16[640,768]{1,0:T(8,128)(2,1)S(1)} collective-permute-done((bf16[640,768]{1,0:T(8,128)(2,1)}, bf16[640,768]{1,0:T(8,128)(2,1)S(1)}, u32[]{:S(2)}, u32[]{:S(2)}) %collective-permute-start.6) | collective-permute-done | bytes 983072 | tf_op jit(solution)/shard_map/ppermute | solution.py:252
  56.0 0.0 copy-start.2
  56.1 0.4 collective-permute-start.8
  56.5 0.0 collective-permute-done.7.y3
  56.5 0.0 copy-start.3
  56.5 3.0 %collective-permute-start.9 = (bf16[320,768]{1,0:T(8,128)(2,1)S(1)}, bf16[320,768]{1,0:T(8,128)(2,1)S(1)}, u32[]{:S(2)}, u32[]{:S(2)}) collective-permute-start(bf16[320,768]{1,0:T(8,128)(2,1)S(1)} %slice.43), channel_id=1, source_target_pairs={{0,3},{1,0},{2,1},{3,2},{4,7},{5,4},{6,5},{7,6},{8,11},{9,8},{10,9... | collective-permute-start | bytes 1474568 | tf_op jit(solution)/shard_map/ppermute | solution.py:252
  59.5 0.3 collective-permute-done.10.z1
  59.8 0.0 copy-start.4
  59.9 1.7 %collective-permute-start.12 = (bf16[320,768]{1,0:T(8,128)(2,1)S(1)}, bf16[320,768]{1,0:T(8,128)(2,1)S(1)}, u32[]{:S(2)}, u32[]{:S(2)}) collective-permute-start(bf16[320,768]{1,0:T(8,128)(2,1)S(1)} %slice.44), channel_id=1, source_target_pairs={{0,4},{4,8},{8,12},{12,0},{1,5},{5,9},{9,13},{13,1},{2,6},{6,10},{... | collective-permute-start | bytes 1474568 | tf_op jit(solution)/shard_map/ppermute | solution.py:252
  61.5 0.0 collective-permute-done.11.z3
  61.5 0.0 copy-start.5
  61.6 0.0 copy-done.2
  61.6 2.4 %collective-permute-start.13 = (bf16[320,768]{1,0:T(8,128)(2,1)S(1)}, bf16[320,768]{1,0:T(8,128)(2,1)S(1)}, u32[]{:S(2)}, u32[]{:S(2)}) collective-permute-start(bf16[320,768]{1,0:T(8,128)(2,1)S(1)} %slice.45), channel_id=1, source_target_pairs={{0,12},{4,0},{8,4},{12,8},{1,13},{5,1},{9,5},{13,9},{2,14},{6,2},{... | collective-permute-start | bytes 1474568 | tf_op jit(solution)/shard_map/ppermute | solution.py:252
  64.0 0.0 copy-done.3
  64.0 0.0 copy-done.4
  64.0 0.0 copy-done.5
  64.0 10.1 %shard_map.59.near_ref = f32[8,1920]{1,0:T(8,128)} custom-call(bf16[640,768]{1,0:T(8,128)(2,1)} %shard_map.58.own, bf16[640,768]{1,0:T(8,128)(2,1)} %copy-done.2, bf16[640,768]{1,0:T(8,128)(2,1)} %copy-done.3, bf16[640,768]{1,0:T(8,128)(2,1)} %copy-done.4, bf16[640,768]{1,0:T(8,128)(2,1)} %copy-done.5), custom_call_target="tpu_custom_call" | custom-call | flops 5662310400 | bytes 6000000 | tf_op jit(solution)/shard_map/pallas_call | solution.py:281
  74.1 0.0 copy-start
  74.1 0.0 copy-start.7
  74.1 0.0 copy-start.8
  74.1 0.0 copy-start.9
  74.1 0.0 collective-permute-done.8.y2a
  74.1 0.0 copy-start.10
  74.1 0.0 collective-permute-done.9.y2b
  74.2 0.0 copy-start.11
  74.2 0.0 collective-permute-done.12.z2a
  74.2 0.0 copy-start.12
  74.2 0.0 collective-permute-done.13.z2b
  74.2 0.7 copy-done.10
  74.9 0.2 copy-done.11
  75.1 0.2 copy-done.12
  75.3 0.0 copy-start.13
  75.3 0.8 copy-done.13
  76.1 10.2 %shard_map.60 = f32[128,128]{1,0:T(8,128)} custom-call(bf16[640,768]{1,0:T(8,128)(2,1)} %shard_map.58.own, bf16[640,768]{1,0:T(8,128)(2,1)} %copy-done.2, bf16[640,768]{1,0:T(8,128)(2,1)} %copy-done.3, bf16[320,768]{1,0:T(8,128)(2,1)} %copy-done.10, bf16[320,768]{1,0:T(8,128)(2,1)} %copy-done.11, bf16[640,768]{1,0:T(8,128)(2,1)} %copy-done.4, ...), custom_call_target="tpu_custom_call" | custom-call | flops 4404019200 | bytes 8000000 | tf_op jit(solution)/shard_map/pallas_call | solution.py:287
  86.3 3.6 %all-to-all-start.2 = ((f32[16,8,128]{2,1,0:T(8,128)}), f32[16,8,128]{2,1,0:T(8,128)S(1)}, u32[]{:S(2)}, u32[]{:S(2)}) async-start(f32[16,8,128]{2,1,0:T(8,128)} %bitcast.62), calls=%async_computation.2 | async-start | bytes 131072 | tf_op jit(solution)/shard_map/all_to_all | solution.py:293
  90.0 7.7 %all-to-all-done.2 = f32[16,8,128]{2,1,0:T(8,128)S(1)} async-done(((f32[16,8,128]{2,1,0:T(8,128)}), f32[16,8,128]{2,1,0:T(8,128)S(1)}, u32[]{:S(2)}, u32[]{:S(2)}) %all-to-all-start.2) | async-done | bytes 65568 | tf_op jit(solution)/shard_map/all_to_all | solution.py:293
  97.6 0.6 copy-done.1
  98.3 1.5 %shard_map.61 = (f32[8,128]{1,0:T(8,128)S(1)}, s32[1,1]{1,0:T(1,128)}) custom-call(f32[128,128]{1,0:T(8,128)} %bitcast.60), custom_call_target="tpu_custom_call" | custom-call | tf_op jit(solution)/shard_map/pallas_call | solution.py:294
  100.5 0.0 copy-done
  100.5 0.0 copy-done.7
  100.5 0.0 copy-done.8
  100.5 0.0 copy-done.9
  100.5 0.0 copy-start.17
  100.5 0.6 copy-done.17
  (7 shorter events, 0.1 us)
Async XLA Ops:
  4.0 2.3 %collective-permute-start.2 = (bf16[416,768]{1,0:T(8,128)(2,1)}, bf16[416,768]{1,0:T(8,128)(2,1)S(1)}, u32[]{:S(2)}, u32[]{:S(2)}) collective-permute-start(bf16[416,768]{1,0:T(8,128)(2,1)} %get-tuple-element.95), channel_id=1, source_target_pairs={{0,16},{16,0},{1,17},{17,1},{2,18},{18,2},{3,19},{19,3},{4,20},{20... | collective-permute-start | bytes 1916936 | tf_op jit(solution)/shard_map/ppermute | solution.py:267
  8.3 10.8 %collective-permute-start.3 = (bf16[208,768]{1,0:T(8,128)(2,1)S(1)}, bf16[208,768]{1,0:T(8,128)(2,1)S(1)}, u32[]{:S(2)}, u32[]{:S(2)}) collective-permute-start(bf16[208,768]{1,0:T(8,128)(2,1)S(1)} %bitcast.59), channel_id=1, source_target_pairs={{0,32},{32,64},{64,96},{96,0},{1,33},{33,65},{65,97},{97,1},{2,34}... | collective-permute-start | bytes 958472 | tf_op jit(solution)/shard_map/ppermute | solution.py:252
  9.8 17.1 %collective-permute-start.4 = (bf16[208,768]{1,0:T(8,128)(2,1)S(1)}, bf16[208,768]{1,0:T(8,128)(2,1)S(1)}, u32[]{:S(2)}, u32[]{:S(2)}) collective-permute-start(bf16[208,768]{1,0:T(8,128)(2,1)S(1)} %bitcast.58), channel_id=1, source_target_pairs={{0,64},{32,96},{64,0},{96,32},{1,65},{33,97},{65,1},{97,33},{2,66}... | collective-permute-start | bytes 958472 | tf_op jit(solution)/shard_map/ppermute | solution.py:252
  12.6 14.4 %collective-permute-start.5 = (bf16[208,768]{1,0:T(8,128)(2,1)S(1)}, bf16[208,768]{1,0:T(8,128)(2,1)S(1)}, u32[]{:S(2)}, u32[]{:S(2)}) collective-permute-start(bf16[208,768]{1,0:T(8,128)(2,1)S(1)} %bitcast.57), channel_id=1, source_target_pairs={{0,96},{32,0},{64,32},{96,64},{1,97},{33,1},{65,33},{97,65},{2,98}... | collective-permute-start | bytes 958472 | tf_op jit(solution)/shard_map/ppermute | solution.py:252
  19.1 7.9 %copy-start.14 = (bf16[208,768]{1,0:T(8,128)(2,1)}, bf16[208,768]{1,0:T(8,128)(2,1)S(1)}, u32[]{:S(2)}) copy-start(bf16[208,768]{1,0:T(8,128)(2,1)S(1)} %collective-permute-done.3.from1_ref) | copy-start | bytes 958468
  27.0 0.8 copy-start.15
  27.0 0.8 copy-start.16
  31.6 24.5 %collective-permute-start.6 = (bf16[640,768]{1,0:T(8,128)(2,1)}, bf16[640,768]{1,0:T(8,128)(2,1)S(1)}, u32[]{:S(2)}, u32[]{:S(2)}) collective-permute-start(bf16[640,768]{1,0:T(8,128)(2,1)} %shard_map.58.own), channel_id=1, source_target_pairs={{0,1},{1,2},{2,3},{3,0},{4,5},{5,6},{6,7},{7,4},{8,9},{9,10},{10,1... | collective-permute-start | bytes 2949128 | tf_op jit(solution)/shard_map/ppermute | solution.py:252
  33.2 23.3 %collective-permute-start.7 = (bf16[640,768]{1,0:T(8,128)(2,1)}, bf16[640,768]{1,0:T(8,128)(2,1)S(1)}, u32[]{:S(2)}, u32[]{:S(2)}) collective-permute-start(bf16[640,768]{1,0:T(8,128)(2,1)} %shard_map.58.own), channel_id=1, source_target_pairs={{0,3},{1,0},{2,1},{3,2},{4,7},{5,4},{6,5},{7,6},{8,11},{9,8},{10,9... | collective-permute-start | bytes 2949128 | tf_op jit(solution)/shard_map/ppermute | solution.py:252
  34.8 25.0 %collective-permute-start.10 = (bf16[640,768]{1,0:T(8,128)(2,1)}, bf16[640,768]{1,0:T(8,128)(2,1)S(1)}, u32[]{:S(2)}, u32[]{:S(2)}) collective-permute-start(bf16[640,768]{1,0:T(8,128)(2,1)} %shard_map.58.own), channel_id=1, source_target_pairs={{0,4},{4,8},{8,12},{12,0},{1,5},{5,9},{9,13},{13,1},{2,6},{6,10},{... | collective-permute-start | bytes 2949128 | tf_op jit(solution)/shard_map/ppermute | solution.py:252
  36.8 24.8 %collective-permute-start.11 = (bf16[640,768]{1,0:T(8,128)(2,1)}, bf16[640,768]{1,0:T(8,128)(2,1)S(1)}, u32[]{:S(2)}, u32[]{:S(2)}) collective-permute-start(bf16[640,768]{1,0:T(8,128)(2,1)} %shard_map.58.own), channel_id=1, source_target_pairs={{0,12},{4,0},{8,4},{12,8},{1,13},{5,1},{9,5},{13,9},{2,14},{6,2},{... | collective-permute-start | bytes 2949128 | tf_op jit(solution)/shard_map/ppermute | solution.py:252
  56.0 5.5 %copy-start.2 = (bf16[640,768]{1,0:T(8,128)(2,1)}, bf16[640,768]{1,0:T(8,128)(2,1)S(1)}, u32[]{:S(2)}) copy-start(bf16[640,768]{1,0:T(8,128)(2,1)S(1)} %collective-permute-done.6.y1) | copy-start | bytes 2949124
  56.1 18.0 %collective-permute-start.8 = (bf16[320,768]{1,0:T(8,128)(2,1)S(1)}, bf16[320,768]{1,0:T(8,128)(2,1)S(1)}, u32[]{:S(2)}, u32[]{:S(2)}) collective-permute-start(bf16[320,768]{1,0:T(8,128)(2,1)S(1)} %slice.42), channel_id=1, source_target_pairs={{0,1},{1,2},{2,3},{3,0},{4,5},{5,6},{6,7},{7,4},{8,9},{9,10},{10,1... | collective-permute-start | bytes 1474568 | tf_op jit(solution)/shard_map/ppermute | solution.py:252
  56.5 7.5 %copy-start.3 = (bf16[640,768]{1,0:T(8,128)(2,1)}, bf16[640,768]{1,0:T(8,128)(2,1)S(1)}, u32[]{:S(2)}) copy-start(bf16[640,768]{1,0:T(8,128)(2,1)S(1)} %collective-permute-done.7.y3) | copy-start | bytes 2949124
  56.5 17.6 %collective-permute-start.9 = (bf16[320,768]{1,0:T(8,128)(2,1)S(1)}, bf16[320,768]{1,0:T(8,128)(2,1)S(1)}, u32[]{:S(2)}, u32[]{:S(2)}) collective-permute-start(bf16[320,768]{1,0:T(8,128)(2,1)S(1)} %slice.43), channel_id=1, source_target_pairs={{0,3},{1,0},{2,1},{3,2},{4,7},{5,4},{6,5},{7,6},{8,11},{9,8},{10,9... | collective-permute-start | bytes 1474568 | tf_op jit(solution)/shard_map/ppermute | solution.py:252
  59.8 4.1 %copy-start.4 = (bf16[640,768]{1,0:T(8,128)(2,1)}, bf16[640,768]{1,0:T(8,128)(2,1)S(1)}, u32[]{:S(2)}) copy-start(bf16[640,768]{1,0:T(8,128)(2,1)S(1)} %collective-permute-done.10.z1) | copy-start | bytes 2949124
  59.9 14.3 %collective-permute-start.12 = (bf16[320,768]{1,0:T(8,128)(2,1)S(1)}, bf16[320,768]{1,0:T(8,128)(2,1)S(1)}, u32[]{:S(2)}, u32[]{:S(2)}) collective-permute-start(bf16[320,768]{1,0:T(8,128)(2,1)S(1)} %slice.44), channel_id=1, source_target_pairs={{0,4},{4,8},{8,12},{12,0},{1,5},{5,9},{9,13},{13,1},{2,6},{6,10},{... | collective-permute-start | bytes 1474568 | tf_op jit(solution)/shard_map/ppermute | solution.py:252
  61.5 2.5 %copy-start.5 = (bf16[640,768]{1,0:T(8,128)(2,1)}, bf16[640,768]{1,0:T(8,128)(2,1)S(1)}, u32[]{:S(2)}) copy-start(bf16[640,768]{1,0:T(8,128)(2,1)S(1)} %collective-permute-done.11.z3) | copy-start | bytes 2949124
  61.6 12.6 %collective-permute-start.13 = (bf16[320,768]{1,0:T(8,128)(2,1)S(1)}, bf16[320,768]{1,0:T(8,128)(2,1)S(1)}, u32[]{:S(2)}, u32[]{:S(2)}) collective-permute-start(bf16[320,768]{1,0:T(8,128)(2,1)S(1)} %slice.45), channel_id=1, source_target_pairs={{0,12},{4,0},{8,4},{12,8},{1,13},{5,1},{9,5},{13,9},{2,14},{6,2},{... | collective-permute-start | bytes 1474568 | tf_op jit(solution)/shard_map/ppermute | solution.py:252
  74.1 26.4 %copy-start = (bf16[512,768]{1,0:T(8,128)(2,1)S(1)}, bf16[512,768]{1,0:T(8,128)(2,1)}, u32[]{:S(2)}) copy-start(bf16[512,768]{1,0:T(8,128)(2,1)} %emb_ref.1) | copy-start | bytes 2359300
  74.1 26.4 %copy-start.7 = (s32[512]{0:T(512)S(1)}, s32[512]{0:T(512)}, u32[]{:S(2)}) copy-start(s32[512]{0:T(512)} %param.15) | copy-start | bytes 6148
  74.1 26.4 %copy-start.8 = (s32[512]{0:T(512)S(1)}, s32[512]{0:T(512)}, u32[]{:S(2)}) copy-start(s32[512]{0:T(512)} %param.12) | copy-start | bytes 6148
  74.1 26.4 %copy-start.9 = (s32[8]{0:T(128)S(1)}, s32[8]{0:T(128)}, u32[]{:S(2)}) copy-start(s32[8]{0:T(128)} %assign_ref.1) | copy-start | bytes 100
  74.1 0.8 copy-start.10
  74.2 1.0 copy-start.11
  74.2 1.1 %copy-start.12 = (bf16[320,768]{1,0:T(8,128)(2,1)}, bf16[320,768]{1,0:T(8,128)(2,1)S(1)}, u32[]{:S(2)}) copy-start(bf16[320,768]{1,0:T(8,128)(2,1)S(1)} %collective-permute-done.12.z2a) | copy-start | bytes 1474564
  75.3 0.8 copy-start.13
  86.3 11.3 %all-to-all-start.2 = ((f32[16,8,128]{2,1,0:T(8,128)}), f32[16,8,128]{2,1,0:T(8,128)S(1)}, u32[]{:S(2)}, u32[]{:S(2)}) async-start(f32[16,8,128]{2,1,0:T(8,128)} %bitcast.62), calls=%async_computation.2 | async-start | bytes 131072 | tf_op jit(solution)/shard_map/all_to_all | solution.py:293
  97.6 0.6 copy-start.1
  100.5 0.6 copy-start.17

commit v3 on v2

--- a/solution.py
+++ b/solution.py
@@ -20,7 +20,7 @@
 PACKED = 640
 HELD = PACKED - 16
 FAR = 256.0
-VMEM = 56 * 2**20
+VMEM = 16 * 2**20
 
 
 def iota(shape, axis):

time: 102 us -> 90.5 us (0.89)
  Pallas kernels: 29.7 us -> 19.9 us
  local copies, waits for them, and re-layouts: 4.13 us -> 0.74 us
  starting transfers between devices: 24.1 us -> 26 us
  other arithmetic: 1.97 us -> 0.11 us
  waiting for transfers between devices: 40.4 us -> 41.8 us
    unnamed x34 -> x10, local copies, waits for them, and re-layouts: 3.99 us -> 0.61 us
    pallas_call x1, Pallas kernels: 10.1 us -> 7.11 us  [fast(): call(near_kernel, jax.ShapeDtypeStruct((8, 3 * PACKED), F32), [pltpu.VMEM...]
    pallas_call x1, Pallas kernels: 10.2 us -> 7.39 us  [fast(): call(far_kernel, jax.ShapeDtypeStruct((128, 128), F32), [pltpu.VMEM((PACK...]
    pallas_call x1, Pallas kernels: 3.79 us -> 1.55 us  [fast(): call(pack_kernel, jax.ShapeDtypeStruct((PACKED, WIDTH), BF16), [pltpu.VME...]
    concatenate x1, other arithmetic: 1.97 us -> 0.11 us  [fast(): jnp.concatenate([same.reshape(shape), other.reshape(shape)], axis=1)]
    all_to_all x1, starting transfers between devices: 3.61 us -> 5.42 us  [fast(): lax.all_to_all(back, ('z', 'y'), split_axis=0, concat_axis=0, tiled=True)]
    ppermute x11, waiting for transfers between devices: 30.5 us -> 32.1 us  [ring(): return lax.ppermute(x, axis, [(i, (i + step) % 4) for i in range(4)])]
  transfers between devices with their start and end apart: 13 -> 13, of which waited for: 6 -> 7; matrix products, arithmetic and copies ran while one was open for 0% -> 0% of each run, Pallas kernels for 10% -> 8%
where the time goes in v3:
time: 90.5 us; the launch traced here: 89.4 us
  waiting for transfers between devices  41.8 us (46%)
  starting transfers between devices  26 us (29%)
  Pallas kernels  19.9 us (22%)
    ppermute x11, waiting for transfers between devices, ring(): return lax.ppermute(x, axis, [(i, (i + step) % 4) for i in range(4)])  32.1 us
    ppermute x11, starting transfers between devices, ring(): return lax.ppermute(x, axis, [(i, (i + step) % 4) for i in range(4)])  20.5 us
    all_to_all x1, waiting for transfers between devices, fast(): lax.all_to_all(back, ('z', 'y'), split_axis=0, concat_axis=0, tiled=True)  7.67 us
    pallas_call x1, Pallas kernels, fast(): call(far_kernel, jax.ShapeDtypeStruct((128, 128), F32), [pltpu.VMEM((PACK...  7.39 us
    pallas_call x1, Pallas kernels, fast(): call(near_kernel, jax.ShapeDtypeStruct((8, 3 * PACKED), F32), [pltpu.VMEM...  7.11 us
    all_to_all x1, starting transfers between devices, fast(): lax.all_to_all(back, ('z', 'y'), split_axis=0, concat_axis=0, tiled=True)  5.42 us
    pallas_call x1, Pallas kernels, fast(): call(prep_kernel, (blocks, blocks), ins=[smem] + [vmem] * 4, cost=cheap)  3.15 us
    ppermute x1, waiting for transfers between devices, fast(): other = lax.ppermute(other, 'core', [(0, 1), (1, 0)])  2.06 us
  transfers between devices with their start and end apart: 13, of which 7 were waited for; matrix products, arithmetic and copies ran while one was open for 0% of the time, Pallas kernels for 8%

profile of v3, /device:TPU:0, one launch (start us, length us, event | category | flops | bytes accessed | tf_op | source)
XLA Modules:
  0.0 89.4 jit_solution(15788704012889784012)
XLA Ops:
  0.0 3.1 %shard_map.57 = (bf16[416,768]{1,0:T(8,128)(2,1)S(1)}, bf16[416,768]{1,0:T(8,128)(2,1)S(1)}) custom-call(s32[8]{0:T(128)} %assign_ref.1, bf16[512,768]{1,0:T(8,128)(2,1)} %emb_ref.1, s32[1,512]{1,0:T(1,128)} %bitcast.63, s32[1,512]{1,0:T(1,128)} %bitcast.65, s32[1,512]{1,0:T(1,128)} %bitcast.62), custom_call_target="tpu_custom_call" | custom-call | flops 1000000000 | bytes 2000000 | tf_op jit(solution)/shard_map/pallas_call | solution.py:261
  3.2 0.1 collective-permute-start.2
  3.2 2.1 %collective-permute-done.2 = bf16[416,768]{1,0:T(8,128)(2,1)S(1)} collective-permute-done((bf16[416,768]{1,0:T(8,128)(2,1)S(1)}, bf16[416,768]{1,0:T(8,128)(2,1)S(1)}, u32[]{:S(2)}, u32[]{:S(2)}) %collective-permute-start.2) | collective-permute-done | bytes 639008 | tf_op jit(solution)/shard_map/ppermute | solution.py:267
  5.3 0.1 pad_maximum_fusion
  5.4 1.6 %collective-permute-start.3 = (bf16[208,768]{1,0:T(8,128)(2,1)S(1)}, bf16[208,768]{1,0:T(8,128)(2,1)S(1)}, u32[]{:S(2)}, u32[]{:S(2)}) collective-permute-start(bf16[208,768]{1,0:T(8,128)(2,1)S(1)} %bitcast.60), channel_id=1, source_target_pairs={{0,32},{32,64},{64,96},{96,0},{1,33},{33,65},{65,97},{97,1},{2,34}... | collective-permute-start | bytes 958472 | tf_op jit(solution)/shard_map/ppermute | solution.py:252
  7.1 2.7 %collective-permute-start.4 = (bf16[208,768]{1,0:T(8,128)(2,1)S(1)}, bf16[208,768]{1,0:T(8,128)(2,1)S(1)}, u32[]{:S(2)}, u32[]{:S(2)}) collective-permute-start(bf16[208,768]{1,0:T(8,128)(2,1)S(1)} %bitcast.59), channel_id=1, source_target_pairs={{0,64},{32,96},{64,0},{96,32},{1,65},{33,97},{65,1},{97,33},{2,66}... | collective-permute-start | bytes 958472 | tf_op jit(solution)/shard_map/ppermute | solution.py:252
  9.8 1.4 %collective-permute-start.5 = (bf16[208,768]{1,0:T(8,128)(2,1)S(1)}, bf16[208,768]{1,0:T(8,128)(2,1)S(1)}, u32[]{:S(2)}, u32[]{:S(2)}) collective-permute-start(bf16[208,768]{1,0:T(8,128)(2,1)S(1)} %bitcast.58), channel_id=1, source_target_pairs={{0,96},{32,0},{64,32},{96,64},{1,97},{33,1},{65,33},{97,65},{2,98}... | collective-permute-start | bytes 958472 | tf_op jit(solution)/shard_map/ppermute | solution.py:252
  11.2 5.0 %collective-permute-done.3.from1_ref = bf16[208,768]{1,0:T(8,128)(2,1)S(1)} collective-permute-done((bf16[208,768]{1,0:T(8,128)(2,1)S(1)}, bf16[208,768]{1,0:T(8,128)(2,1)S(1)}, u32[]{:S(2)}, u32[]{:S(2)}) %collective-permute-start.3) | collective-permute-done | bytes 319520 | tf_op jit(solution)/shard_map/ppermute | solution.py:252
  16.3 7.9 %collective-permute-done.4.from2_ref = bf16[208,768]{1,0:T(8,128)(2,1)S(1)} collective-permute-done((bf16[208,768]{1,0:T(8,128)(2,1)S(1)}, bf16[208,768]{1,0:T(8,128)(2,1)S(1)}, u32[]{:S(2)}, u32[]{:S(2)}) %collective-permute-start.4) | collective-permute-done | bytes 319520 | tf_op jit(solution)/shard_map/ppermute | solution.py:252
  24.2 0.0 collective-permute-done.5.from3_ref
  24.2 1.5 %shard_map.58.own = bf16[640,768]{1,0:T(8,128)(2,1)S(1)} custom-call(bf16[208,768]{1,0:T(8,128)(2,1)S(1)} %bitcast.48, bf16[208,768]{1,0:T(8,128)(2,1)S(1)} %collective-permute-done.3.from1_ref, bf16[208,768]{1,0:T(8,128)(2,1)S(1)} %collective-permute-done.4.from2_ref, bf16[208,768]{1,0:T(8,128)(2,1)S(1)} %collective-permute-done.5.from3_ref), custom_call_target="tpu_custom_call" | custom-call | flops 1000000000 | bytes 2000000 | tf_op jit(solution)/shard_map/pallas_call | solution.py:270
  25.8 1.6 %collective-permute-start.6 = (bf16[640,768]{1,0:T(8,128)(2,1)S(1)}, bf16[640,768]{1,0:T(8,128)(2,1)S(1)}, u32[]{:S(2)}, u32[]{:S(2)}) collective-permute-start(bf16[640,768]{1,0:T(8,128)(2,1)S(1)} %shard_map.58.own), channel_id=1, source_target_pairs={{0,1},{1,2},{2,3},{3,0},{4,5},{5,6},{6,7},{7,4},{8,9},{9,10},{10,1... | collective-permute-start | bytes 2949128 | tf_op jit(solution)/shard_map/ppermute | solution.py:252
  27.4 1.7 %collective-permute-start.7 = (bf16[640,768]{1,0:T(8,128)(2,1)S(1)}, bf16[640,768]{1,0:T(8,128)(2,1)S(1)}, u32[]{:S(2)}, u32[]{:S(2)}) collective-permute-start(bf16[640,768]{1,0:T(8,128)(2,1)S(1)} %shard_map.58.own), channel_id=1, source_target_pairs={{0,3},{1,0},{2,1},{3,2},{4,7},{5,4},{6,5},{7,6},{8,11},{9,8},{10,9... | collective-permute-start | bytes 2949128 | tf_op jit(solution)/shard_map/ppermute | solution.py:252
  29.1 1.9 %collective-permute-start.10 = (bf16[640,768]{1,0:T(8,128)(2,1)S(1)}, bf16[640,768]{1,0:T(8,128)(2,1)S(1)}, u32[]{:S(2)}, u32[]{:S(2)}) collective-permute-start(bf16[640,768]{1,0:T(8,128)(2,1)S(1)} %shard_map.58.own), channel_id=1, source_target_pairs={{0,4},{4,8},{8,12},{12,0},{1,5},{5,9},{9,13},{13,1},{2,6},{6,10},{... | collective-permute-start | bytes 2949128 | tf_op jit(solution)/shard_map/ppermute | solution.py:252
  31.0 2.1 %collective-permute-start.11 = (bf16[640,768]{1,0:T(8,128)(2,1)S(1)}, bf16[640,768]{1,0:T(8,128)(2,1)S(1)}, u32[]{:S(2)}, u32[]{:S(2)}) collective-permute-start(bf16[640,768]{1,0:T(8,128)(2,1)S(1)} %shard_map.58.own), channel_id=1, source_target_pairs={{0,12},{4,0},{8,4},{12,8},{1,13},{5,1},{9,5},{13,9},{2,14},{6,2},{... | collective-permute-start | bytes 2949128 | tf_op jit(solution)/shard_map/ppermute | solution.py:252
  33.1 17.0 %collective-permute-done.6.y1 = bf16[640,768]{1,0:T(8,128)(2,1)S(1)} collective-permute-done((bf16[640,768]{1,0:T(8,128)(2,1)S(1)}, bf16[640,768]{1,0:T(8,128)(2,1)S(1)}, u32[]{:S(2)}, u32[]{:S(2)}) %collective-permute-start.6) | collective-permute-done | bytes 983072 | tf_op jit(solution)/shard_map/ppermute | solution.py:252
  50.1 0.4 collective-permute-start.8
  50.5 0.0 collective-permute-done.7.y3
  50.5 3.0 %collective-permute-start.9 = (bf16[320,768]{1,0:T(8,128)(2,1)S(1)}, bf16[320,768]{1,0:T(8,128)(2,1)S(1)}, u32[]{:S(2)}, u32[]{:S(2)}) collective-permute-start(bf16[320,768]{1,0:T(8,128)(2,1)S(1)} %slice.43), channel_id=1, source_target_pairs={{0,3},{1,0},{2,1},{3,2},{4,7},{5,4},{6,5},{7,6},{8,11},{9,8},{10,9... | collective-permute-start | bytes 1474568 | tf_op jit(solution)/shard_map/ppermute | solution.py:252
  53.5 0.4 collective-permute-done.10.z1
  53.9 1.6 %collective-permute-start.12 = (bf16[320,768]{1,0:T(8,128)(2,1)S(1)}, bf16[320,768]{1,0:T(8,128)(2,1)S(1)}, u32[]{:S(2)}, u32[]{:S(2)}) collective-permute-start(bf16[320,768]{1,0:T(8,128)(2,1)S(1)} %slice.44), channel_id=1, source_target_pairs={{0,4},{4,8},{8,12},{12,0},{1,5},{5,9},{9,13},{13,1},{2,6},{6,10},{... | collective-permute-start | bytes 1474568 | tf_op jit(solution)/shard_map/ppermute | solution.py:252
  55.5 0.0 collective-permute-done.11.z3
  55.6 2.4 %collective-permute-start.13 = (bf16[320,768]{1,0:T(8,128)(2,1)S(1)}, bf16[320,768]{1,0:T(8,128)(2,1)S(1)}, u32[]{:S(2)}, u32[]{:S(2)}) collective-permute-start(bf16[320,768]{1,0:T(8,128)(2,1)S(1)} %slice.45), channel_id=1, source_target_pairs={{0,12},{4,0},{8,4},{12,8},{1,13},{5,1},{9,5},{13,9},{2,14},{6,2},{... | collective-permute-start | bytes 1474568 | tf_op jit(solution)/shard_map/ppermute | solution.py:252
  58.0 7.1 %shard_map.59.near_ref = f32[8,1920]{1,0:T(8,128)S(1)} custom-call(bf16[640,768]{1,0:T(8,128)(2,1)S(1)} %shard_map.58.own, bf16[640,768]{1,0:T(8,128)(2,1)S(1)} %collective-permute-done.6.y1, bf16[640,768]{1,0:T(8,128)(2,1)S(1)} %collective-permute-done.7.y3, bf16[640,768]{1,0:T(8,128)(2,1)S(1)} %collective-permute-done.10.z1, ...), custom_call_target="tpu_custom_call" | custom-call | flops 5662310400 | bytes 6000000 | tf_op jit(solution)/shard_map/pallas_call | solution.py:281
  65.1 0.0 copy-start
  65.1 0.0 copy-start.2
  65.1 0.0 copy-start.3
  65.1 0.0 copy-start.4
  65.1 0.0 collective-permute-done.8.y2a
  65.2 0.0 collective-permute-done.9.y2b
  65.2 1.8 %collective-permute-done.12.z2a = bf16[320,768]{1,0:T(8,128)(2,1)S(1)} collective-permute-done((bf16[320,768]{1,0:T(8,128)(2,1)S(1)}, bf16[320,768]{1,0:T(8,128)(2,1)S(1)}, u32[]{:S(2)}, u32[]{:S(2)}) %collective-permute-start.12) | collective-permute-done | bytes 491552 | tf_op jit(solution)/shard_map/ppermute | solution.py:252
  66.9 0.0 collective-permute-done.13.z2b
  66.9 7.4 %shard_map.60 = f32[128,128]{1,0:T(8,128)} custom-call(bf16[640,768]{1,0:T(8,128)(2,1)S(1)} %shard_map.58.own, bf16[640,768]{1,0:T(8,128)(2,1)S(1)} %collective-permute-done.6.y1, bf16[640,768]{1,0:T(8,128)(2,1)S(1)} %collective-permute-done.7.y3, bf16[320,768]{1,0:T(8,128)(2,1)S(1)} %collective-permute-done.8.y2a, ...), custom_call_target="tpu_custom_call" | custom-call | flops 4404019200 | bytes 8000000 | tf_op jit(solution)/shard_map/pallas_call | solution.py:287
  74.3 5.4 %all-to-all-start.2 = ((f32[16,8,128]{2,1,0:T(8,128)}), f32[16,8,128]{2,1,0:T(8,128)S(1)}, u32[]{:S(2)}, u32[]{:S(2)}) async-start(f32[16,8,128]{2,1,0:T(8,128)} %bitcast.18), calls=%async_computation.2 | async-start | bytes 131072 | tf_op jit(solution)/shard_map/all_to_all | solution.py:293
  79.8 7.7 %all-to-all-done.2 = f32[16,8,128]{2,1,0:T(8,128)S(1)} async-done(((f32[16,8,128]{2,1,0:T(8,128)}), f32[16,8,128]{2,1,0:T(8,128)S(1)}, u32[]{:S(2)}, u32[]{:S(2)}) %all-to-all-start.2) | async-done | bytes 65568 | tf_op jit(solution)/shard_map/all_to_all | solution.py:293
  87.4 0.7 shard_map.61
  88.8 0.0 copy-done
  88.8 0.0 copy-done.2
  88.8 0.0 copy-done.3
  88.8 0.0 copy-done.4
  88.8 0.0 copy-start.5
  88.9 0.6 copy-done.5
  (5 shorter events, 0.1 us)
Async XLA Ops:
  3.2 2.2 %collective-permute-start.2 = (bf16[416,768]{1,0:T(8,128)(2,1)S(1)}, bf16[416,768]{1,0:T(8,128)(2,1)S(1)}, u32[]{:S(2)}, u32[]{:S(2)}) collective-permute-start(bf16[416,768]{1,0:T(8,128)(2,1)S(1)} %get-tuple-element.95), channel_id=1, source_target_pairs={{0,16},{16,0},{1,17},{17,1},{2,18},{18,2},{3,19},{19,3},{4,20},{20... | collective-permute-start | bytes 1916936 | tf_op jit(solution)/shard_map/ppermute | solution.py:267
  5.4 10.9 %collective-permute-start.3 = (bf16[208,768]{1,0:T(8,128)(2,1)S(1)}, bf16[208,768]{1,0:T(8,128)(2,1)S(1)}, u32[]{:S(2)}, u32[]{:S(2)}) collective-permute-start(bf16[208,768]{1,0:T(8,128)(2,1)S(1)} %bitcast.60), channel_id=1, source_target_pairs={{0,32},{32,64},{64,96},{96,0},{1,33},{33,65},{65,97},{97,1},{2,34}... | collective-permute-start | bytes 958472 | tf_op jit(solution)/shard_map/ppermute | solution.py:252
  7.1 17.1 %collective-permute-start.4 = (bf16[208,768]{1,0:T(8,128)(2,1)S(1)}, bf16[208,768]{1,0:T(8,128)(2,1)S(1)}, u32[]{:S(2)}, u32[]{:S(2)}) collective-permute-start(bf16[208,768]{1,0:T(8,128)(2,1)S(1)} %bitcast.59), channel_id=1, source_target_pairs={{0,64},{32,96},{64,0},{96,32},{1,65},{33,97},{65,1},{97,33},{2,66}... | collective-permute-start | bytes 958472 | tf_op jit(solution)/shard_map/ppermute | solution.py:252
  9.8 14.4 %collective-permute-start.5 = (bf16[208,768]{1,0:T(8,128)(2,1)S(1)}, bf16[208,768]{1,0:T(8,128)(2,1)S(1)}, u32[]{:S(2)}, u32[]{:S(2)}) collective-permute-start(bf16[208,768]{1,0:T(8,128)(2,1)S(1)} %bitcast.58), channel_id=1, source_target_pairs={{0,96},{32,0},{64,32},{96,64},{1,97},{33,1},{65,33},{97,65},{2,98}... | collective-permute-start | bytes 958472 | tf_op jit(solution)/shard_map/ppermute | solution.py:252
  25.8 24.3 %collective-permute-start.6 = (bf16[640,768]{1,0:T(8,128)(2,1)S(1)}, bf16[640,768]{1,0:T(8,128)(2,1)S(1)}, u32[]{:S(2)}, u32[]{:S(2)}) collective-permute-start(bf16[640,768]{1,0:T(8,128)(2,1)S(1)} %shard_map.58.own), channel_id=1, source_target_pairs={{0,1},{1,2},{2,3},{3,0},{4,5},{5,6},{6,7},{7,4},{8,9},{9,10},{10,1... | collective-permute-start | bytes 2949128 | tf_op jit(solution)/shard_map/ppermute | solution.py:252
  27.4 23.1 %collective-permute-start.7 = (bf16[640,768]{1,0:T(8,128)(2,1)S(1)}, bf16[640,768]{1,0:T(8,128)(2,1)S(1)}, u32[]{:S(2)}, u32[]{:S(2)}) collective-permute-start(bf16[640,768]{1,0:T(8,128)(2,1)S(1)} %shard_map.58.own), channel_id=1, source_target_pairs={{0,3},{1,0},{2,1},{3,2},{4,7},{5,4},{6,5},{7,6},{8,11},{9,8},{10,9... | collective-permute-start | bytes 2949128 | tf_op jit(solution)/shard_map/ppermute | solution.py:252
  29.1 24.8 %collective-permute-start.10 = (bf16[640,768]{1,0:T(8,128)(2,1)S(1)}, bf16[640,768]{1,0:T(8,128)(2,1)S(1)}, u32[]{:S(2)}, u32[]{:S(2)}) collective-permute-start(bf16[640,768]{1,0:T(8,128)(2,1)S(1)} %shard_map.58.own), channel_id=1, source_target_pairs={{0,4},{4,8},{8,12},{12,0},{1,5},{5,9},{9,13},{13,1},{2,6},{6,10},{... | collective-permute-start | bytes 2949128 | tf_op jit(solution)/shard_map/ppermute | solution.py:252
  31.0 24.6 %collective-permute-start.11 = (bf16[640,768]{1,0:T(8,128)(2,1)S(1)}, bf16[640,768]{1,0:T(8,128)(2,1)S(1)}, u32[]{:S(2)}, u32[]{:S(2)}) collective-permute-start(bf16[640,768]{1,0:T(8,128)(2,1)S(1)} %shard_map.58.own), channel_id=1, source_target_pairs={{0,12},{4,0},{8,4},{12,8},{1,13},{5,1},{9,5},{13,9},{2,14},{6,2},{... | collective-permute-start | bytes 2949128 | tf_op jit(solution)/shard_map/ppermute | solution.py:252
  50.1 15.0 %collective-permute-start.8 = (bf16[320,768]{1,0:T(8,128)(2,1)S(1)}, bf16[320,768]{1,0:T(8,128)(2,1)S(1)}, u32[]{:S(2)}, u32[]{:S(2)}) collective-permute-start(bf16[320,768]{1,0:T(8,128)(2,1)S(1)} %slice.42), channel_id=1, source_target_pairs={{0,1},{1,2},{2,3},{3,0},{4,5},{5,6},{6,7},{7,4},{8,9},{9,10},{10,1... | collective-permute-start | bytes 1474568 | tf_op jit(solution)/shard_map/ppermute | solution.py:252
  50.5 14.6 %collective-permute-start.9 = (bf16[320,768]{1,0:T(8,128)(2,1)S(1)}, bf16[320,768]{1,0:T(8,128)(2,1)S(1)}, u32[]{:S(2)}, u32[]{:S(2)}) collective-permute-start(bf16[320,768]{1,0:T(8,128)(2,1)S(1)} %slice.43), channel_id=1, source_target_pairs={{0,3},{1,0},{2,1},{3,2},{4,7},{5,4},{6,5},{7,6},{8,11},{9,8},{10,9... | collective-permute-start | bytes 1474568 | tf_op jit(solution)/shard_map/ppermute | solution.py:252
  53.9 13.0 %collective-permute-start.12 = (bf16[320,768]{1,0:T(8,128)(2,1)S(1)}, bf16[320,768]{1,0:T(8,128)(2,1)S(1)}, u32[]{:S(2)}, u32[]{:S(2)}) collective-permute-start(bf16[320,768]{1,0:T(8,128)(2,1)S(1)} %slice.44), channel_id=1, source_target_pairs={{0,4},{4,8},{8,12},{12,0},{1,5},{5,9},{9,13},{13,1},{2,6},{6,10},{... | collective-permute-start | bytes 1474568 | tf_op jit(solution)/shard_map/ppermute | solution.py:252
  55.6 11.4 %collective-permute-start.13 = (bf16[320,768]{1,0:T(8,128)(2,1)S(1)}, bf16[320,768]{1,0:T(8,128)(2,1)S(1)}, u32[]{:S(2)}, u32[]{:S(2)}) collective-permute-start(bf16[320,768]{1,0:T(8,128)(2,1)S(1)} %slice.45), channel_id=1, source_target_pairs={{0,12},{4,0},{8,4},{12,8},{1,13},{5,1},{9,5},{13,9},{2,14},{6,2},{... | collective-permute-start | bytes 1474568 | tf_op jit(solution)/shard_map/ppermute | solution.py:252
  65.1 23.7 %copy-start = (bf16[512,768]{1,0:T(8,128)(2,1)S(1)}, bf16[512,768]{1,0:T(8,128)(2,1)}, u32[]{:S(2)}) copy-start(bf16[512,768]{1,0:T(8,128)(2,1)} %emb_ref.1) | copy-start | bytes 2359300
  65.1 23.7 %copy-start.2 = (s32[512]{0:T(512)S(1)}, s32[512]{0:T(512)}, u32[]{:S(2)}) copy-start(s32[512]{0:T(512)} %param.15) | copy-start | bytes 6148
  65.1 23.7 %copy-start.3 = (s32[512]{0:T(512)S(1)}, s32[512]{0:T(512)}, u32[]{:S(2)}) copy-start(s32[512]{0:T(512)} %param.12) | copy-start | bytes 6148
  65.1 23.7 %copy-start.4 = (s32[8]{0:T(128)S(1)}, s32[8]{0:T(128)}, u32[]{:S(2)}) copy-start(s32[8]{0:T(128)} %assign_ref.1) | copy-start | bytes 100
  74.3 13.1 %all-to-all-start.2 = ((f32[16,8,128]{2,1,0:T(8,128)}), f32[16,8,128]{2,1,0:T(8,128)S(1)}, u32[]{:S(2)}, u32[]{:S(2)}) async-start(f32[16,8,128]{2,1,0:T(8,128)} %bitcast.18), calls=%async_computation.2 | async-start | bytes 131072 | tf_op jit(solution)/shard_map/all_to_all | solution.py:293
  88.8 0.6 copy-start.5

commit v4 on v3

--- a/solution.py
+++ b/solution.py
@@ -57,12 +57,13 @@
     wide = emb_ref[...].astype(F32)
     mean = jnp.mean(wide * wide, axis=1, keepdims=True)
     unit = (wide * lax.rsqrt(mean + 1e-06) * (1.0 / math.sqrt(WIDTH))).astype(BF16)
-    my_x, my_core = lax.axis_index("x"), lax.axis_index("core")
+    my_x, my_core, my_y = lax.axis_index("x"), lax.axis_index("core"), lax.axis_index("y")
     cid = cid_ref[...]
     group = jnp.zeros_like(cid)
     for c in range(KINDS):
-        away = lax.rem(assign_ref[c] // 2 - my_x + 4, 4)
-        away += 4 * lax.rem(assign_ref[c] + my_core, 2)
+        core = lax.rem(assign_ref[c], 2)
+        away = lax.rem(assign_ref[c] // 2 - jnp.where(core == 0, my_x, my_y) + 4, 4)
+        away += 4 * lax.rem(core + my_core, 2)
         group = jnp.where(cid == c, away, group)
     group = group.astype(F32)
     place = place_ref[...].astype(F32)
@@ -100,11 +101,12 @@
         ref[...] = mul(placing, both).astype(BF16)
 
 
-def pack_kernel(here_ref, from1_ref, from2_ref, from3_ref, out_ref, in_ref):
+def pack_kernel(here_ref, from1_ref, from2_ref, from3_ref, out_ref, over_ref, in_ref):
     count = KINDS * BLOCK
     for k, ref in enumerate((here_ref, from1_ref, from2_ref, from3_ref)):
         in_ref[k * 2 * BLOCK : (k + 1) * 2 * BLOCK, :] = ref[...]
-    my_x, my_core = lax.axis_index("x"), lax.axis_index("core")
+    my_core = lax.axis_index("core")
+    my_line = jnp.where(my_core == 0, lax.axis_index("x"), lax.axis_index("y"))
     at = iota((32, count), 0)
     pick = hot(iota((32, count), 1) == (at % 8) * BLOCK + SEND + at // 8)
     numbers = mul(pick, in_ref[:, 0:128])
@@ -120,7 +122,7 @@
         mine = n[b : b + 1, :]
         position = jnp.where((step >= 0.0) & (step < mine), start + step, position)
         base = jnp.where(line == b, start, base)
-        from_device = 2 * lax.rem(my_x - b // 2 + 4, 4) + lax.rem(my_core + b % 2, 2)
+        from_device = 2 * lax.rem(my_line - b // 2 + 4, 4) + lax.rem(my_core + b % 2, 2)
         source = jnp.where(line == b, from_device.astype(F32), source)
         start = start + mine
     position = jnp.where(position < HELD, position, -1.0)
@@ -136,7 +138,9 @@
     source = jnp.sum(mine * source, axis=0, keepdims=True)
     counts = numbers[24:32, :]
     over = jnp.max(jnp.where(counts > SEND, 1.0, 0.0), axis=0, keepdims=True)
-    over = jnp.maximum(over, jnp.where(jnp.sum(counts, axis=0, keepdims=True) > HELD, 1.0, 0.0))
+    ours = iota((1, 128), 1) % 2 == my_core
+    full = ours & (jnp.sum(counts, axis=0, keepdims=True) > HELD)
+    over = jnp.maximum(over, jnp.where(full, 1.0, 0.0))
     over = jnp.max(over, axis=1, keepdims=True)
     valid = (code > 0.0) & (iota((1, PACKED), 1) < HELD)
     final = rows_of(
@@ -144,8 +148,8 @@
         jnp.where(valid, low, 0.0),
         jnp.where(valid, code, 0.0),
         jnp.where(valid, source, 0.0),
-        jnp.broadcast_to(over, (1, PACKED)),
     )
+    over_ref[...] = jnp.broadcast_to(over, (8, 128))
     final = jnp.concatenate([final, jnp.zeros((8, WIDTH - PACKED), F32)], axis=1)
     final = jnp.concatenate([final, jnp.zeros((8, WIDTH), F32)], axis=0)
     out_ref[HELD:PACKED, :] = final.astype(BF16)
@@ -167,58 +171,78 @@
     return jnp.maximum(best, jnp.max(scores.reshape(count // 8, 8, n), axis=0))
 
 
-def near_kernel(own, y1, y3, z1, z3, best_ref, order_ref):
-    cols = (own, z1, z3)
-    order_ref[...] = jnp.transpose(rows_of(*[orders_of(numbers_of(c)) for c in cols]))
-    for i, rows in enumerate((own, y1, y3)):
-        order = orders_of(numbers_of(rows))
-        best = jnp.full((8, PACKED), -2.0, F32)
-        for k, col in enumerate(cols):
-            best = earlier_max(best, rows, order, col, order_ref[:, k : k + 1])
-        best_ref[:, i * PACKED : (i + 1) * PACKED] = best
-
-
-def far_kernel(own, y1, y3, y2a, y2b, z1, z3, z2a, z2b, near_ref, out_ref, y2, order_ref, sent):
+def orders_down(*refs):
+    return jnp.transpose(rows_of(*[orders_of(numbers_of(r)) for r in refs]))
+
+
+def all_earlier(best, rows, cols, orders, first):
+    order = orders_of(numbers_of(rows))
+    for k, col in enumerate(cols):
+        best = earlier_max(best, rows, order, col, orders[:, first + k : first + k + 1])
+    return best
+
+
+def nothing():
+    return jnp.full((8, PACKED), -2.0, F32)
+
+
+def near_kernel(own, m1, m3, z1, best_ref, order_ref):
+    order_ref[...] = orders_down(z1, own, m1, m3)
+    for i, rows in enumerate((own, m1, m3)):
+        best_ref[i] = all_earlier(nothing(), rows, (z1, own), order_ref, 0)
+    best_ref[3] = all_earlier(nothing(), z1, (own, m1, m3), order_ref, 1)
+
+
+def middle_kernel(own, z1, m2a, m2b, near_ref, m2, best_ref, order_ref):
     half = PACKED // 2
-    y2[0:half, :] = y2a[...]
-    y2[half:PACKED, :] = y2b[...]
-    order_ref[...] = jnp.transpose(rows_of(*[orders_of(numbers_of(c)) for c in (own, z1, z3, z2b)]))
-    over = jnp.zeros((1, 128), F32)
-    for ref in (own, y1, y3, y2b, z1, z3, z2b):
-        over = jnp.maximum(over, numbers_of(ref)[4:5, 0:128])
+    m2[0:half, :] = m2a[...]
+    m2[half:PACKED, :] = m2b[...]
+    order_ref[...] = orders_down(z1, own, m2)
+    best_ref[0] = all_earlier(nothing(), m2, (z1, own), order_ref, 0)
+    best_ref[1] = all_earlier(near_ref[3], z1, (m2,), order_ref, 2)
+
+
+def to_owners(best, numbers):
+    best = jnp.maximum(jnp.max(best, axis=0, keepdims=True), -1.0)
+    high = best.astype(BF16).astype(F32)
+    low = best - high
+    middle = low.astype(BF16).astype(F32)
+    low = low - middle
+    lines = jnp.where((iota_f((KINDS, PACKED), 0) == numbers[3:4, :]) & (numbers[2:3, :] > 0.0), 1.0, 0.0)
+    pieces = jnp.concatenate([lines, lines * high, lines * middle, lines * low], axis=0)
+    code = jnp.transpose(rows_of(numbers[2:3, :]))[:, 0:1]
+    put = mul(pieces.astype(BF16), hot(iota_f((PACKED, 128), 1) == code - 1.0))
+    return (put[0:8, :] - 1.0) + (put[8:16, :] + put[16:24, :] + put[24:32, :])
+
+
+OVER = 5 * KINDS
+
+
+def far_kernel(own, m1, m3, m2, z1, z2, near_ref, middle_ref, over_ref, other_over_ref, out_ref, order_ref, sent):
+    order_ref[...] = orders_down(z2)
     sent[...] = jnp.zeros((128, 128), F32)
-    sent[4 * KINDS : 4 * KINDS + 8, :] = jnp.broadcast_to(over, (8, 128))
-    for q, rows in enumerate((own, y1, y3, y2)):
-        numbers = numbers_of(rows)
-        order = orders_of(numbers)
-        if q < 3:
-            best = near_ref[:, q * PACKED : (q + 1) * PACKED]
-        else:
-            best = jnp.full((8, PACKED), -2.0, F32)
-            for k, col in enumerate((own, z1, z3)):
-                best = earlier_max(best, rows, order, col, order_ref[:, k : k + 1])
-        best = earlier_max(best, rows, order, z2a, order_ref[0:half, 3:4])
-        best = earlier_max(best, rows, order, z2b, order_ref[half:PACKED, 3:4])
-        best = jnp.maximum(jnp.max(best, axis=0, keepdims=True), -1.0)
-        high = best.astype(BF16).astype(F32)
-        low = best - high
-        middle = low.astype(BF16).astype(F32)
-        low = low - middle
-        lines = jnp.where(
-            (iota_f((KINDS, PACKED), 0) == numbers[3:4, :]) & (numbers[2:3, :] > 0.0), 1.0, 0.0
-        )
-        pieces = jnp.concatenate([lines, lines * high, lines * middle, lines * low], axis=0)
-        code = jnp.transpose(rows_of(numbers[2:3, :]))[:, 0:1]
-        put = mul(pieces.astype(BF16), hot(iota_f((PACKED, 128), 1) == code - 1.0))
-        sent[q * KINDS : (q + 1) * KINDS, :] = (
-            (put[0:8, :] - 1.0) + (put[8:16, :] + put[16:24, :] + put[24:32, :])
-        )
-    out_ref[...] = jnp.transpose(sent[...])
-
-
-def final_kernel(in_ref, out_ref, over_ref):
-    got = jnp.transpose(in_ref[...])
-    over_ref[0, 0] = (jnp.max(got[4 * KINDS : 4 * KINDS + 1, :]) > 0.5).astype(I32)
+    over = jnp.maximum(over_ref[...], other_over_ref[...])
+    sent[OVER : OVER + 8, :] = over
+    sent[4 * KINDS : 5 * KINDS, :] = to_owners(middle_ref[1], numbers_of(z1))
+    for q, (rows, best) in enumerate(((own, near_ref[0]), (m1, near_ref[1]), (m3, near_ref[2]), (m2, middle_ref[0]))):
+        best = all_earlier(best, rows, (z2,), order_ref, 0)
+        sent[q * KINDS : (q + 1) * KINDS, :] = to_owners(best, numbers_of(rows))
+    out_ref[...] = jnp.broadcast_to(over[0:1, :], (512, 128))
+    to_x = jnp.where(lax.axis_index("core") == 0, lax.axis_index("x"), lax.axis_index("y"))
+    out_ref[pl.ds(pl.multiple_of(to_x * 128, 128), 128), :] = jnp.transpose(sent[...])
+
+
+def final_kernel(in_ref, out_ref, over_ref, picked):
+    my_x, my_core = lax.axis_index("x"), lax.axis_index("core")
+    over = jnp.where(iota((512, 128), 1) == OVER, in_ref[...], 0.0)
+    over_ref[0, 0] = (jnp.max(over) > 0.5).astype(I32)
+    first = jnp.where(my_core == 0, my_x * 128, my_x * 8)
+    step = jnp.where(my_core == 0, 8, 128)
+    for z in range(4):
+        for r in range(4):
+            at = pl.multiple_of(first + z * 32 + r * step, 8)
+            picked[(z * 4 + r) * 8 : (z * 4 + r) * 8 + 8, :] = in_ref[pl.ds(at, 8), :]
+    got = jnp.transpose(picked[...])
     lane = iota((KINDS, 128), 1) % 32
     best = got[0:KINDS, :]
     for q, away in ((1, 3), (2, 1), (3, 2)):
@@ -229,7 +253,14 @@
             pltpu.roll(part, 128 + 8 * away - 32, 1),
         )
         best = jnp.maximum(best, moved)
-    out_ref[...] = best
+    part = got[4 * KINDS : 5 * KINDS, :]
+    best = jnp.maximum(best, jnp.where(my_core == 0, pltpu.roll(part, 32, 1), pltpu.roll(part, 96, 1)))
+    shift = lane // 8 - iota((KINDS, 128), 0) // 2
+    turned = best
+    for d in (-3, -2, -1, 1, 2, 3):
+        moved = pltpu.roll(pltpu.roll(best, (8 - 2 * d) % 8, 0), (8 * d) % 128, 1)
+        turned = jnp.where(shift == d, moved, turned)
+    out_ref[...] = jnp.where(my_core == 0, best, turned)
 
 
 def call(kernel, out, scratch=(), ins=None, outs=None, cost=None):
@@ -248,8 +279,26 @@
     )
 
 
-def ring(x, axis, step):
-    return lax.ppermute(x, axis, [(i, (i + step) % 4) for i in range(4)])
+def move(a, to):
+    at = lambda x, c, z, y: ((x % 4 * 2 + c) * 4 + z % 4) * 4 + y % 4
+    places = [(x, c, z, y) for x in range(4) for c in range(2) for z in range(4) for y in range(4)]
+    return lax.ppermute(a, AXES, [(at(*p), at(*to(*p))) for p in places])
+
+
+def across(a, step):
+    return move(a, lambda x, c, z, y: (x + (1 - c) * step, c, z, y + c * step))
+
+
+def along(a, step):
+    return move(a, lambda x, c, z, y: (x + c * step, c, z, y + (1 - c) * step))
+
+
+def down(a):
+    return move(a, lambda x, c, z, y: (x, c, z - 1 + 2 * c, y))
+
+
+def core_swap(a):
+    return lax.ppermute(a, "core", [(0, 1), (1, 0)])
 
 
 def fast(embeddings, cluster_id, row_order, assignment, placement):
@@ -264,36 +313,40 @@
         ins=[smem] + [vmem] * 4,
         cost=cheap,
     )(assignment, embeddings, line(cluster_id), line(row_order), line(placement))
-    other = lax.ppermute(other, "core", [(0, 1), (1, 0)])
+    other = core_swap(other)
     shape = (4, 1, BLOCK, WIDTH)
     both = jnp.concatenate([same.reshape(shape), other.reshape(shape)], axis=1).reshape(4, 2 * BLOCK, WIDTH)
-    own = call(
+    own, over = call(
         pack_kernel,
-        jax.ShapeDtypeStruct((PACKED, WIDTH), BF16),
+        (jax.ShapeDtypeStruct((PACKED, WIDTH), BF16), jax.ShapeDtypeStruct((8, 128), F32)),
         [pltpu.VMEM((KINDS * BLOCK, WIDTH), BF16)],
         cost=cheap,
-    )(both[0], *[ring(both[k], "x", k) for k in (1, 2, 3)])
+    )(both[0], *[across(both[k], k) for k in (1, 2, 3)])
     half = PACKED // 2
-    y1, y3, z1, z3 = ring(own, "y", 1), ring(own, "y", -1), ring(own, "z", 1), ring(own, "z", -1)
-    y2a, y2b = ring(y1[:half], "y", 1), ring(y3[half:], "y", -1)
-    z2a, z2b = ring(z1[:half], "z", 1), ring(z3[half:], "z", -1)
-    pair = 2 * PACKED * PACKED * WIDTH
-    near = call(
-        near_kernel,
-        jax.ShapeDtypeStruct((8, 3 * PACKED), F32),
-        [pltpu.VMEM((PACKED, 8), F32)],
-        cost=pl.CostEstimate(flops=9 * pair, bytes_accessed=6 * 10**6, transcendentals=0),
-    )(own, y1, y3, z1, z3)
+    z1, m1, m3 = down(own), along(own, 1), along(own, -1)
+    other_over = core_swap(over)
+    z2, m2a, m2b = down(z1), along(m1[:half], 1), along(m3[half:], -1)
+    product = 2 * PACKED * PACKED * WIDTH
+    cost = lambda n: pl.CostEstimate(flops=n * product, bytes_accessed=6 * 10**6, transcendentals=0)
+    order = pltpu.VMEM((PACKED, 8), F32)
+    near = call(near_kernel, jax.ShapeDtypeStruct((4, 8, PACKED), F32), [order], cost=cost(9))(own, m1, m3, z1)
+    m2, middle = call(
+        middle_kernel,
+        (jax.ShapeDtypeStruct((PACKED, WIDTH), BF16), jax.ShapeDtypeStruct((2, 8, PACKED), F32)),
+        [order],
+        cost=cost(3),
+    )(own, z1, m2a, m2b, near)
     back = call(
         far_kernel,
-        jax.ShapeDtypeStruct((128, 128), F32),
-        [pltpu.VMEM((PACKED, WIDTH), BF16), pltpu.VMEM((PACKED, 8), F32), pltpu.VMEM((128, 128), F32)],
-        cost=pl.CostEstimate(flops=7 * pair, bytes_accessed=8 * 10**6, transcendentals=0),
-    )(own, y1, y3, y2a, y2b, z1, z3, z2a, z2b, near)
-    back = lax.all_to_all(back, ("z", "y"), split_axis=0, concat_axis=0, tiled=True)
+        jax.ShapeDtypeStruct((512, 128), F32),
+        [order, pltpu.VMEM((128, 128), F32)],
+        cost=cost(4),
+    )(own, m1, m3, m2, z1, z2, near, middle, over, other_over)
+    back = lax.all_to_all(back, ("x", "z", "y"), split_axis=0, concat_axis=0, tiled=True)
     best, over = call(
         final_kernel,
         (jax.ShapeDtypeStruct((KINDS, 128), F32), jax.ShapeDtypeStruct((1, 1), I32)),
+        [pltpu.VMEM((128, 128), F32)],
         ins=[vmem],
         outs=(vmem, smem),
     )(back)

time: 90.5 us -> 80.6 us (0.89)
  waiting for transfers between devices: 41.8 us -> 31 us
  Pallas kernels: 19.9 us -> 21.2 us
    ppermute x12 -> x11, waiting for transfers between devices: 34.2 us -> 20.5 us  [the longest x9 18.5 us: move(): return lax.ppermute(a, AXES, [(at(*p), at(*to(*p))) for p in places])]
    all_to_all x1, waiting for transfers between devices: 7.67 us -> 10.4 us  [fast(): lax.all_to_all(back, ('x', 'z', 'y'), split_axis=0, concat_axis=0, tiled=...]
    pallas_call x3 -> x4, Pallas kernels: 16.1 us -> 17.3 us  [the longest x1 7.1 us: fast(): call(near_kernel, jax.ShapeDtypeStruct((4, 8, PACKED), F32), [order], cos...]
    all_to_all x1, starting transfers between devices: 5.42 us -> 6.54 us  [fast(): lax.all_to_all(back, ('x', 'z', 'y'), split_axis=0, concat_axis=0, tiled=...]
    ppermute x12 -> x11, starting transfers between devices: 20.6 us -> 20 us  [the longest x9 20 us: move(): return lax.ppermute(a, AXES, [(at(*p), at(*to(*p))) for p in places])]
  transfers between devices with their start and end apart: 13 -> 12, of which waited for: 7 -> 6; matrix products, arithmetic and copies ran while one was open for 0% -> 0% of each run, Pallas kernels for 8% -> 12%
where the time goes in v4:
time: 80.6 us; the launch traced here: 80.4 us
  waiting for transfers between devices  31 us (38%)
  starting transfers between devices  26.6 us (33%)
  Pallas kernels  21.2 us (26%)
  between operations  0.84 us (1%)
    ppermute x9, starting transfers between devices, move(): return lax.ppermute(a, AXES, [(at(*p), at(*to(*p))) for p in places])  20 us
    ppermute x9, waiting for transfers between devices, move(): return lax.ppermute(a, AXES, [(at(*p), at(*to(*p))) for p in places])  18.5 us
    all_to_all x1, waiting for transfers between devices, fast(): lax.all_to_all(back, ('x', 'z', 'y'), split_axis=0, concat_axis=0, tiled=...  10.4 us
    pallas_call x1, Pallas kernels, fast(): call(near_kernel, jax.ShapeDtypeStruct((4, 8, PACKED), F32), [order], cos...  7.1 us
    all_to_all x1, starting transfers between devices, fast(): lax.all_to_all(back, ('x', 'z', 'y'), split_axis=0, concat_axis=0, tiled=...  6.54 us
    pallas_call x1, Pallas kernels, fast(): call(far_kernel, jax.ShapeDtypeStruct((512, 128), F32), [order, pltpu.VME...  6.13 us
    pallas_call x1, Pallas kernels, fast(): call(prep_kernel, (blocks, blocks), ins=[smem] + [vmem] * 4, cost=cheap)  3.16 us
    pallas_call x1, Pallas kernels, fast(): call(middle_kernel, (jax.ShapeDtypeStruct((PACKED, WIDTH), BF16), jax.Sha...  2.54 us
  transfers between devices with their start and end apart: 12, of which 6 were waited for; matrix products, arithmetic and copies ran while one was open for 0% of the time, Pallas kernels for 12%

profile of v4, /device:TPU:0, one launch (start us, length us, event | category | flops | bytes accessed | tf_op | source)
XLA Modules:
  0.0 80.4 jit_solution(455299269851598507)
XLA Ops:
  0.0 3.2 %shard_map.57 = (bf16[416,768]{1,0:T(8,128)(2,1)S(1)}, bf16[416,768]{1,0:T(8,128)(2,1)S(1)}) custom-call(s32[8]{0:T(128)} %assign_ref.1, bf16[512,768]{1,0:T(8,128)(2,1)} %emb_ref.1, s32[1,512]{1,0:T(1,128)} %bitcast.63, s32[1,512]{1,0:T(1,128)} %bitcast.65, s32[1,512]{1,0:T(1,128)} %bitcast.62), custom_call_target="tpu_custom_call" | custom-call | flops 1000000000 | bytes 2000000 | tf_op jit(solution)/shard_map/pallas_call | solution.py:310
  3.2 0.1 collective-permute-start.2
  3.3 2.1 %collective-permute-done.2 = bf16[416,768]{1,0:T(8,128)(2,1)S(1)} collective-permute-done((bf16[416,768]{1,0:T(8,128)(2,1)S(1)}, bf16[416,768]{1,0:T(8,128)(2,1)S(1)}, u32[]{:S(2)}, u32[]{:S(2)}) %collective-permute-start.2) | collective-permute-done | bytes 639008 | tf_op jit(solution)/shard_map/ppermute | solution.py:301
  5.3 0.1 pad_maximum_fusion
  5.4 1.6 %collective-permute-start.3 = (bf16[208,768]{1,0:T(8,128)(2,1)S(1)}, bf16[208,768]{1,0:T(8,128)(2,1)S(1)}, u32[]{:S(2)}, u32[]{:S(2)}) collective-permute-start(bf16[208,768]{1,0:T(8,128)(2,1)S(1)} %bitcast.60), channel_id=1, source_target_pairs={{0,32},{1,33},{2,34},{3,35},{4,36},{5,37},{6,38},{7,39},{8,40},{9,... | collective-permute-start | bytes 958472 | tf_op jit(solution)/shard_map/ppermute | solution.py:285
  7.1 2.7 %collective-permute-start.4 = (bf16[208,768]{1,0:T(8,128)(2,1)S(1)}, bf16[208,768]{1,0:T(8,128)(2,1)S(1)}, u32[]{:S(2)}, u32[]{:S(2)}) collective-permute-start(bf16[208,768]{1,0:T(8,128)(2,1)S(1)} %bitcast.59), channel_id=1, source_target_pairs={{0,64},{1,65},{2,66},{3,67},{4,68},{5,69},{6,70},{7,71},{8,72},{9,... | collective-permute-start | bytes 958472 | tf_op jit(solution)/shard_map/ppermute | solution.py:285
  9.8 1.4 %collective-permute-start.5 = (bf16[208,768]{1,0:T(8,128)(2,1)S(1)}, bf16[208,768]{1,0:T(8,128)(2,1)S(1)}, u32[]{:S(2)}, u32[]{:S(2)}) collective-permute-start(bf16[208,768]{1,0:T(8,128)(2,1)S(1)} %bitcast.58), channel_id=1, source_target_pairs={{0,96},{1,97},{2,98},{3,99},{4,100},{5,101},{6,102},{7,103},{8,104... | collective-permute-start | bytes 958472 | tf_op jit(solution)/shard_map/ppermute | solution.py:285
  11.2 2.5 %collective-permute-done.3.from1_ref = bf16[208,768]{1,0:T(8,128)(2,1)S(1)} collective-permute-done((bf16[208,768]{1,0:T(8,128)(2,1)S(1)}, bf16[208,768]{1,0:T(8,128)(2,1)S(1)}, u32[]{:S(2)}, u32[]{:S(2)}) %collective-permute-start.3) | collective-permute-done | bytes 319520 | tf_op jit(solution)/shard_map/ppermute | solution.py:285
  13.7 4.5 %collective-permute-done.4.from2_ref = bf16[208,768]{1,0:T(8,128)(2,1)S(1)} collective-permute-done((bf16[208,768]{1,0:T(8,128)(2,1)S(1)}, bf16[208,768]{1,0:T(8,128)(2,1)S(1)}, u32[]{:S(2)}, u32[]{:S(2)}) %collective-permute-start.4) | collective-permute-done | bytes 319520 | tf_op jit(solution)/shard_map/ppermute | solution.py:285
  18.2 0.0 collective-permute-done.5.from3_ref
  18.2 1.6 %shard_map.58 = (bf16[640,768]{1,0:T(8,128)(2,1)S(1)}, f32[8,128]{1,0:T(8,128)S(1)}) custom-call(bf16[208,768]{1,0:T(8,128)(2,1)S(1)} %bitcast.49, bf16[208,768]{1,0:T(8,128)(2,1)S(1)} %collective-permute-done.3.from1_ref, bf16[208,768]{1,0:T(8,128)(2,1)S(1)} %collective-permute-done.4.from2_ref, bf16[208,768]{1,0:T(8,128)(2,1)S(1)} %collective-permute-done.5.from3_ref), custom_call_target="tpu_custom_call" | custom-call | flops 1000000000 | bytes 2000000 | tf_op jit(solution)/shard_map/pallas_call | solution.py:319
  19.8 4.1 %collective-permute-start.8 = (bf16[640,768]{1,0:T(8,128)(2,1)S(1)}, bf16[640,768]{1,0:T(8,128)(2,1)S(1)}, u32[]{:S(2)}, u32[]{:S(2)}) collective-permute-start(bf16[640,768]{1,0:T(8,128)(2,1)S(1)} %get-tuple-element.100.own), channel_id=1, source_target_pairs={{0,12},{1,13},{2,14},{3,15},{4,0},{5,1},{6,2},{7,3},{8,4},{9,5},{1... | collective-permute-start | bytes 2949128 | tf_op jit(solution)/shard_map/ppermute | solution.py:285
  23.9 3.0 %collective-permute-start.7 = (bf16[640,768]{1,0:T(8,128)(2,1)S(1)}, bf16[640,768]{1,0:T(8,128)(2,1)S(1)}, u32[]{:S(2)}, u32[]{:S(2)}) collective-permute-start(bf16[640,768]{1,0:T(8,128)(2,1)S(1)} %get-tuple-element.100.own), channel_id=1, source_target_pairs={{0,3},{1,0},{2,1},{3,2},{4,7},{5,4},{6,5},{7,6},{8,11},{9,8},{10,9... | collective-permute-start | bytes 2949128 | tf_op jit(solution)/shard_map/ppermute | solution.py:285
  26.9 0.0 collective-permute-start.6
  26.9 8.6 %collective-permute-done.8.z1 = bf16[640,768]{1,0:T(8,128)(2,1)S(1)} collective-permute-done((bf16[640,768]{1,0:T(8,128)(2,1)S(1)}, bf16[640,768]{1,0:T(8,128)(2,1)S(1)}, u32[]{:S(2)}, u32[]{:S(2)}) %collective-permute-start.8) | collective-permute-done | bytes 983072 | tf_op jit(solution)/shard_map/ppermute | solution.py:285
  35.5 3.7 %collective-permute-start.11 = (bf16[640,768]{1,0:T(8,128)(2,1)S(1)}, bf16[640,768]{1,0:T(8,128)(2,1)S(1)}, u32[]{:S(2)}, u32[]{:S(2)}) collective-permute-start(bf16[640,768]{1,0:T(8,128)(2,1)S(1)} %collective-permute-done.8.z1), channel_id=1, source_target_pairs={{0,12},{1,13},{2,14},{3,15},{4,0},{5,1},{6,2},{7,3},{8,4},{9,5},{1... | collective-permute-start | bytes 2949128 | tf_op jit(solution)/shard_map/ppermute | solution.py:285
  39.2 0.0 collective-permute-start.12
  39.2 0.0 collective-permute-done.7.m3
  39.2 3.1 %collective-permute-start.10 = (bf16[320,768]{1,0:T(8,128)(2,1)S(1)}, bf16[320,768]{1,0:T(8,128)(2,1)S(1)}, u32[]{:S(2)}, u32[]{:S(2)}) collective-permute-start(bf16[320,768]{1,0:T(8,128)(2,1)S(1)} %slice.35), channel_id=1, source_target_pairs={{0,3},{1,0},{2,1},{3,2},{4,7},{5,4},{6,5},{7,6},{8,11},{9,8},{10,9... | collective-permute-start | bytes 1474568 | tf_op jit(solution)/shard_map/ppermute | solution.py:285
  42.3 0.0 collective-permute-done.6.m1
  42.3 0.3 collective-permute-start.9
  42.6 7.1 %shard_map.59.near_ref = f32[4,8,640]{2,1,0:T(8,128)S(1)} custom-call(bf16[640,768]{1,0:T(8,128)(2,1)S(1)} %get-tuple-element.100.own, bf16[640,768]{1,0:T(8,128)(2,1)S(1)} %collective-permute-done.6.m1, bf16[640,768]{1,0:T(8,128)(2,1)S(1)} %collective-permute-done.7.m3, bf16[640,768]{1,0:T(8,128)(2,1)S(1)} %collective-permute-done.8.z1), custom_call_target="tpu_custom_call" | custom-call | flops 5662310400 | bytes 6000000 | tf_op jit(solution)/shard_map/pallas_call | solution.py:332
  49.7 0.0 collective-permute-done.10.m2b
  49.7 2.9 %collective-permute-done.9.m2a = bf16[320,768]{1,0:T(8,128)(2,1)S(1)} collective-permute-done((bf16[320,768]{1,0:T(8,128)(2,1)S(1)}, bf16[320,768]{1,0:T(8,128)(2,1)S(1)}, u32[]{:S(2)}, u32[]{:S(2)}) %collective-permute-start.9) | collective-permute-done | bytes 491552 | tf_op jit(solution)/shard_map/ppermute | solution.py:285
  52.6 2.5 %shard_map.60 = (bf16[640,768]{1,0:T(8,128)(2,1)S(1)}, f32[2,8,640]{2,1,0:T(8,128)S(1)}) custom-call(bf16[640,768]{1,0:T(8,128)(2,1)S(1)} %get-tuple-element.100.own, bf16[640,768]{1,0:T(8,128)(2,1)S(1)} %collective-permute-done.8.z1, bf16[320,768]{1,0:T(8,128)(2,1)S(1)} %collective-permute-done.9.m2a, bf16[320,768]{1,0:T(8,128)(2,1)S(1)} %collective-permute-done.10.m2b, ...), custom_call_target="tpu_custom_call" | custom-call | flops 1887436800 | bytes 6000000 | tf_op jit(solution)/shard_map/pallas_call | solution.py:333
  55.2 0.0 collective-permute-done.12.other_over_ref
  55.2 0.0 collective-permute-done.11.z2
  55.2 0.0 copy-start
  55.2 0.0 copy-start.2
  55.2 0.0 copy-start.3
  55.2 0.0 copy-start.4
  55.2 6.1 %shard_map.61 = f32[512,128]{1,0:T(8,128)} custom-call(bf16[640,768]{1,0:T(8,128)(2,1)S(1)} %get-tuple-element.100.own, bf16[640,768]{1,0:T(8,128)(2,1)S(1)} %collective-permute-done.6.m1, bf16[640,768]{1,0:T(8,128)(2,1)S(1)} %collective-permute-done.7.m3, bf16[640,768]{1,0:T(8,128)(2,1)S(1)} %get-tuple-element.101.m2, ...), custom_call_target="tpu_custom_call" | custom-call | flops 2516582400 | bytes 6000000 | tf_op jit(solution)/shard_map/pallas_call | solution.py:339
  61.4 6.5 %all-to-all-start.2 = ((f32[64,8,128]{2,1,0:T(8,128)}), f32[64,8,128]{2,1,0:T(8,128)S(1)}, u32[]{:S(2)}, u32[]{:S(2)}) async-start(f32[64,8,128]{2,1,0:T(8,128)} %bitcast.18), calls=%async_computation.2 | async-start | bytes 524288 | tf_op jit(solution)/shard_map/all_to_all | solution.py:345
  67.9 10.4 %all-to-all-done.2 = f32[64,8,128]{2,1,0:T(8,128)S(1)} async-done(((f32[64,8,128]{2,1,0:T(8,128)}), f32[64,8,128]{2,1,0:T(8,128)S(1)}, u32[]{:S(2)}, u32[]{:S(2)}) %all-to-all-start.2) | async-done | bytes 262176 | tf_op jit(solution)/shard_map/all_to_all | solution.py:345
  78.3 0.7 shard_map.62
  79.7 0.0 copy-done
  79.8 0.0 copy-done.2
  79.8 0.0 copy-done.3
  79.8 0.0 copy-done.4
  79.8 0.0 copy-start.5
  79.8 0.6 copy-done.5
  (3 shorter events, 0.1 us)
Async XLA Ops:
  3.2 2.2 %collective-permute-start.2 = (bf16[416,768]{1,0:T(8,128)(2,1)S(1)}, bf16[416,768]{1,0:T(8,128)(2,1)S(1)}, u32[]{:S(2)}, u32[]{:S(2)}) collective-permute-start(bf16[416,768]{1,0:T(8,128)(2,1)S(1)} %get-tuple-element.99), channel_id=1, source_target_pairs={{0,16},{16,0},{1,17},{17,1},{2,18},{18,2},{3,19},{19,3},{4,20},{20... | collective-permute-start | bytes 1916936 | tf_op jit(solution)/shard_map/ppermute | solution.py:301
  5.4 8.3 %collective-permute-start.3 = (bf16[208,768]{1,0:T(8,128)(2,1)S(1)}, bf16[208,768]{1,0:T(8,128)(2,1)S(1)}, u32[]{:S(2)}, u32[]{:S(2)}) collective-permute-start(bf16[208,768]{1,0:T(8,128)(2,1)S(1)} %bitcast.60), channel_id=1, source_target_pairs={{0,32},{1,33},{2,34},{3,35},{4,36},{5,37},{6,38},{7,39},{8,40},{9,... | collective-permute-start | bytes 958472 | tf_op jit(solution)/shard_map/ppermute | solution.py:285
  7.1 11.1 %collective-permute-start.4 = (bf16[208,768]{1,0:T(8,128)(2,1)S(1)}, bf16[208,768]{1,0:T(8,128)(2,1)S(1)}, u32[]{:S(2)}, u32[]{:S(2)}) collective-permute-start(bf16[208,768]{1,0:T(8,128)(2,1)S(1)} %bitcast.59), channel_id=1, source_target_pairs={{0,64},{1,65},{2,66},{3,67},{4,68},{5,69},{6,70},{7,71},{8,72},{9,... | collective-permute-start | bytes 958472 | tf_op jit(solution)/shard_map/ppermute | solution.py:285
  9.8 8.4 %collective-permute-start.5 = (bf16[208,768]{1,0:T(8,128)(2,1)S(1)}, bf16[208,768]{1,0:T(8,128)(2,1)S(1)}, u32[]{:S(2)}, u32[]{:S(2)}) collective-permute-start(bf16[208,768]{1,0:T(8,128)(2,1)S(1)} %bitcast.58), channel_id=1, source_target_pairs={{0,96},{1,97},{2,98},{3,99},{4,100},{5,101},{6,102},{7,103},{8,104... | collective-permute-start | bytes 958472 | tf_op jit(solution)/shard_map/ppermute | solution.py:285
  19.8 15.7 %collective-permute-start.8 = (bf16[640,768]{1,0:T(8,128)(2,1)S(1)}, bf16[640,768]{1,0:T(8,128)(2,1)S(1)}, u32[]{:S(2)}, u32[]{:S(2)}) collective-permute-start(bf16[640,768]{1,0:T(8,128)(2,1)S(1)} %get-tuple-element.100.own), channel_id=1, source_target_pairs={{0,12},{1,13},{2,14},{3,15},{4,0},{5,1},{6,2},{7,3},{8,4},{9,5},{1... | collective-permute-start | bytes 2949128 | tf_op jit(solution)/shard_map/ppermute | solution.py:285
  23.9 15.3 %collective-permute-start.7 = (bf16[640,768]{1,0:T(8,128)(2,1)S(1)}, bf16[640,768]{1,0:T(8,128)(2,1)S(1)}, u32[]{:S(2)}, u32[]{:S(2)}) collective-permute-start(bf16[640,768]{1,0:T(8,128)(2,1)S(1)} %get-tuple-element.100.own), channel_id=1, source_target_pairs={{0,3},{1,0},{2,1},{3,2},{4,7},{5,4},{6,5},{7,6},{8,11},{9,8},{10,9... | collective-permute-start | bytes 2949128 | tf_op jit(solution)/shard_map/ppermute | solution.py:285
  26.9 15.4 %collective-permute-start.6 = (bf16[640,768]{1,0:T(8,128)(2,1)S(1)}, bf16[640,768]{1,0:T(8,128)(2,1)S(1)}, u32[]{:S(2)}, u32[]{:S(2)}) collective-permute-start(bf16[640,768]{1,0:T(8,128)(2,1)S(1)} %get-tuple-element.100.own), channel_id=1, source_target_pairs={{0,1},{1,2},{2,3},{3,0},{4,5},{5,6},{6,7},{7,4},{8,9},{9,10},{10,1... | collective-permute-start | bytes 2949128 | tf_op jit(solution)/shard_map/ppermute | solution.py:285
  35.5 19.7 %collective-permute-start.11 = (bf16[640,768]{1,0:T(8,128)(2,1)S(1)}, bf16[640,768]{1,0:T(8,128)(2,1)S(1)}, u32[]{:S(2)}, u32[]{:S(2)}) collective-permute-start(bf16[640,768]{1,0:T(8,128)(2,1)S(1)} %collective-permute-done.8.z1), channel_id=1, source_target_pairs={{0,12},{1,13},{2,14},{3,15},{4,0},{5,1},{6,2},{7,3},{8,4},{9,5},{1... | collective-permute-start | bytes 2949128 | tf_op jit(solution)/shard_map/ppermute | solution.py:285
  39.2 16.0 %collective-permute-start.12 = (f32[8,128]{1,0:T(8,128)S(1)}, f32[8,128]{1,0:T(8,128)S(1)}, u32[]{:S(2)}, u32[]{:S(2)}) collective-permute-start(f32[8,128]{1,0:T(8,128)S(1)} %get-tuple-element.103.over_ref), channel_id=1, source_target_pairs={{0,16},{16,0},{1,17},{17,1},{2,18},{18,2},{3,19},{19,3},{4,20},{20... | collective-permute-start | bytes 12296 | tf_op jit(solution)/shard_map/ppermute | solution.py:301
  39.2 10.5 %collective-permute-start.10 = (bf16[320,768]{1,0:T(8,128)(2,1)S(1)}, bf16[320,768]{1,0:T(8,128)(2,1)S(1)}, u32[]{:S(2)}, u32[]{:S(2)}) collective-permute-start(bf16[320,768]{1,0:T(8,128)(2,1)S(1)} %slice.35), channel_id=1, source_target_pairs={{0,3},{1,0},{2,1},{3,2},{4,7},{5,4},{6,5},{7,6},{8,11},{9,8},{10,9... | collective-permute-start | bytes 1474568 | tf_op jit(solution)/shard_map/ppermute | solution.py:285
  42.3 10.3 %collective-permute-start.9 = (bf16[320,768]{1,0:T(8,128)(2,1)S(1)}, bf16[320,768]{1,0:T(8,128)(2,1)S(1)}, u32[]{:S(2)}, u32[]{:S(2)}) collective-permute-start(bf16[320,768]{1,0:T(8,128)(2,1)S(1)} %slice.34), channel_id=1, source_target_pairs={{0,1},{1,2},{2,3},{3,0},{4,5},{5,6},{6,7},{7,4},{8,9},{9,10},{10,1... | collective-permute-start | bytes 1474568 | tf_op jit(solution)/shard_map/ppermute | solution.py:285
  55.2 24.6 %copy-start = (bf16[512,768]{1,0:T(8,128)(2,1)S(1)}, bf16[512,768]{1,0:T(8,128)(2,1)}, u32[]{:S(2)}) copy-start(bf16[512,768]{1,0:T(8,128)(2,1)} %emb_ref.1) | copy-start | bytes 2359300
  55.2 24.6 %copy-start.2 = (s32[512]{0:T(512)S(1)}, s32[512]{0:T(512)}, u32[]{:S(2)}) copy-start(s32[512]{0:T(512)} %param.15) | copy-start | bytes 6148
  55.2 24.5 %copy-start.3 = (s32[512]{0:T(512)S(1)}, s32[512]{0:T(512)}, u32[]{:S(2)}) copy-start(s32[512]{0:T(512)} %param.12) | copy-start | bytes 6148
  55.2 24.5 %copy-start.4 = (s32[8]{0:T(128)S(1)}, s32[8]{0:T(128)}, u32[]{:S(2)}) copy-start(s32[8]{0:T(128)} %assign_ref.1) | copy-start | bytes 100
  61.4 17.0 %all-to-all-start.2 = ((f32[64,8,128]{2,1,0:T(8,128)}), f32[64,8,128]{2,1,0:T(8,128)S(1)}, u32[]{:S(2)}, u32[]{:S(2)}) async-start(f32[64,8,128]{2,1,0:T(8,128)} %bitcast.18), calls=%async_computation.2 | async-start | bytes 524288 | tf_op jit(solution)/shard_map/all_to_all | solution.py:345
  79.8 0.6 copy-start.5

commit v5 on v4

--- a/solution.py
+++ b/solution.py
@@ -18,7 +18,9 @@
 SEND = 96
 BLOCK = SEND + 8
 PACKED = 640
-HELD = PACKED - 16
+HEAD = 16
+HELD = PACKED - HEAD
+HALF = PACKED // 2
 FAR = 256.0
 VMEM = 16 * 2**20
 
@@ -53,7 +55,7 @@
     return out
 
 
-def prep_kernel(assign_ref, emb_ref, cid_ref, order_ref, place_ref, same_ref, other_ref):
+def prep_kernel(assign_ref, emb_ref, cid_ref, order_ref, place_ref, other_ref, both_ref, target_ref):
     wide = emb_ref[...].astype(F32)
     mean = jnp.mean(wide * wide, axis=1, keepdims=True)
     unit = (wide * lax.rsqrt(mean + 1e-06) * (1.0 / math.sqrt(WIDTH))).astype(BF16)
@@ -95,13 +97,19 @@
     at = jnp.where(at < 32, (at % 8) * BLOCK + SEND + at // 8, -1).astype(F32)
     target = jnp.concatenate([jnp.where(fits, group * BLOCK + in_group, -1.0), at], axis=1)
     both = jnp.concatenate([unit, numbers], axis=0)
+    both_ref[...] = both
+    target_ref[...] = jnp.broadcast_to(target, (8, ROWS + 128))
     half = 4 * BLOCK
-    for ref, first in ((other_ref, half), (same_ref, 0)):
-        placing = hot(iota_f((half, ROWS + 128), 0) == target - first)
-        ref[...] = mul(placing, both).astype(BF16)
-
-
-def pack_kernel(here_ref, from1_ref, from2_ref, from3_ref, out_ref, over_ref, in_ref):
+    placing = hot(iota_f((half, ROWS + 128), 0) == target - half)
+    other_ref[...] = mul(placing, both).astype(BF16)
+
+
+def same_kernel(both_ref, target_ref, same_ref):
+    placing = hot(iota_f((4 * BLOCK, ROWS + 128), 0) == target_ref[0:1, :])
+    same_ref[...] = mul(placing, both_ref[...]).astype(BF16)
+
+
+def pack_kernel(here_ref, from1_ref, from2_ref, from3_ref, out_ref, low_ref, high_ref, over_ref, in_ref):
     count = KINDS * BLOCK
     for k, ref in enumerate((here_ref, from1_ref, from2_ref, from3_ref)):
         in_ref[k * 2 * BLOCK : (k + 1) * 2 * BLOCK, :] = ref[...]
@@ -116,7 +124,7 @@
     source = jnp.zeros((KINDS, 1), F32)
     lane = iota_f((1, count), 1)
     position = jnp.full((1, count), -1.0, F32)
-    start = jnp.zeros((1, 1), F32)
+    start = jnp.full((1, 1), float(HEAD), F32)
     for b in range(KINDS):
         step = lane - b * BLOCK
         mine = n[b : b + 1, :]
@@ -125,9 +133,9 @@
         from_device = 2 * lax.rem(my_line - b // 2 + 4, 4) + lax.rem(my_core + b % 2, 2)
         source = jnp.where(line == b, from_device.astype(F32), source)
         start = start + mine
-    position = jnp.where(position < HELD, position, -1.0)
-    placing = hot(iota_f((HELD, count), 0) == position)
-    out_ref[0:HELD, :] = mul(placing, in_ref[...]).astype(BF16)
+    position = jnp.where(position < PACKED, position, -1.0)
+    placing = hot(iota_f((HELD, count), 0) == position - HEAD)
+    out_ref[HEAD:PACKED, :] = mul(placing, in_ref[...]).astype(BF16)
     step = iota_f((KINDS, PACKED), 1) - base
     mine = jnp.where((step >= 0.0) & (step < n), 1.0, 0.0)
     slot = jnp.sum(mine * step, axis=0, keepdims=True)
@@ -142,7 +150,7 @@
     full = ours & (jnp.sum(counts, axis=0, keepdims=True) > HELD)
     over = jnp.maximum(over, jnp.where(full, 1.0, 0.0))
     over = jnp.max(over, axis=1, keepdims=True)
-    valid = (code > 0.0) & (iota((1, PACKED), 1) < HELD)
+    valid = code > 0.0
     final = rows_of(
         jnp.where(valid, high, FAR),
         jnp.where(valid, low, 0.0),
@@ -152,12 +160,13 @@
     over_ref[...] = jnp.broadcast_to(over, (8, 128))
     final = jnp.concatenate([final, jnp.zeros((8, WIDTH - PACKED), F32)], axis=1)
     final = jnp.concatenate([final, jnp.zeros((8, WIDTH), F32)], axis=0)
-    out_ref[HELD:PACKED, :] = final.astype(BF16)
+    out_ref[0:HEAD, :] = final.astype(BF16)
+    low_ref[...] = out_ref[0:HALF, :]
+    high_ref[...] = out_ref[HALF:PACKED, :]
 
 
 def numbers_of(ref):
-    n = ref.shape[0]
-    return ref[n - 16 : n, :].astype(F32)[0:8, 0:PACKED]
+    return ref[0:HEAD, :].astype(F32)[0:8, 0:PACKED]
 
 
 def orders_of(numbers):
@@ -186,47 +195,85 @@
     return jnp.full((8, PACKED), -2.0, F32)
 
 
-def near_kernel(own, m1, m3, z1, best_ref, order_ref):
-    order_ref[...] = orders_down(z1, own, m1, m3)
-    for i, rows in enumerate((own, m1, m3)):
-        best_ref[i] = all_earlier(nothing(), rows, (z1, own), order_ref, 0)
-    best_ref[3] = all_earlier(nothing(), z1, (own, m1, m3), order_ref, 1)
-
-
-def middle_kernel(own, z1, m2a, m2b, near_ref, m2, best_ref, order_ref):
-    half = PACKED // 2
-    m2[0:half, :] = m2a[...]
-    m2[half:PACKED, :] = m2b[...]
-    order_ref[...] = orders_down(z1, own, m2)
-    best_ref[0] = all_earlier(nothing(), m2, (z1, own), order_ref, 0)
-    best_ref[1] = all_earlier(near_ref[3], z1, (m2,), order_ref, 2)
-
-
-def to_owners(best, numbers):
+def owner_lines(numbers, lines_ref, hot_ref, q):
+    lines_ref[q] = jnp.where((iota_f((KINDS, PACKED), 0) == numbers[3:4, :]) & (numbers[2:3, :] > 0.0), 1.0, 0.0)
+    code = jnp.transpose(rows_of(numbers[2:3, :]))[:, 0:1]
+    hot_ref[q] = hot(iota_f((PACKED, 128), 1) == code - 1.0)
+
+
+def half_earlier(best, rows, half, order):
+    return earlier_max(best, rows, orders_of(numbers_of(rows)), half, order)
+
+
+def first_kernel(own, z1a, z1b, z1, best_ref, lines_ref, hot_ref, order_ref):
+    z1[0:HALF, :] = z1a[...]
+    z1[HALF:PACKED, :] = z1b[...]
+    order_ref[...] = orders_down(z1, own)
+    best_ref[0] = all_earlier(nothing(), own, (z1, own), order_ref, 0)
+    best_ref[1] = all_earlier(nothing(), z1, (own,), order_ref, 1)
+    owner_lines(numbers_of(own), lines_ref, hot_ref, 0)
+    owner_lines(numbers_of(z1), lines_ref, hot_ref, 1)
+
+
+def near_kernel(own, m1, m3, z1, z2a, first_ref, best_ref, lines_ref, hot_ref, order_ref):
+    order_ref[...] = orders_down(z1, own, m1, m3, z2a)
+    there = order_ref[0:HALF, 4:5]
+    best_ref[2] = all_earlier(first_ref[1], z1, (m1, m3), order_ref, 2)
+    best_ref[0] = half_earlier(all_earlier(nothing(), m1, (z1, own), order_ref, 0), m1, z2a, there)
+    best_ref[1] = half_earlier(all_earlier(nothing(), m3, (z1, own), order_ref, 0), m3, z2a, there)
+    best_ref[3] = half_earlier(first_ref[0], own, z2a, there)
+    owner_lines(numbers_of(m1), lines_ref, hot_ref, 0)
+    owner_lines(numbers_of(m3), lines_ref, hot_ref, 1)
+
+
+def middle_kernel(
+    own, m2a, m2b, z1, z2a, near_ref, first_lines_ref, first_hot_ref, m2, best_ref, sent_ref, lines_ref, hot_ref, order_ref
+):
+    m2[0:HALF, :] = m2a[...]
+    m2[HALF:PACKED, :] = m2b[...]
+    order_ref[...] = orders_down(z1, own, m2, z2a)
+    best = all_earlier(near_ref[2], z1, (m2,), order_ref, 2)
+    best_ref[0] = half_earlier(
+        all_earlier(nothing(), m2, (z1, own), order_ref, 0), m2, z2a, order_ref[0:HALF, 3:4]
+    )
+    sent_ref[...] = to_owners(best, first_lines_ref[1], first_hot_ref[1])
+    owner_lines(numbers_of(m2), lines_ref, hot_ref, 0)
+
+
+def to_owners(best, lines, places):
     best = jnp.maximum(jnp.max(best, axis=0, keepdims=True), -1.0)
     high = best.astype(BF16).astype(F32)
     low = best - high
     middle = low.astype(BF16).astype(F32)
     low = low - middle
-    lines = jnp.where((iota_f((KINDS, PACKED), 0) == numbers[3:4, :]) & (numbers[2:3, :] > 0.0), 1.0, 0.0)
     pieces = jnp.concatenate([lines, lines * high, lines * middle, lines * low], axis=0)
-    code = jnp.transpose(rows_of(numbers[2:3, :]))[:, 0:1]
-    put = mul(pieces.astype(BF16), hot(iota_f((PACKED, 128), 1) == code - 1.0))
+    put = mul(pieces.astype(BF16), places)
     return (put[0:8, :] - 1.0) + (put[8:16, :] + put[16:24, :] + put[24:32, :])
 
 
 OVER = 5 * KINDS
 
 
-def far_kernel(own, m1, m3, m2, z1, z2, near_ref, middle_ref, over_ref, other_over_ref, out_ref, order_ref, sent):
-    order_ref[...] = orders_down(z2)
+def far_kernel(
+    own, m1, m3, m2, z2b, first_lines, first_hot, near_ref, near_lines, near_hot,
+    middle_ref, middle_sent, middle_lines, middle_hot, orders, over_ref, other_over_ref, out_ref, sent,
+):
     sent[...] = jnp.zeros((128, 128), F32)
     over = jnp.maximum(over_ref[...], other_over_ref[...])
     sent[OVER : OVER + 8, :] = over
-    sent[4 * KINDS : 5 * KINDS, :] = to_owners(middle_ref[1], numbers_of(z1))
-    for q, (rows, best) in enumerate(((own, near_ref[0]), (m1, near_ref[1]), (m3, near_ref[2]), (m2, middle_ref[0]))):
-        best = all_earlier(best, rows, (z2,), order_ref, 0)
-        sent[q * KINDS : (q + 1) * KINDS, :] = to_owners(best, numbers_of(rows))
+    sent[3 * KINDS : 4 * KINDS, :] = middle_sent[...]
+    there = orders[HALF:PACKED, 3:4]
+    bests = [
+        half_earlier(best, rows, z2b, there)
+        for rows, best in ((own, near_ref[3]), (m1, near_ref[0]), (m3, near_ref[1]), (m2, middle_ref[0]))
+    ]
+    for q, best, lines, places in (
+        (0, bests[0], first_lines[0], first_hot[0]),
+        (1, bests[1], near_lines[0], near_hot[0]),
+        (2, bests[2], near_lines[1], near_hot[1]),
+        (4, bests[3], middle_lines[0], middle_hot[0]),
+    ):
+        sent[q * KINDS : (q + 1) * KINDS, :] = to_owners(best, lines, places)
     out_ref[...] = jnp.broadcast_to(over[0:1, :], (512, 128))
     to_x = jnp.where(lax.axis_index("core") == 0, lax.axis_index("x"), lax.axis_index("y"))
     out_ref[pl.ds(pl.multiple_of(to_x * 128, 128), 128), :] = jnp.transpose(sent[...])
@@ -245,7 +292,7 @@
     got = jnp.transpose(picked[...])
     lane = iota((KINDS, 128), 1) % 32
     best = got[0:KINDS, :]
-    for q, away in ((1, 3), (2, 1), (3, 2)):
+    for q, away in ((1, 3), (2, 1), (4, 2)):
         part = got[q * KINDS : (q + 1) * KINDS, :]
         moved = jnp.where(
             lane >= 8 * away,
@@ -253,7 +300,7 @@
             pltpu.roll(part, 128 + 8 * away - 32, 1),
         )
         best = jnp.maximum(best, moved)
-    part = got[4 * KINDS : 5 * KINDS, :]
+    part = got[3 * KINDS : 4 * KINDS, :]
     best = jnp.maximum(best, jnp.where(my_core == 0, pltpu.roll(part, 32, 1), pltpu.roll(part, 96, 1)))
     shift = lane // 8 - iota((KINDS, 128), 0) // 2
     turned = best
@@ -307,41 +354,55 @@
     line = lambda a: a.reshape(1, ROWS)
     cheap = pl.CostEstimate(flops=10**9, bytes_accessed=2 * 10**6, transcendentals=0)
     blocks = jax.ShapeDtypeStruct((4 * BLOCK, WIDTH), BF16)
-    same, other = call(
+    other, pool, target = call(
         prep_kernel,
-        (blocks, blocks),
+        (
+            blocks,
+            jax.ShapeDtypeStruct((ROWS + 128, WIDTH), BF16),
+            jax.ShapeDtypeStruct((8, ROWS + 128), F32),
+        ),
         ins=[smem] + [vmem] * 4,
         cost=cheap,
     )(assignment, embeddings, line(cluster_id), line(row_order), line(placement))
     other = core_swap(other)
+    same = call(same_kernel, blocks, cost=cheap)(pool, target)
     shape = (4, 1, BLOCK, WIDTH)
     both = jnp.concatenate([same.reshape(shape), other.reshape(shape)], axis=1).reshape(4, 2 * BLOCK, WIDTH)
-    own, over = call(
+    piece = jax.ShapeDtypeStruct((HALF, WIDTH), BF16)
+    part = jax.ShapeDtypeStruct((PACKED, WIDTH), BF16)
+    own, low, high, over = call(
         pack_kernel,
-        (jax.ShapeDtypeStruct((PACKED, WIDTH), BF16), jax.ShapeDtypeStruct((8, 128), F32)),
+        (part, piece, piece, jax.ShapeDtypeStruct((8, 128), F32)),
         [pltpu.VMEM((KINDS * BLOCK, WIDTH), BF16)],
         cost=cheap,
     )(both[0], *[across(both[k], k) for k in (1, 2, 3)])
-    half = PACKED // 2
-    z1, m1, m3 = down(own), along(own, 1), along(own, -1)
+    z1a, z1b = down(low), down(high)
+    m1, m3 = along(own, 1), along(own, -1)
     other_over = core_swap(over)
-    z2, m2a, m2b = down(z1), along(m1[:half], 1), along(m3[half:], -1)
+    z2a, z2b = down(z1a), down(z1b)
+    m2a, m2b = along(m1[:HALF], 1), along(m3[HALF:], -1)
     product = 2 * PACKED * PACKED * WIDTH
     cost = lambda n: pl.CostEstimate(flops=n * product, bytes_accessed=6 * 10**6, transcendentals=0)
     order = pltpu.VMEM((PACKED, 8), F32)
-    near = call(near_kernel, jax.ShapeDtypeStruct((4, 8, PACKED), F32), [order], cost=cost(9))(own, m1, m3, z1)
-    m2, middle = call(
+    made = lambda n, k: (
+        jax.ShapeDtypeStruct((n, 8, PACKED), F32),
+        jax.ShapeDtypeStruct((k, 8, PACKED), F32),
+        jax.ShapeDtypeStruct((k, PACKED, 128), BF16),
+    )
+    z1, *first = call(first_kernel, (part, *made(2, 2)), [order], cost=cost(3))(own, z1a, z1b)
+    near = call(near_kernel, made(4, 2), [order], cost=cost(7))(own, m1, m3, z1, z2a, first[0])
+    best, lines, hots = made(1, 1)
+    m2, *middle, orders = call(
         middle_kernel,
-        (jax.ShapeDtypeStruct((PACKED, WIDTH), BF16), jax.ShapeDtypeStruct((2, 8, PACKED), F32)),
-        [order],
+        (part, best, jax.ShapeDtypeStruct((8, 128), F32), lines, hots, jax.ShapeDtypeStruct((PACKED, 8), F32)),
         cost=cost(3),
-    )(own, z1, m2a, m2b, near)
+    )(own, m2a, m2b, z1, z2a, near[0], *first[1:])
     back = call(
         far_kernel,
         jax.ShapeDtypeStruct((512, 128), F32),
-        [order, pltpu.VMEM((128, 128), F32)],
-        cost=cost(4),
-    )(own, m1, m3, m2, z1, z2, near, middle, over, other_over)
+        [pltpu.VMEM((128, 128), F32)],
+        cost=cost(2),
+    )(own, m1, m3, m2, z2b, *first[1:], *near, *middle, orders, over, other_over)
     back = lax.all_to_all(back, ("x", "z", "y"), split_axis=0, concat_axis=0, tiled=True)
     best, over = call(
         final_kernel,

time: 80.6 us -> 78 us (0.968)
  waiting for transfers between devices: 31 us -> 24.7 us
  starting transfers between devices: 26.6 us -> 31.2 us
  Pallas kernels: 21.2 us -> 20.3 us
    ppermute x9 -> x11, waiting for transfers between devices: 18.5 us -> 12.9 us  [move(): return lax.ppermute(a, AXES, [(at(*p), at(*to(*p))) for p in places])]
    ppermute x9 -> x11, starting transfers between devices: 20 us -> 22.9 us  [move(): return lax.ppermute(a, AXES, [(at(*p), at(*to(*p))) for p in places])]
    all_to_all x1, starting transfers between devices: 6.54 us -> 8.19 us  [fast(): lax.all_to_all(back, ('x', 'z', 'y'), split_axis=0, concat_axis=0, tiled=...]
    pallas_call x5 -> x7, Pallas kernels: 20.5 us -> 19.5 us  [the longest x1 6.17 us: fast(): call(near_kernel, made(4, 2), [order], cost=cost(7))]
  transfers between devices with their start and end apart: 12 -> 14, of which waited for: 6 -> 5; matrix products, arithmetic and copies ran while one was open for 0% -> 0% of each run, Pallas kernels for 12% -> 16%
where the time goes in v5:
time: 78 us; the launch traced here: 77.8 us
  starting transfers between devices  31.2 us (40%)
  waiting for transfers between devices  24.7 us (32%)
  Pallas kernels  20.3 us (26%)
  between operations  0.85 us (1%)
    ppermute x11, starting transfers between devices, move(): return lax.ppermute(a, AXES, [(at(*p), at(*to(*p))) for p in places])  22.9 us
    ppermute x11, waiting for transfers between devices, move(): return lax.ppermute(a, AXES, [(at(*p), at(*to(*p))) for p in places])  12.9 us
    all_to_all x1, waiting for transfers between devices, fast(): lax.all_to_all(back, ('x', 'z', 'y'), split_axis=0, concat_axis=0, tiled=...  10.4 us
    all_to_all x1, starting transfers between devices, fast(): lax.all_to_all(back, ('x', 'z', 'y'), split_axis=0, concat_axis=0, tiled=...  8.19 us
    pallas_call x1, Pallas kernels, fast(): call(near_kernel, made(4, 2), [order], cost=cost(7))  6.17 us
    pallas_call x1, Pallas kernels, fast(): call(middle_kernel, (part, best, jax.ShapeDtypeStruct((8, 128), F32), lin...  3.04 us
    pallas_call x1, Pallas kernels, fast(): call(prep_kernel, (blocks, jax.ShapeDtypeStruct((ROWS + 128, WIDTH), BF16...  2.8 us
    pallas_call x1, Pallas kernels, fast(): call(first_kernel, (part, *made(2, 2)), [order], cost=cost(3))  2.67 us
  transfers between devices with their start and end apart: 14, of which 5 were waited for; matrix products, arithmetic and copies ran while one was open for 0% of the time, Pallas kernels for 16%

profile of v5, /device:TPU:0, one launch (start us, length us, event | category | flops | bytes accessed | tf_op | source)
XLA Modules:
  0.0 77.8 jit_solution(8624705341857512882)
XLA Ops:
  0.0 2.8 %shard_map.57 = (bf16[416,768]{1,0:T(8,128)(2,1)S(1)}, bf16[640,768]{1,0:T(8,128)(2,1)S(1)}, f32[8,640]{1,0:T(8,128)S(1)}) custom-call(s32[8]{0:T(128)} %assign_ref.1, bf16[512,768]{1,0:T(8,128)(2,1)} %emb_ref.1, s32[1,512]{1,0:T(1,128)} %bitcast.63, s32[1,512]{1,0:T(1,128)} %bitcast.65, s32[1,512]{1,0:T(1,128)} %bitcast.62), custom_call_target="tpu_custom_call" | custom-call | flops 1000000000 | bytes 2000000 | tf_op jit(solution)/shard_map/pallas_call | solution.py:357
  2.8 0.1 collective-permute-start.2
  2.9 0.7 shard_map.58
  3.6 1.4 %collective-permute-done.2 = bf16[416,768]{1,0:T(8,128)(2,1)S(1)} collective-permute-done((bf16[416,768]{1,0:T(8,128)(2,1)S(1)}, bf16[416,768]{1,0:T(8,128)(2,1)S(1)}, u32[]{:S(2)}, u32[]{:S(2)}) %collective-permute-start.2) | collective-permute-done | bytes 639008 | tf_op jit(solution)/shard_map/ppermute | solution.py:348
  5.0 0.1 pad_maximum_fusion
  5.1 1.6 %collective-permute-start.3 = (bf16[208,768]{1,0:T(8,128)(2,1)S(1)}, bf16[208,768]{1,0:T(8,128)(2,1)S(1)}, u32[]{:S(2)}, u32[]{:S(2)}) collective-permute-start(bf16[208,768]{1,0:T(8,128)(2,1)S(1)} %bitcast.60), channel_id=1, source_target_pairs={{0,32},{1,33},{2,34},{3,35},{4,36},{5,37},{6,38},{7,39},{8,40},{9,... | collective-permute-start | bytes 958472 | tf_op jit(solution)/shard_map/ppermute | solution.py:332
  6.7 2.7 %collective-permute-start.4 = (bf16[208,768]{1,0:T(8,128)(2,1)S(1)}, bf16[208,768]{1,0:T(8,128)(2,1)S(1)}, u32[]{:S(2)}, u32[]{:S(2)}) collective-permute-start(bf16[208,768]{1,0:T(8,128)(2,1)S(1)} %bitcast.59), channel_id=1, source_target_pairs={{0,64},{1,65},{2,66},{3,67},{4,68},{5,69},{6,70},{7,71},{8,72},{9,... | collective-permute-start | bytes 958472 | tf_op jit(solution)/shard_map/ppermute | solution.py:332
  9.5 1.4 %collective-permute-start.5 = (bf16[208,768]{1,0:T(8,128)(2,1)S(1)}, bf16[208,768]{1,0:T(8,128)(2,1)S(1)}, u32[]{:S(2)}, u32[]{:S(2)}) collective-permute-start(bf16[208,768]{1,0:T(8,128)(2,1)S(1)} %bitcast.58), channel_id=1, source_target_pairs={{0,96},{1,97},{2,98},{3,99},{4,100},{5,101},{6,102},{7,103},{8,104... | collective-permute-start | bytes 958472 | tf_op jit(solution)/shard_map/ppermute | solution.py:332
  10.9 2.5 %collective-permute-done.3.from1_ref = bf16[208,768]{1,0:T(8,128)(2,1)S(1)} collective-permute-done((bf16[208,768]{1,0:T(8,128)(2,1)S(1)}, bf16[208,768]{1,0:T(8,128)(2,1)S(1)}, u32[]{:S(2)}, u32[]{:S(2)}) %collective-permute-start.3) | collective-permute-done | bytes 319520 | tf_op jit(solution)/shard_map/ppermute | solution.py:332
  13.3 4.5 %collective-permute-done.4.from2_ref = bf16[208,768]{1,0:T(8,128)(2,1)S(1)} collective-permute-done((bf16[208,768]{1,0:T(8,128)(2,1)S(1)}, bf16[208,768]{1,0:T(8,128)(2,1)S(1)}, u32[]{:S(2)}, u32[]{:S(2)}) %collective-permute-start.4) | collective-permute-done | bytes 319520 | tf_op jit(solution)/shard_map/ppermute | solution.py:332
  17.8 0.0 collective-permute-done.5.from3_ref
  17.8 1.5 %shard_map.59 = (bf16[640,768]{1,0:T(8,128)(2,1)S(1)}, bf16[320,768]{1,0:T(8,128)(2,1)S(1)}, bf16[320,768]{1,0:T(8,128)(2,1)S(1)}, f32[8,128]{1,0:T(8,128)S(1)}) custom-call(bf16[208,768]{1,0:T(8,128)(2,1)S(1)} %bitcast.49, bf16[208,768]{1,0:T(8,128)(2,1)S(1)} %collective-permute-done.3.from1_ref, bf16[208,768]{1,0:T(8,128)(2,1)S(1)} %collective-permute-done.4.from2_ref, ...), custom_call_target="tpu_custom_call" | custom-call | flops 1000000000 | bytes 2000000 | tf_op jit(solution)/shard_map/pallas_call | solution.py:373
  19.4 1.6 %collective-permute-start.6 = (bf16[640,768]{1,0:T(8,128)(2,1)S(1)}, bf16[640,768]{1,0:T(8,128)(2,1)S(1)}, u32[]{:S(2)}, u32[]{:S(2)}) collective-permute-start(bf16[640,768]{1,0:T(8,128)(2,1)S(1)} %get-tuple-element.115.own), channel_id=1, source_target_pairs={{0,1},{1,2},{2,3},{3,0},{4,5},{5,6},{6,7},{7,4},{8,9},{9,10},{10,1... | collective-permute-start | bytes 2949128 | tf_op jit(solution)/shard_map/ppermute | solution.py:332
  21.0 1.7 %collective-permute-start.7 = (bf16[640,768]{1,0:T(8,128)(2,1)S(1)}, bf16[640,768]{1,0:T(8,128)(2,1)S(1)}, u32[]{:S(2)}, u32[]{:S(2)}) collective-permute-start(bf16[640,768]{1,0:T(8,128)(2,1)S(1)} %get-tuple-element.115.own), channel_id=1, source_target_pairs={{0,3},{1,0},{2,1},{3,2},{4,7},{5,4},{6,5},{7,6},{8,11},{9,8},{10,9... | collective-permute-start | bytes 2949128 | tf_op jit(solution)/shard_map/ppermute | solution.py:332
  22.7 4.0 %collective-permute-start.10 = (bf16[320,768]{1,0:T(8,128)(2,1)S(1)}, bf16[320,768]{1,0:T(8,128)(2,1)S(1)}, u32[]{:S(2)}, u32[]{:S(2)}) collective-permute-start(bf16[320,768]{1,0:T(8,128)(2,1)S(1)} %get-tuple-element.116), channel_id=1, source_target_pairs={{0,12},{1,13},{2,14},{3,15},{4,0},{5,1},{6,2},{7,3},{8,4},{9,5},{1... | collective-permute-start | bytes 1474568 | tf_op jit(solution)/shard_map/ppermute | solution.py:332
  26.7 0.4 collective-permute-start.11
  27.1 5.9 %collective-permute-done.10.z1a = bf16[320,768]{1,0:T(8,128)(2,1)S(1)} collective-permute-done((bf16[320,768]{1,0:T(8,128)(2,1)S(1)}, bf16[320,768]{1,0:T(8,128)(2,1)S(1)}, u32[]{:S(2)}, u32[]{:S(2)}) %collective-permute-start.10) | collective-permute-done | bytes 491552 | tf_op jit(solution)/shard_map/ppermute | solution.py:332
  33.1 3.7 %collective-permute-start.12 = (bf16[320,768]{1,0:T(8,128)(2,1)S(1)}, bf16[320,768]{1,0:T(8,128)(2,1)S(1)}, u32[]{:S(2)}, u32[]{:S(2)}) collective-permute-start(bf16[320,768]{1,0:T(8,128)(2,1)S(1)} %collective-permute-done.10.z1a), channel_id=1, source_target_pairs={{0,12},{1,13},{2,14},{3,15},{4,0},{5,1},{6,2},{7,3},{8,4},{9,5},{1... | collective-permute-start | bytes 1474568 | tf_op jit(solution)/shard_map/ppermute | solution.py:332
  36.8 0.0 collective-permute-start.14
  36.8 0.0 collective-permute-done.6.m1
  36.8 0.4 collective-permute-start.8
  37.3 0.0 collective-permute-done.7.m3
  37.3 2.9 %collective-permute-start.9 = (bf16[320,768]{1,0:T(8,128)(2,1)S(1)}, bf16[320,768]{1,0:T(8,128)(2,1)S(1)}, u32[]{:S(2)}, u32[]{:S(2)}) collective-permute-start(bf16[320,768]{1,0:T(8,128)(2,1)S(1)} %slice.35), channel_id=1, source_target_pairs={{0,3},{1,0},{2,1},{3,2},{4,7},{5,4},{6,5},{7,6},{8,11},{9,8},{10,9... | collective-permute-start | bytes 1474568 | tf_op jit(solution)/shard_map/ppermute | solution.py:332
  40.2 0.0 collective-permute-done.11.z1b
  40.2 2.7 %shard_map.60 = (bf16[640,768]{1,0:T(8,128)(2,1)S(1)}, f32[2,8,640]{2,1,0:T(8,128)S(1)}, f32[2,8,640]{2,1,0:T(8,128)S(1)}, bf16[2,640,128]{2,1,0:T(8,128)(2,1)S(1)}) custom-call(bf16[640,768]{1,0:T(8,128)(2,1)S(1)} %get-tuple-element.115.own, bf16[320,768]{1,0:T(8,128)(2,1)S(1)} %collective-permute-done.10.z1a, bf16[320,768]{1,0:T(8,128)(2,1)S(1)} %collective-permute-done.11.z1b), custom_call_target="tpu_custom_call" | custom-call | flops 1887436800 | bytes 6000000 | tf_op jit(solution)/shard_map/pallas_call | solution.py:392
  42.9 2.3 %collective-permute-start.13 = (bf16[320,768]{1,0:T(8,128)(2,1)S(1)}, bf16[320,768]{1,0:T(8,128)(2,1)S(1)}, u32[]{:S(2)}, u32[]{:S(2)}) collective-permute-start(bf16[320,768]{1,0:T(8,128)(2,1)S(1)} %collective-permute-done.11.z1b), channel_id=1, source_target_pairs={{0,12},{1,13},{2,14},{3,15},{4,0},{5,1},{6,2},{7,3},{8,4},{9,5},{1... | collective-permute-start | bytes 1474568 | tf_op jit(solution)/shard_map/ppermute | solution.py:332
  45.2 0.0 collective-permute-done.12.z2a
  45.2 6.2 %shard_map.61 = (f32[4,8,640]{2,1,0:T(8,128)S(1)}, f32[2,8,640]{2,1,0:T(8,128)S(1)}, bf16[2,640,128]{2,1,0:T(8,128)(2,1)S(1)}) custom-call(bf16[640,768]{1,0:T(8,128)(2,1)S(1)} %get-tuple-element.115.own, bf16[640,768]{1,0:T(8,128)(2,1)S(1)} %collective-permute-done.6.m1, bf16[640,768]{1,0:T(8,128)(2,1)S(1)} %collective-permute-done.7.m3, ...), custom_call_target="tpu_custom_call" | custom-call | flops 4404019200 | bytes 6000000 | tf_op jit(solution)/shard_map/pallas_call | solution.py:393
  51.4 0.0 collective-permute-done.8.m2a
  51.4 0.0 collective-permute-done.9.m2b
  51.4 3.0 %shard_map.62 = (bf16[640,768]{1,0:T(8,128)(2,1)S(1)}, f32[1,8,640]{2,1,0:T(8,128)S(1)}, f32[8,128]{1,0:T(8,128)S(1)}, f32[1,8,640]{2,1,0:T(8,128)S(1)}, bf16[1,...) custom-call(bf16[640,768]{1,0:T(8,128)(2,1)S(1)} %get-tuple-element.115.own, ...), custom_call_target="tpu_custom_call" | custom-call | flops 1887436800 | bytes 6000000 | tf_op jit(solution)/shard_map/pallas_call | solution.py:395
  54.4 0.0 collective-permute-done.14.other_over_ref
  54.4 0.0 collective-permute-done.13.z2b
  54.4 0.0 copy-start
  54.5 0.0 copy-start.2
  54.5 0.0 copy-start.3
  54.5 0.0 copy-start.4
  54.5 2.7 %shard_map.63 = f32[512,128]{1,0:T(8,128)} custom-call(bf16[640,768]{1,0:T(8,128)(2,1)S(1)} %get-tuple-element.115.own, bf16[640,768]{1,0:T(8,128)(2,1)S(1)} %collective-permute-done.6.m1, bf16[640,768]{1,0:T(8,128)(2,1)S(1)} %collective-permute-done.7.m3, bf16[640,768]{1,0:T(8,128)(2,1)S(1)} %get-tuple-element.123.m2, ...), custom_call_target="tpu_custom_call" | custom-call | flops 1258291200 | bytes 6000000 | tf_op jit(solution)/shard_map/pallas_call | solution.py:400
  57.2 8.2 %all-to-all-start.2 = ((f32[64,8,128]{2,1,0:T(8,128)}), f32[64,8,128]{2,1,0:T(8,128)S(1)}, u32[]{:S(2)}, u32[]{:S(2)}) async-start(f32[64,8,128]{2,1,0:T(8,128)} %bitcast.18), calls=%async_computation.2 | async-start | bytes 524288 | tf_op jit(solution)/shard_map/all_to_all | solution.py:406
  65.3 10.4 %all-to-all-done.2 = f32[64,8,128]{2,1,0:T(8,128)S(1)} async-done(((f32[64,8,128]{2,1,0:T(8,128)}), f32[64,8,128]{2,1,0:T(8,128)S(1)}, u32[]{:S(2)}, u32[]{:S(2)}) %all-to-all-start.2) | async-done | bytes 262176 | tf_op jit(solution)/shard_map/all_to_all | solution.py:406
  75.8 0.7 shard_map.64
  77.2 0.0 copy-done
  77.2 0.0 copy-done.2
  77.2 0.0 copy-done.3
  77.2 0.0 copy-done.4
  77.2 0.0 copy-start.5
  77.2 0.6 copy-done.5
  (3 shorter events, 0.1 us)
Async XLA Ops:
  2.8 2.2 %collective-permute-start.2 = (bf16[416,768]{1,0:T(8,128)(2,1)S(1)}, bf16[416,768]{1,0:T(8,128)(2,1)S(1)}, u32[]{:S(2)}, u32[]{:S(2)}) collective-permute-start(bf16[416,768]{1,0:T(8,128)(2,1)S(1)} %get-tuple-element.114), channel_id=1, source_target_pairs={{0,16},{16,0},{1,17},{17,1},{2,18},{18,2},{3,19},{19,3},{4,20},{20... | collective-permute-start | bytes 1916936 | tf_op jit(solution)/shard_map/ppermute | solution.py:348
  5.1 8.3 %collective-permute-start.3 = (bf16[208,768]{1,0:T(8,128)(2,1)S(1)}, bf16[208,768]{1,0:T(8,128)(2,1)S(1)}, u32[]{:S(2)}, u32[]{:S(2)}) collective-permute-start(bf16[208,768]{1,0:T(8,128)(2,1)S(1)} %bitcast.60), channel_id=1, source_target_pairs={{0,32},{1,33},{2,34},{3,35},{4,36},{5,37},{6,38},{7,39},{8,40},{9,... | collective-permute-start | bytes 958472 | tf_op jit(solution)/shard_map/ppermute | solution.py:332
  6.7 11.1 %collective-permute-start.4 = (bf16[208,768]{1,0:T(8,128)(2,1)S(1)}, bf16[208,768]{1,0:T(8,128)(2,1)S(1)}, u32[]{:S(2)}, u32[]{:S(2)}) collective-permute-start(bf16[208,768]{1,0:T(8,128)(2,1)S(1)} %bitcast.59), channel_id=1, source_target_pairs={{0,64},{1,65},{2,66},{3,67},{4,68},{5,69},{6,70},{7,71},{8,72},{9,... | collective-permute-start | bytes 958472 | tf_op jit(solution)/shard_map/ppermute | solution.py:332
  9.5 8.4 %collective-permute-start.5 = (bf16[208,768]{1,0:T(8,128)(2,1)S(1)}, bf16[208,768]{1,0:T(8,128)(2,1)S(1)}, u32[]{:S(2)}, u32[]{:S(2)}) collective-permute-start(bf16[208,768]{1,0:T(8,128)(2,1)S(1)} %bitcast.58), channel_id=1, source_target_pairs={{0,96},{1,97},{2,98},{3,99},{4,100},{5,101},{6,102},{7,103},{8,104... | collective-permute-start | bytes 958472 | tf_op jit(solution)/shard_map/ppermute | solution.py:332
  19.4 17.4 %collective-permute-start.6 = (bf16[640,768]{1,0:T(8,128)(2,1)S(1)}, bf16[640,768]{1,0:T(8,128)(2,1)S(1)}, u32[]{:S(2)}, u32[]{:S(2)}) collective-permute-start(bf16[640,768]{1,0:T(8,128)(2,1)S(1)} %get-tuple-element.115.own), channel_id=1, source_target_pairs={{0,1},{1,2},{2,3},{3,0},{4,5},{5,6},{6,7},{7,4},{8,9},{9,10},{10,1... | collective-permute-start | bytes 2949128 | tf_op jit(solution)/shard_map/ppermute | solution.py:332
  21.0 16.2 %collective-permute-start.7 = (bf16[640,768]{1,0:T(8,128)(2,1)S(1)}, bf16[640,768]{1,0:T(8,128)(2,1)S(1)}, u32[]{:S(2)}, u32[]{:S(2)}) collective-permute-start(bf16[640,768]{1,0:T(8,128)(2,1)S(1)} %get-tuple-element.115.own), channel_id=1, source_target_pairs={{0,3},{1,0},{2,1},{3,2},{4,7},{5,4},{6,5},{7,6},{8,11},{9,8},{10,9... | collective-permute-start | bytes 2949128 | tf_op jit(solution)/shard_map/ppermute | solution.py:332
  22.7 10.4 %collective-permute-start.10 = (bf16[320,768]{1,0:T(8,128)(2,1)S(1)}, bf16[320,768]{1,0:T(8,128)(2,1)S(1)}, u32[]{:S(2)}, u32[]{:S(2)}) collective-permute-start(bf16[320,768]{1,0:T(8,128)(2,1)S(1)} %get-tuple-element.116), channel_id=1, source_target_pairs={{0,12},{1,13},{2,14},{3,15},{4,0},{5,1},{6,2},{7,3},{8,4},{9,5},{1... | collective-permute-start | bytes 1474568 | tf_op jit(solution)/shard_map/ppermute | solution.py:332
  26.7 13.5 %collective-permute-start.11 = (bf16[320,768]{1,0:T(8,128)(2,1)S(1)}, bf16[320,768]{1,0:T(8,128)(2,1)S(1)}, u32[]{:S(2)}, u32[]{:S(2)}) collective-permute-start(bf16[320,768]{1,0:T(8,128)(2,1)S(1)} %get-tuple-element.117), channel_id=1, source_target_pairs={{0,12},{1,13},{2,14},{3,15},{4,0},{5,1},{6,2},{7,3},{8,4},{9,5},{1... | collective-permute-start | bytes 1474568 | tf_op jit(solution)/shard_map/ppermute | solution.py:332
  33.1 12.1 %collective-permute-start.12 = (bf16[320,768]{1,0:T(8,128)(2,1)S(1)}, bf16[320,768]{1,0:T(8,128)(2,1)S(1)}, u32[]{:S(2)}, u32[]{:S(2)}) collective-permute-start(bf16[320,768]{1,0:T(8,128)(2,1)S(1)} %collective-permute-done.10.z1a), channel_id=1, source_target_pairs={{0,12},{1,13},{2,14},{3,15},{4,0},{5,1},{6,2},{7,3},{8,4},{9,5},{1... | collective-permute-start | bytes 1474568 | tf_op jit(solution)/shard_map/ppermute | solution.py:332
  36.8 17.7 %collective-permute-start.14 = (f32[8,128]{1,0:T(8,128)S(1)}, f32[8,128]{1,0:T(8,128)S(1)}, u32[]{:S(2)}, u32[]{:S(2)}) collective-permute-start(f32[8,128]{1,0:T(8,128)S(1)} %get-tuple-element.131.over_ref), channel_id=1, source_target_pairs={{0,16},{16,0},{1,17},{17,1},{2,18},{18,2},{3,19},{19,3},{4,20},{20... | collective-permute-start | bytes 12296 | tf_op jit(solution)/shard_map/ppermute | solution.py:348
  36.8 14.5 %collective-permute-start.8 = (bf16[320,768]{1,0:T(8,128)(2,1)S(1)}, bf16[320,768]{1,0:T(8,128)(2,1)S(1)}, u32[]{:S(2)}, u32[]{:S(2)}) collective-permute-start(bf16[320,768]{1,0:T(8,128)(2,1)S(1)} %slice.34), channel_id=1, source_target_pairs={{0,1},{1,2},{2,3},{3,0},{4,5},{5,6},{6,7},{7,4},{8,9},{9,10},{10,1... | collective-permute-start | bytes 1474568 | tf_op jit(solution)/shard_map/ppermute | solution.py:332
  37.3 14.1 %collective-permute-start.9 = (bf16[320,768]{1,0:T(8,128)(2,1)S(1)}, bf16[320,768]{1,0:T(8,128)(2,1)S(1)}, u32[]{:S(2)}, u32[]{:S(2)}) collective-permute-start(bf16[320,768]{1,0:T(8,128)(2,1)S(1)} %slice.35), channel_id=1, source_target_pairs={{0,3},{1,0},{2,1},{3,2},{4,7},{5,4},{6,5},{7,6},{8,11},{9,8},{10,9... | collective-permute-start | bytes 1474568 | tf_op jit(solution)/shard_map/ppermute | solution.py:332
  42.9 11.5 %collective-permute-start.13 = (bf16[320,768]{1,0:T(8,128)(2,1)S(1)}, bf16[320,768]{1,0:T(8,128)(2,1)S(1)}, u32[]{:S(2)}, u32[]{:S(2)}) collective-permute-start(bf16[320,768]{1,0:T(8,128)(2,1)S(1)} %collective-permute-done.11.z1b), channel_id=1, source_target_pairs={{0,12},{1,13},{2,14},{3,15},{4,0},{5,1},{6,2},{7,3},{8,4},{9,5},{1... | collective-permute-start | bytes 1474568 | tf_op jit(solution)/shard_map/ppermute | solution.py:332
  54.4 22.7 %copy-start = (bf16[512,768]{1,0:T(8,128)(2,1)S(1)}, bf16[512,768]{1,0:T(8,128)(2,1)}, u32[]{:S(2)}) copy-start(bf16[512,768]{1,0:T(8,128)(2,1)} %emb_ref.1) | copy-start | bytes 2359300
  54.5 22.7 %copy-start.2 = (s32[512]{0:T(512)S(1)}, s32[512]{0:T(512)}, u32[]{:S(2)}) copy-start(s32[512]{0:T(512)} %param.15) | copy-start | bytes 6148
  54.5 22.7 %copy-start.3 = (s32[512]{0:T(512)S(1)}, s32[512]{0:T(512)}, u32[]{:S(2)}) copy-start(s32[512]{0:T(512)} %param.12) | copy-start | bytes 6148
  54.5 22.7 %copy-start.4 = (s32[8]{0:T(128)S(1)}, s32[8]{0:T(128)}, u32[]{:S(2)}) copy-start(s32[8]{0:T(128)} %assign_ref.1) | copy-start | bytes 100
  57.2 18.6 %all-to-all-start.2 = ((f32[64,8,128]{2,1,0:T(8,128)}), f32[64,8,128]{2,1,0:T(8,128)S(1)}, u32[]{:S(2)}, u32[]{:S(2)}) async-start(f32[64,8,128]{2,1,0:T(8,128)} %bitcast.18), calls=%async_computation.2 | async-start | bytes 524288 | tf_op jit(solution)/shard_map/all_to_all | solution.py:406
  77.2 0.6 copy-start.5

commit v6 on v5

--- a/solution.py
+++ b/solution.py
@@ -205,38 +205,55 @@
     return earlier_max(best, rows, orders_of(numbers_of(rows)), half, order)
 
 
-def first_kernel(own, z1a, z1b, z1, best_ref, lines_ref, hot_ref, order_ref):
+def both_ways(best, far_best, rows, z1, z1_order):
+    scores = mul_nt(z1[...], rows[...])
+    earlier = z1_order < orders_of(numbers_of(rows))
+    count, n = scores.shape
+    ours = jnp.where(earlier, scores, -2.0)
+    theirs = jnp.where(earlier, -2.0, scores)
+    for k in range(n // 128):
+        far_best = jnp.maximum(far_best, theirs[:, k * 128 : (k + 1) * 128])
+    return jnp.maximum(best, jnp.max(ours.reshape(count // 8, 8, n), axis=0)), far_best
+
+
+def own_kernel(own, best_ref, lines_ref, hot_ref, order_ref):
+    order_ref[...] = orders_down(own)
+    best_ref[0] = all_earlier(nothing(), own, (own,), order_ref, 0)
+    owner_lines(numbers_of(own), lines_ref, hot_ref, 0)
+
+
+def ring_kernel(own, m1, m3, over_a, over_b, best_ref, lines_ref, hot_ref, over_ref, order_ref):
+    order_ref[...] = orders_down(own)
+    for i, rows in enumerate((m1, m3)):
+        best_ref[i] = all_earlier(nothing(), rows, (own,), order_ref, 0)
+        owner_lines(numbers_of(rows), lines_ref, hot_ref, i)
+    over_ref[...] = jnp.maximum(over_a[...], over_b[...])
+
+
+def near_kernel(own, m1, m3, z1a, z1b, z2a, own_ref, ring_ref, z1, best_ref, far_best_ref, lines_ref, hot_ref, order_ref):
     z1[0:HALF, :] = z1a[...]
     z1[HALF:PACKED, :] = z1b[...]
-    order_ref[...] = orders_down(z1, own)
-    best_ref[0] = all_earlier(nothing(), own, (z1, own), order_ref, 0)
-    best_ref[1] = all_earlier(nothing(), z1, (own,), order_ref, 1)
-    owner_lines(numbers_of(own), lines_ref, hot_ref, 0)
-    owner_lines(numbers_of(z1), lines_ref, hot_ref, 1)
-
-
-def near_kernel(own, m1, m3, z1, z2a, first_ref, best_ref, lines_ref, hot_ref, order_ref):
-    order_ref[...] = orders_down(z1, own, m1, m3, z2a)
-    there = order_ref[0:HALF, 4:5]
-    best_ref[2] = all_earlier(first_ref[1], z1, (m1, m3), order_ref, 2)
-    best_ref[0] = half_earlier(all_earlier(nothing(), m1, (z1, own), order_ref, 0), m1, z2a, there)
-    best_ref[1] = half_earlier(all_earlier(nothing(), m3, (z1, own), order_ref, 0), m3, z2a, there)
-    best_ref[3] = half_earlier(first_ref[0], own, z2a, there)
-    owner_lines(numbers_of(m1), lines_ref, hot_ref, 0)
-    owner_lines(numbers_of(m3), lines_ref, hot_ref, 1)
+    order_ref[...] = orders_down(z1, z2a)
+    far_best = jnp.full((PACKED, 128), -2.0, F32)
+    for i, (rows, best) in enumerate(((own, own_ref[0]), (m1, ring_ref[0]), (m3, ring_ref[1]))):
+        best, far_best = both_ways(best, far_best, rows, z1, order_ref[:, 0:1])
+        best_ref[i] = half_earlier(best, rows, z2a, order_ref[0:HALF, 1:2])
+    far_best_ref[...] = far_best
+    owner_lines(numbers_of(z1), lines_ref, hot_ref, 0)
 
 
 def middle_kernel(
-    own, m2a, m2b, z1, z2a, near_ref, first_lines_ref, first_hot_ref, m2, best_ref, sent_ref, lines_ref, hot_ref, order_ref
+    own, m2a, m2b, z1, z2a, far_best_ref, z1_lines, z1_hot, m2, best_ref, sent_ref, lines_ref, hot_ref, order_ref
 ):
     m2[0:HALF, :] = m2a[...]
     m2[HALF:PACKED, :] = m2b[...]
-    order_ref[...] = orders_down(z1, own, m2, z2a)
-    best = all_earlier(near_ref[2], z1, (m2,), order_ref, 2)
-    best_ref[0] = half_earlier(
-        all_earlier(nothing(), m2, (z1, own), order_ref, 0), m2, z2a, order_ref[0:HALF, 3:4]
-    )
-    sent_ref[...] = to_owners(best, first_lines_ref[1], first_hot_ref[1])
+    order_ref[...] = orders_down(z1, own, z2a)
+    best, far_best = both_ways(nothing(), far_best_ref[...], m2, z1, order_ref[:, 0:1])
+    far_best = jnp.max(far_best, axis=1, keepdims=True)
+    far_best = jnp.transpose(jnp.broadcast_to(far_best, (PACKED, 8)))
+    best = all_earlier(best, m2, (own,), order_ref, 1)
+    best_ref[0] = half_earlier(best, m2, z2a, order_ref[0:HALF, 2:3])
+    sent_ref[...] = to_owners(far_best, z1_lines[0], z1_hot[0])
     owner_lines(numbers_of(m2), lines_ref, hot_ref, 0)
 
 
@@ -255,22 +272,22 @@
 
 
 def far_kernel(
-    own, m1, m3, m2, z2b, first_lines, first_hot, near_ref, near_lines, near_hot,
-    middle_ref, middle_sent, middle_lines, middle_hot, orders, over_ref, other_over_ref, out_ref, sent,
+    own, m1, m3, m2, z2b, own_lines, own_hot, ring_lines, ring_hot, near_ref,
+    middle_ref, middle_sent, middle_lines, middle_hot, orders, over_ref, out_ref, sent,
 ):
     sent[...] = jnp.zeros((128, 128), F32)
-    over = jnp.maximum(over_ref[...], other_over_ref[...])
+    over = over_ref[...]
     sent[OVER : OVER + 8, :] = over
     sent[3 * KINDS : 4 * KINDS, :] = middle_sent[...]
-    there = orders[HALF:PACKED, 3:4]
+    there = orders[HALF:PACKED, 2:3]
     bests = [
         half_earlier(best, rows, z2b, there)
-        for rows, best in ((own, near_ref[3]), (m1, near_ref[0]), (m3, near_ref[1]), (m2, middle_ref[0]))
+        for rows, best in ((own, near_ref[0]), (m1, near_ref[1]), (m3, near_ref[2]), (m2, middle_ref[0]))
     ]
     for q, best, lines, places in (
-        (0, bests[0], first_lines[0], first_hot[0]),
-        (1, bests[1], near_lines[0], near_hot[0]),
-        (2, bests[2], near_lines[1], near_hot[1]),
+        (0, bests[0], own_lines[0], own_hot[0]),
+        (1, bests[1], ring_lines[0], ring_hot[0]),
+        (2, bests[2], ring_lines[1], ring_hot[1]),
         (4, bests[3], middle_lines[0], middle_hot[0]),
     ):
         sent[q * KINDS : (q + 1) * KINDS, :] = to_owners(best, lines, places)
@@ -389,20 +406,25 @@
         jax.ShapeDtypeStruct((k, 8, PACKED), F32),
         jax.ShapeDtypeStruct((k, PACKED, 128), BF16),
     )
-    z1, *first = call(first_kernel, (part, *made(2, 2)), [order], cost=cost(3))(own, z1a, z1b)
-    near = call(near_kernel, made(4, 2), [order], cost=cost(7))(own, m1, m3, z1, z2a, first[0])
+    flag = jax.ShapeDtypeStruct((8, 128), F32)
+    mine = call(own_kernel, made(1, 1), [order], cost=cost(1))(own)
+    *ringed, over = call(ring_kernel, (*made(2, 2), flag), [order], cost=cost(2))(own, m1, m3, over, other_over)
+    best, lines, hots = made(3, 1)
+    z1, near, far_best, *z1_places = call(
+        near_kernel, (part, best, jax.ShapeDtypeStruct((PACKED, 128), F32), lines, hots), [order], cost=cost(5)
+    )(own, m1, m3, z1a, z1b, z2a, mine[0], ringed[0])
     best, lines, hots = made(1, 1)
     m2, *middle, orders = call(
         middle_kernel,
-        (part, best, jax.ShapeDtypeStruct((8, 128), F32), lines, hots, jax.ShapeDtypeStruct((PACKED, 8), F32)),
+        (part, best, flag, lines, hots, jax.ShapeDtypeStruct((PACKED, 8), F32)),
         cost=cost(3),
-    )(own, m2a, m2b, z1, z2a, near[0], *first[1:])
+    )(own, m2a, m2b, z1, z2a, far_best, *z1_places)
     back = call(
         far_kernel,
         jax.ShapeDtypeStruct((512, 128), F32),
         [pltpu.VMEM((128, 128), F32)],
         cost=cost(2),
-    )(own, m1, m3, m2, z2b, *first[1:], *near, *middle, orders, over, other_over)
+    )(own, m1, m3, m2, z2b, *mine[1:], *ringed[1:], near, *middle, orders, over)
     back = lax.all_to_all(back, ("x", "z", "y"), split_axis=0, concat_axis=0, tiled=True)
     best, over = call(
         final_kernel,

time: 78 us -> 75.6 us (0.969)
  waiting for transfers between devices: 24.7 us -> 28 us
  starting transfers between devices: 31.2 us -> 28.2 us
  Pallas kernels: 20.3 us -> 17.5 us
    ppermute x11, waiting for transfers between devices: 12.9 us -> 16.1 us  [move(): return lax.ppermute(a, AXES, [(at(*p), at(*to(*p))) for p in places])]
    pallas_call x3 -> x4, Pallas kernels: 11.9 us -> 9.1 us  [the longest x1 3.89 us: fast(): call(near_kernel, (part, best, jax.ShapeDtypeStruct((PACKED, 128), F32),...]
    all_to_all x1, starting transfers between devices: 8.19 us -> 5.97 us  [fast(): lax.all_to_all(back, ('x', 'z', 'y'), split_axis=0, concat_axis=0, tiled=...]
    ppermute x11, starting transfers between devices: 22.9 us -> 22.1 us  [move(): return lax.ppermute(a, AXES, [(at(*p), at(*to(*p))) for p in places])]
  transfers between devices with their start and end apart: 14 -> 14, of which waited for: 5 -> 6; matrix products, arithmetic and copies ran while one was open for 0% -> 0% of each run, Pallas kernels for 16% -> 13%
where the time goes in v6:
time: 75.6 us; the launch traced here: 75.4 us
  starting transfers between devices  28.2 us (37%)
  waiting for transfers between devices  28 us (37%)
  Pallas kernels  17.5 us (23%)
  between operations  0.87 us (1%)
    ppermute x11, starting transfers between devices, move(): return lax.ppermute(a, AXES, [(at(*p), at(*to(*p))) for p in places])  22.1 us
    ppermute x11, waiting for transfers between devices, move(): return lax.ppermute(a, AXES, [(at(*p), at(*to(*p))) for p in places])  16.1 us
    all_to_all x1, waiting for transfers between devices, fast(): lax.all_to_all(back, ('x', 'z', 'y'), split_axis=0, concat_axis=0, tiled=...  10.5 us
    all_to_all x1, starting transfers between devices, fast(): lax.all_to_all(back, ('x', 'z', 'y'), split_axis=0, concat_axis=0, tiled=...  5.97 us
    pallas_call x1, Pallas kernels, fast(): call(near_kernel, (part, best, jax.ShapeDtypeStruct((PACKED, 128), F32),...  3.89 us
    pallas_call x1, Pallas kernels, fast(): call(prep_kernel, (blocks, jax.ShapeDtypeStruct((ROWS + 128, WIDTH), BF16...  2.8 us
    pallas_call x1, Pallas kernels, fast(): call(far_kernel, jax.ShapeDtypeStruct((512, 128), F32), [pltpu.VMEM((128,...  2.66 us
    pallas_call x1, Pallas kernels, fast(): call(middle_kernel, (part, best, flag, lines, hots, jax.ShapeDtypeStruct(...  2.32 us
  transfers between devices with their start and end apart: 14, of which 6 were waited for; matrix products, arithmetic and copies ran while one was open for 0% of the time, Pallas kernels for 13%

profile of v6, /device:TPU:0, one launch (start us, length us, event | category | flops | bytes accessed | tf_op | source)
XLA Modules:
  0.0 75.4 jit_solution(9322741816767865520)
XLA Ops:
  0.0 2.8 %shard_map.57 = (bf16[416,768]{1,0:T(8,128)(2,1)S(1)}, bf16[640,768]{1,0:T(8,128)(2,1)S(1)}, f32[8,640]{1,0:T(8,128)S(1)}) custom-call(s32[8]{0:T(128)} %assign_ref.1, bf16[512,768]{1,0:T(8,128)(2,1)} %emb_ref.1, s32[1,512]{1,0:T(1,128)} %bitcast.65, s32[1,512]{1,0:T(1,128)} %bitcast.67, s32[1,512]{1,0:T(1,128)} %bitcast.64), custom_call_target="tpu_custom_call" | custom-call | flops 1000000000 | bytes 2000000 | tf_op jit(solution)/shard_map/pallas_call | solution.py:374
  2.8 0.1 collective-permute-start.2
  2.9 0.7 shard_map.58
  3.6 1.4 %collective-permute-done.2 = bf16[416,768]{1,0:T(8,128)(2,1)S(1)} collective-permute-done((bf16[416,768]{1,0:T(8,128)(2,1)S(1)}, bf16[416,768]{1,0:T(8,128)(2,1)S(1)}, u32[]{:S(2)}, u32[]{:S(2)}) %collective-permute-start.2) | collective-permute-done | bytes 639008 | tf_op jit(solution)/shard_map/ppermute | solution.py:365
  5.0 0.1 pad_maximum_fusion
  5.1 2.9 %collective-permute-start.5 = (bf16[208,768]{1,0:T(8,128)(2,1)S(1)}, bf16[208,768]{1,0:T(8,128)(2,1)S(1)}, u32[]{:S(2)}, u32[]{:S(2)}) collective-permute-start(bf16[208,768]{1,0:T(8,128)(2,1)S(1)} %bitcast.62), channel_id=1, source_target_pairs={{0,96},{1,97},{2,98},{3,99},{4,100},{5,101},{6,102},{7,103},{8,104... | collective-permute-start | bytes 958472 | tf_op jit(solution)/shard_map/ppermute | solution.py:349
  8.0 0.0 collective-permute-start.3
  8.0 2.3 %collective-permute-start.4 = (bf16[208,768]{1,0:T(8,128)(2,1)S(1)}, bf16[208,768]{1,0:T(8,128)(2,1)S(1)}, u32[]{:S(2)}, u32[]{:S(2)}) collective-permute-start(bf16[208,768]{1,0:T(8,128)(2,1)S(1)} %bitcast.60), channel_id=1, source_target_pairs={{0,64},{1,65},{2,66},{3,67},{4,68},{5,69},{6,70},{7,71},{8,72},{9,... | collective-permute-start | bytes 958472 | tf_op jit(solution)/shard_map/ppermute | solution.py:349
  10.3 2.2 %collective-permute-done.5.from3_ref = bf16[208,768]{1,0:T(8,128)(2,1)S(1)} collective-permute-done((bf16[208,768]{1,0:T(8,128)(2,1)S(1)}, bf16[208,768]{1,0:T(8,128)(2,1)S(1)}, u32[]{:S(2)}, u32[]{:S(2)}) %collective-permute-start.5) | collective-permute-done | bytes 319520 | tf_op jit(solution)/shard_map/ppermute | solution.py:349
  12.5 7.1 %collective-permute-done.3.from1_ref = bf16[208,768]{1,0:T(8,128)(2,1)S(1)} collective-permute-done((bf16[208,768]{1,0:T(8,128)(2,1)S(1)}, bf16[208,768]{1,0:T(8,128)(2,1)S(1)}, u32[]{:S(2)}, u32[]{:S(2)}) %collective-permute-start.3) | collective-permute-done | bytes 319520 | tf_op jit(solution)/shard_map/ppermute | solution.py:349
  19.6 0.0 collective-permute-done.4.from2_ref
  19.6 1.6 %shard_map.59 = (bf16[640,768]{1,0:T(8,128)(2,1)S(1)}, bf16[320,768]{1,0:T(8,128)(2,1)S(1)}, bf16[320,768]{1,0:T(8,128)(2,1)S(1)}, f32[8,128]{1,0:T(8,128)S(1)}) custom-call(bf16[208,768]{1,0:T(8,128)(2,1)S(1)} %bitcast.51, bf16[208,768]{1,0:T(8,128)(2,1)S(1)} %collective-permute-done.3.from1_ref, bf16[208,768]{1,0:T(8,128)(2,1)S(1)} %collective-permute-done.4.from2_ref, ...), custom_call_target="tpu_custom_call" | custom-call | flops 1000000000 | bytes 2000000 | tf_op jit(solution)/shard_map/pallas_call | solution.py:390
  21.2 3.1 %collective-permute-start.7 = (bf16[640,768]{1,0:T(8,128)(2,1)S(1)}, bf16[640,768]{1,0:T(8,128)(2,1)S(1)}, u32[]{:S(2)}, u32[]{:S(2)}) collective-permute-start(bf16[640,768]{1,0:T(8,128)(2,1)S(1)} %get-tuple-element.120.own), channel_id=1, source_target_pairs={{0,3},{1,0},{2,1},{3,2},{4,7},{5,4},{6,5},{7,6},{8,11},{9,8},{10,9... | collective-permute-start | bytes 2949128 | tf_op jit(solution)/shard_map/ppermute | solution.py:349
  24.3 0.0 collective-permute-start.6
  24.3 4.0 %collective-permute-start.10 = (bf16[320,768]{1,0:T(8,128)(2,1)S(1)}, bf16[320,768]{1,0:T(8,128)(2,1)S(1)}, u32[]{:S(2)}, u32[]{:S(2)}) collective-permute-start(bf16[320,768]{1,0:T(8,128)(2,1)S(1)} %get-tuple-element.121), channel_id=1, source_target_pairs={{0,12},{1,13},{2,14},{3,15},{4,0},{5,1},{6,2},{7,3},{8,4},{9,5},{1... | collective-permute-start | bytes 1474568 | tf_op jit(solution)/shard_map/ppermute | solution.py:349
  28.3 0.4 collective-permute-start.11
  28.7 5.9 %collective-permute-done.10.z1a = bf16[320,768]{1,0:T(8,128)(2,1)S(1)} collective-permute-done((bf16[320,768]{1,0:T(8,128)(2,1)S(1)}, bf16[320,768]{1,0:T(8,128)(2,1)S(1)}, u32[]{:S(2)}, u32[]{:S(2)}) %collective-permute-start.10) | collective-permute-done | bytes 491552 | tf_op jit(solution)/shard_map/ppermute | solution.py:349
  34.6 3.7 %collective-permute-start.12 = (bf16[320,768]{1,0:T(8,128)(2,1)S(1)}, bf16[320,768]{1,0:T(8,128)(2,1)S(1)}, u32[]{:S(2)}, u32[]{:S(2)}) collective-permute-start(bf16[320,768]{1,0:T(8,128)(2,1)S(1)} %collective-permute-done.10.z1a), channel_id=1, source_target_pairs={{0,12},{1,13},{2,14},{3,15},{4,0},{5,1},{6,2},{7,3},{8,4},{9,5},{1... | collective-permute-start | bytes 1474568 | tf_op jit(solution)/shard_map/ppermute | solution.py:349
  38.3 0.0 collective-permute-done.7.m3
  38.4 3.3 %collective-permute-start.9 = (bf16[320,768]{1,0:T(8,128)(2,1)S(1)}, bf16[320,768]{1,0:T(8,128)(2,1)S(1)}, u32[]{:S(2)}, u32[]{:S(2)}) collective-permute-start(bf16[320,768]{1,0:T(8,128)(2,1)S(1)} %slice.35), channel_id=1, source_target_pairs={{0,3},{1,0},{2,1},{3,2},{4,7},{5,4},{6,5},{7,6},{8,11},{9,8},{10,9... | collective-permute-start | bytes 1474568 | tf_op jit(solution)/shard_map/ppermute | solution.py:349
  41.7 0.0 collective-permute-done.6.m1
  41.7 0.1 collective-permute-start.8
  41.8 0.1 collective-permute-start.13
  41.9 1.1 %shard_map.60 = (f32[1,8,640]{2,1,0:T(8,128)S(1)}, f32[1,8,640]{2,1,0:T(8,128)S(1)}, bf16[1,640,128]{2,1,0:T(8,128)(2,1)S(1)}) custom-call(bf16[640,768]{1,0:T(8,128)(2,1)S(1)} %get-tuple-element.120.own), custom_call_target="tpu_custom_call" | custom-call | flops 629145600 | bytes 6000000 | tf_op jit(solution)/shard_map/pallas_call | solution.py:410
  43.0 0.0 collective-permute-done.11.z1b
  43.0 2.3 %collective-permute-start.14 = (bf16[320,768]{1,0:T(8,128)(2,1)S(1)}, bf16[320,768]{1,0:T(8,128)(2,1)S(1)}, u32[]{:S(2)}, u32[]{:S(2)}) collective-permute-start(bf16[320,768]{1,0:T(8,128)(2,1)S(1)} %collective-permute-done.11.z1b), channel_id=1, source_target_pairs={{0,12},{1,13},{2,14},{3,15},{4,0},{5,1},{6,2},{7,3},{8,4},{9,5},{1... | collective-permute-start | bytes 1474568 | tf_op jit(solution)/shard_map/ppermute | solution.py:349
  45.3 0.0 collective-permute-done.13.over_b
  45.3 1.8 %shard_map.61 = (f32[2,8,640]{2,1,0:T(8,128)S(1)}, f32[2,8,640]{2,1,0:T(8,128)S(1)}, bf16[2,640,128]{2,1,0:T(8,128)(2,1)S(1)}, f32[8,128]{1,0:T(8,128)S(1)}) custom-call(bf16[640,768]{1,0:T(8,128)(2,1)S(1)} %get-tuple-element.120.own, bf16[640,768]{1,0:T(8,128)(2,1)S(1)} %collective-permute-done.6.m1, bf16[640,768]{1,0:T(8,128)(2,1)S(1)} %collective-permute-done.7.m3, ...), custom_call_target="tpu_custom_call" | custom-call | flops 1258291200 | bytes 6000000 | tf_op jit(solution)/shard_map/pallas_call | solution.py:411
  47.1 0.0 collective-permute-done.12.z2a
  47.1 3.9 %shard_map.62 = (bf16[640,768]{1,0:T(8,128)(2,1)S(1)}, f32[3,8,640]{2,1,0:T(8,128)S(1)}, f32[640,128]{1,0:T(8,128)S(1)}, f32[1,8,640]{2,1,0:T(8,128)S(1)}, bf16[1,640,128]{2,1,0:T(8,128)(2,1)S(1)}) custom-call(bf16[640,768]{1,0:T(8,128)(2,1)S(1)} %get-tuple-element.120.own, bf16[640,768]{1,0:T(8,128)(2,1)S(1)} %collective-permute-done.6.m1, ...), custom_call_target="tpu_custom_call" | custom-call | flops 3145728000 | bytes 6000000 | tf_op jit(solution)/shard_map/pallas_call | solution.py:413
  51.0 0.0 collective-permute-done.9.m2b
  51.0 0.8 %collective-permute-done.8.m2a = bf16[320,768]{1,0:T(8,128)(2,1)S(1)} collective-permute-done((bf16[320,768]{1,0:T(8,128)(2,1)S(1)}, bf16[320,768]{1,0:T(8,128)(2,1)S(1)}, u32[]{:S(2)}, u32[]{:S(2)}) %collective-permute-start.8) | collective-permute-done | bytes 491552 | tf_op jit(solution)/shard_map/ppermute | solution.py:349
  51.8 2.3 %shard_map.63 = (bf16[640,768]{1,0:T(8,128)(2,1)S(1)}, f32[1,8,640]{2,1,0:T(8,128)S(1)}, f32[8,128]{1,0:T(8,128)S(1)}, f32[1,8,640]{2,1,0:T(8,128)S(1)}, bf16[1,...) custom-call(bf16[640,768]{1,0:T(8,128)(2,1)S(1)} %get-tuple-element.120.own, ...), custom_call_target="tpu_custom_call" | custom-call | flops 1887436800 | bytes 6000000 | tf_op jit(solution)/shard_map/pallas_call | solution.py:417
  54.2 0.0 collective-permute-done.14.z2b
  54.2 0.0 copy-start
  54.2 0.0 copy-start.2
  54.2 0.0 copy-start.3
  54.2 0.0 copy-start.4
  54.2 2.7 %shard_map.64 = f32[512,128]{1,0:T(8,128)} custom-call(bf16[640,768]{1,0:T(8,128)(2,1)S(1)} %get-tuple-element.120.own, bf16[640,768]{1,0:T(8,128)(2,1)S(1)} %collective-permute-done.6.m1, bf16[640,768]{1,0:T(8,128)(2,1)S(1)} %collective-permute-done.7.m3, bf16[640,768]{1,0:T(8,128)(2,1)S(1)} %get-tuple-element.130.m2, ...), custom_call_target="tpu_custom_call" | custom-call | flops 1258291200 | bytes 6000000 | tf_op jit(solution)/shard_map/pallas_call | solution.py:422
  56.9 6.0 %all-to-all-start.2 = ((f32[64,8,128]{2,1,0:T(8,128)}), f32[64,8,128]{2,1,0:T(8,128)S(1)}, u32[]{:S(2)}, u32[]{:S(2)}) async-start(f32[64,8,128]{2,1,0:T(8,128)} %bitcast.18), calls=%async_computation.2 | async-start | bytes 524288 | tf_op jit(solution)/shard_map/all_to_all | solution.py:428
  62.9 10.5 %all-to-all-done.2 = f32[64,8,128]{2,1,0:T(8,128)S(1)} async-done(((f32[64,8,128]{2,1,0:T(8,128)}), f32[64,8,128]{2,1,0:T(8,128)S(1)}, u32[]{:S(2)}, u32[]{:S(2)}) %all-to-all-start.2) | async-done | bytes 262176 | tf_op jit(solution)/shard_map/all_to_all | solution.py:428
  73.3 0.7 shard_map.65
  74.7 0.0 copy-done
  74.7 0.0 copy-done.2
  74.7 0.0 copy-done.3
  74.8 0.0 copy-done.4
  74.8 0.0 copy-start.5
  74.8 0.6 copy-done.5
  (3 shorter events, 0.1 us)
Async XLA Ops:
  2.8 2.2 %collective-permute-start.2 = (bf16[416,768]{1,0:T(8,128)(2,1)S(1)}, bf16[416,768]{1,0:T(8,128)(2,1)S(1)}, u32[]{:S(2)}, u32[]{:S(2)}) collective-permute-start(bf16[416,768]{1,0:T(8,128)(2,1)S(1)} %get-tuple-element.119), channel_id=1, source_target_pairs={{0,16},{16,0},{1,17},{17,1},{2,18},{18,2},{3,19},{19,3},{4,20},{20... | collective-permute-start | bytes 1916936 | tf_op jit(solution)/shard_map/ppermute | solution.py:365
  5.1 7.4 %collective-permute-start.5 = (bf16[208,768]{1,0:T(8,128)(2,1)S(1)}, bf16[208,768]{1,0:T(8,128)(2,1)S(1)}, u32[]{:S(2)}, u32[]{:S(2)}) collective-permute-start(bf16[208,768]{1,0:T(8,128)(2,1)S(1)} %bitcast.62), channel_id=1, source_target_pairs={{0,96},{1,97},{2,98},{3,99},{4,100},{5,101},{6,102},{7,103},{8,104... | collective-permute-start | bytes 958472 | tf_op jit(solution)/shard_map/ppermute | solution.py:349
  8.0 11.6 %collective-permute-start.3 = (bf16[208,768]{1,0:T(8,128)(2,1)S(1)}, bf16[208,768]{1,0:T(8,128)(2,1)S(1)}, u32[]{:S(2)}, u32[]{:S(2)}) collective-permute-start(bf16[208,768]{1,0:T(8,128)(2,1)S(1)} %bitcast.61), channel_id=1, source_target_pairs={{0,32},{1,33},{2,34},{3,35},{4,36},{5,37},{6,38},{7,39},{8,40},{9,... | collective-permute-start | bytes 958472 | tf_op jit(solution)/shard_map/ppermute | solution.py:349
  8.0 11.6 %collective-permute-start.4 = (bf16[208,768]{1,0:T(8,128)(2,1)S(1)}, bf16[208,768]{1,0:T(8,128)(2,1)S(1)}, u32[]{:S(2)}, u32[]{:S(2)}) collective-permute-start(bf16[208,768]{1,0:T(8,128)(2,1)S(1)} %bitcast.60), channel_id=1, source_target_pairs={{0,64},{1,65},{2,66},{3,67},{4,68},{5,69},{6,70},{7,71},{8,72},{9,... | collective-permute-start | bytes 958472 | tf_op jit(solution)/shard_map/ppermute | solution.py:349
  21.2 17.2 %collective-permute-start.7 = (bf16[640,768]{1,0:T(8,128)(2,1)S(1)}, bf16[640,768]{1,0:T(8,128)(2,1)S(1)}, u32[]{:S(2)}, u32[]{:S(2)}) collective-permute-start(bf16[640,768]{1,0:T(8,128)(2,1)S(1)} %get-tuple-element.120.own), channel_id=1, source_target_pairs={{0,3},{1,0},{2,1},{3,2},{4,7},{5,4},{6,5},{7,6},{8,11},{9,8},{10,9... | collective-permute-start | bytes 2949128 | tf_op jit(solution)/shard_map/ppermute | solution.py:349
  24.3 17.4 %collective-permute-start.6 = (bf16[640,768]{1,0:T(8,128)(2,1)S(1)}, bf16[640,768]{1,0:T(8,128)(2,1)S(1)}, u32[]{:S(2)}, u32[]{:S(2)}) collective-permute-start(bf16[640,768]{1,0:T(8,128)(2,1)S(1)} %get-tuple-element.120.own), channel_id=1, source_target_pairs={{0,1},{1,2},{2,3},{3,0},{4,5},{5,6},{6,7},{7,4},{8,9},{9,10},{10,1... | collective-permute-start | bytes 2949128 | tf_op jit(solution)/shard_map/ppermute | solution.py:349
  24.3 10.4 %collective-permute-start.10 = (bf16[320,768]{1,0:T(8,128)(2,1)S(1)}, bf16[320,768]{1,0:T(8,128)(2,1)S(1)}, u32[]{:S(2)}, u32[]{:S(2)}) collective-permute-start(bf16[320,768]{1,0:T(8,128)(2,1)S(1)} %get-tuple-element.121), channel_id=1, source_target_pairs={{0,12},{1,13},{2,14},{3,15},{4,0},{5,1},{6,2},{7,3},{8,4},{9,5},{1... | collective-permute-start | bytes 1474568 | tf_op jit(solution)/shard_map/ppermute | solution.py:349
  28.3 14.7 %collective-permute-start.11 = (bf16[320,768]{1,0:T(8,128)(2,1)S(1)}, bf16[320,768]{1,0:T(8,128)(2,1)S(1)}, u32[]{:S(2)}, u32[]{:S(2)}) collective-permute-start(bf16[320,768]{1,0:T(8,128)(2,1)S(1)} %get-tuple-element.122), channel_id=1, source_target_pairs={{0,12},{1,13},{2,14},{3,15},{4,0},{5,1},{6,2},{7,3},{8,4},{9,5},{1... | collective-permute-start | bytes 1474568 | tf_op jit(solution)/shard_map/ppermute | solution.py:349
  34.6 12.4 %collective-permute-start.12 = (bf16[320,768]{1,0:T(8,128)(2,1)S(1)}, bf16[320,768]{1,0:T(8,128)(2,1)S(1)}, u32[]{:S(2)}, u32[]{:S(2)}) collective-permute-start(bf16[320,768]{1,0:T(8,128)(2,1)S(1)} %collective-permute-done.10.z1a), channel_id=1, source_target_pairs={{0,12},{1,13},{2,14},{3,15},{4,0},{5,1},{6,2},{7,3},{8,4},{9,5},{1... | collective-permute-start | bytes 1474568 | tf_op jit(solution)/shard_map/ppermute | solution.py:349
  38.4 12.6 %collective-permute-start.9 = (bf16[320,768]{1,0:T(8,128)(2,1)S(1)}, bf16[320,768]{1,0:T(8,128)(2,1)S(1)}, u32[]{:S(2)}, u32[]{:S(2)}) collective-permute-start(bf16[320,768]{1,0:T(8,128)(2,1)S(1)} %slice.35), channel_id=1, source_target_pairs={{0,3},{1,0},{2,1},{3,2},{4,7},{5,4},{6,5},{7,6},{8,11},{9,8},{10,9... | collective-permute-start | bytes 1474568 | tf_op jit(solution)/shard_map/ppermute | solution.py:349
  41.7 10.1 %collective-permute-start.8 = (bf16[320,768]{1,0:T(8,128)(2,1)S(1)}, bf16[320,768]{1,0:T(8,128)(2,1)S(1)}, u32[]{:S(2)}, u32[]{:S(2)}) collective-permute-start(bf16[320,768]{1,0:T(8,128)(2,1)S(1)} %slice.34), channel_id=1, source_target_pairs={{0,1},{1,2},{2,3},{3,0},{4,5},{5,6},{6,7},{7,4},{8,9},{9,10},{10,1... | collective-permute-start | bytes 1474568 | tf_op jit(solution)/shard_map/ppermute | solution.py:349
  41.8 3.5 %collective-permute-start.13 = (f32[8,128]{1,0:T(8,128)S(1)}, f32[8,128]{1,0:T(8,128)S(1)}, u32[]{:S(2)}, u32[]{:S(2)}) collective-permute-start(f32[8,128]{1,0:T(8,128)S(1)} %get-tuple-element.124.over_a), channel_id=1, source_target_pairs={{0,16},{16,0},{1,17},{17,1},{2,18},{18,2},{3,19},{19,3},{4,20},{20... | collective-permute-start | bytes 12296 | tf_op jit(solution)/shard_map/ppermute | solution.py:365
  43.0 11.2 %collective-permute-start.14 = (bf16[320,768]{1,0:T(8,128)(2,1)S(1)}, bf16[320,768]{1,0:T(8,128)(2,1)S(1)}, u32[]{:S(2)}, u32[]{:S(2)}) collective-permute-start(bf16[320,768]{1,0:T(8,128)(2,1)S(1)} %collective-permute-done.11.z1b), channel_id=1, source_target_pairs={{0,12},{1,13},{2,14},{3,15},{4,0},{5,1},{6,2},{7,3},{8,4},{9,5},{1... | collective-permute-start | bytes 1474568 | tf_op jit(solution)/shard_map/ppermute | solution.py:349
  54.2 20.6 %copy-start = (bf16[512,768]{1,0:T(8,128)(2,1)S(1)}, bf16[512,768]{1,0:T(8,128)(2,1)}, u32[]{:S(2)}) copy-start(bf16[512,768]{1,0:T(8,128)(2,1)} %emb_ref.1) | copy-start | bytes 2359300
  54.2 20.6 %copy-start.2 = (s32[512]{0:T(512)S(1)}, s32[512]{0:T(512)}, u32[]{:S(2)}) copy-start(s32[512]{0:T(512)} %param.15) | copy-start | bytes 6148
  54.2 20.6 %copy-start.3 = (s32[512]{0:T(512)S(1)}, s32[512]{0:T(512)}, u32[]{:S(2)}) copy-start(s32[512]{0:T(512)} %param.12) | copy-start | bytes 6148
  54.2 20.6 %copy-start.4 = (s32[8]{0:T(128)S(1)}, s32[8]{0:T(128)}, u32[]{:S(2)}) copy-start(s32[8]{0:T(128)} %assign_ref.1) | copy-start | bytes 100
  56.9 16.5 %all-to-all-start.2 = ((f32[64,8,128]{2,1,0:T(8,128)}), f32[64,8,128]{2,1,0:T(8,128)S(1)}, u32[]{:S(2)}, u32[]{:S(2)}) async-start(f32[64,8,128]{2,1,0:T(8,128)} %bitcast.18), calls=%async_computation.2 | async-start | bytes 524288 | tf_op jit(solution)/shard_map/all_to_all | solution.py:428
  74.8 0.6 copy-start.5

commit v7 on v6

--- a/solution.py
+++ b/solution.py
@@ -109,7 +109,7 @@
     same_ref[...] = mul(placing, both_ref[...]).astype(BF16)
 
 
-def pack_kernel(here_ref, from1_ref, from2_ref, from3_ref, out_ref, low_ref, high_ref, over_ref, in_ref):
+def pack_kernel(here_ref, from1_ref, from3_ref, from2_ref, out_ref, low_ref, high_ref, over_ref, in_ref):
     count = KINDS * BLOCK
     for k, ref in enumerate((here_ref, from1_ref, from2_ref, from3_ref)):
         in_ref[k * 2 * BLOCK : (k + 1) * 2 * BLOCK, :] = ref[...]
@@ -222,6 +222,10 @@
     owner_lines(numbers_of(own), lines_ref, hot_ref, 0)
 
 
+def pass_kernel(part, own_best, out_ref):
+    out_ref[...] = part[...]
+
+
 def ring_kernel(own, m1, m3, over_a, over_b, best_ref, lines_ref, hot_ref, over_ref, order_ref):
     order_ref[...] = orders_down(own)
     for i, rows in enumerate((m1, m3)):
@@ -385,6 +389,7 @@
     same = call(same_kernel, blocks, cost=cheap)(pool, target)
     shape = (4, 1, BLOCK, WIDTH)
     both = jnp.concatenate([same.reshape(shape), other.reshape(shape)], axis=1).reshape(4, 2 * BLOCK, WIDTH)
+    arrived = [across(both[k], k) for k in (2, 1, 3)]
     piece = jax.ShapeDtypeStruct((HALF, WIDTH), BF16)
     part = jax.ShapeDtypeStruct((PACKED, WIDTH), BF16)
     own, low, high, over = call(
@@ -392,11 +397,11 @@
         (part, piece, piece, jax.ShapeDtypeStruct((8, 128), F32)),
         [pltpu.VMEM((KINDS * BLOCK, WIDTH), BF16)],
         cost=cheap,
-    )(both[0], *[across(both[k], k) for k in (1, 2, 3)])
+    )(both[0], *arrived[1:], arrived[0])
     z1a, z1b = down(low), down(high)
     m1, m3 = along(own, 1), along(own, -1)
     other_over = core_swap(over)
-    z2a, z2b = down(z1a), down(z1b)
+    z2b = down(z1b)
     m2a, m2b = along(m1[:HALF], 1), along(m3[HALF:], -1)
     product = 2 * PACKED * PACKED * WIDTH
     cost = lambda n: pl.CostEstimate(flops=n * product, bytes_accessed=6 * 10**6, transcendentals=0)
@@ -408,6 +413,7 @@
     )
     flag = jax.ShapeDtypeStruct((8, 128), F32)
     mine = call(own_kernel, made(1, 1), [order], cost=cost(1))(own)
+    z2a = down(call(pass_kernel, piece)(z1a, mine[0]))
     *ringed, over = call(ring_kernel, (*made(2, 2), flag), [order], cost=cost(2))(own, m1, m3, over, other_over)
     best, lines, hots = made(3, 1)
     z1, near, far_best, *z1_places = call(

time: 75.6 us -> 75.2 us (level)
  waiting for transfers between devices: 28 us -> 24.5 us
  starting transfers between devices: 28.2 us -> 31.3 us
    ppermute x11, waiting for transfers between devices: 16.1 us -> 12.7 us  [move(): return lax.ppermute(a, AXES, [(at(*p), at(*to(*p))) for p in places])]
    all_to_all x1, starting transfers between devices: 5.97 us -> 7.89 us  [fast(): lax.all_to_all(back, ('x', 'z', 'y'), split_axis=0, concat_axis=0, tiled=...]
    ppermute x11, starting transfers between devices: 22.1 us -> 23.3 us  [move(): return lax.ppermute(a, AXES, [(at(*p), at(*to(*p))) for p in places])]
  transfers between devices with their start and end apart: 14 -> 14, of which waited for: 6 -> 7; matrix products, arithmetic and copies ran while one was open for 0% -> 0% of each run, Pallas kernels for 13% -> 13%
where the time goes in v7:
time: 75.2 us; the launch traced here: 75 us
  starting transfers between devices  31.3 us (42%)
  waiting for transfers between devices  24.5 us (33%)
  Pallas kernels  17.5 us (23%)
  between operations  0.88 us (1%)
    ppermute x11, starting transfers between devices, move(): return lax.ppermute(a, AXES, [(at(*p), at(*to(*p))) for p in places])  23.3 us
    ppermute x11, waiting for transfers between devices, move(): return lax.ppermute(a, AXES, [(at(*p), at(*to(*p))) for p in places])  12.7 us
    all_to_all x1, waiting for transfers between devices, fast(): lax.all_to_all(back, ('x', 'z', 'y'), split_axis=0, concat_axis=0, tiled=...  10.4 us
    all_to_all x1, starting transfers between devices, fast(): lax.all_to_all(back, ('x', 'z', 'y'), split_axis=0, concat_axis=0, tiled=...  7.89 us
    pallas_call x1, Pallas kernels, fast(): call(near_kernel, (part, best, jax.ShapeDtypeStruct((PACKED, 128), F32),...  3.85 us
    pallas_call x1, Pallas kernels, fast(): call(prep_kernel, (blocks, jax.ShapeDtypeStruct((ROWS + 128, WIDTH), BF16...  2.8 us
    pallas_call x1, Pallas kernels, fast(): call(far_kernel, jax.ShapeDtypeStruct((512, 128), F32), [pltpu.VMEM((128,...  2.66 us
    pallas_call x1, Pallas kernels, fast(): call(middle_kernel, (part, best, flag, lines, hots, jax.ShapeDtypeStruct(...  2.3 us
  transfers between devices with their start and end apart: 14, of which 7 were waited for; matrix products, arithmetic and copies ran while one was open for 0% of the time, Pallas kernels for 13%

profile of v7, /device:TPU:0, one launch (start us, length us, event | category | flops | bytes accessed | tf_op | source)
XLA Modules:
  0.0 75.0 jit_solution(11232597091742624465)
XLA Ops:
  0.0 2.8 %shard_map.57 = (bf16[416,768]{1,0:T(8,128)(2,1)S(1)}, bf16[640,768]{1,0:T(8,128)(2,1)S(1)}, f32[8,640]{1,0:T(8,128)S(1)}) custom-call(s32[8]{0:T(128)} %assign_ref.1, bf16[512,768]{1,0:T(8,128)(2,1)} %emb_ref.1, s32[1,512]{1,0:T(1,128)} %bitcast.65, s32[1,512]{1,0:T(1,128)} %bitcast.67, s32[1,512]{1,0:T(1,128)} %bitcast.64), custom_call_target="tpu_custom_call" | custom-call | flops 1000000000 | bytes 2000000 | tf_op jit(solution)/shard_map/pallas_call | solution.py:378
  2.8 0.1 collective-permute-start.2
  2.9 0.7 shard_map.58
  3.6 1.4 %collective-permute-done.2 = bf16[416,768]{1,0:T(8,128)(2,1)S(1)} collective-permute-done((bf16[416,768]{1,0:T(8,128)(2,1)S(1)}, bf16[416,768]{1,0:T(8,128)(2,1)S(1)}, u32[]{:S(2)}, u32[]{:S(2)}) %collective-permute-start.2) | collective-permute-done | bytes 639008 | tf_op jit(solution)/shard_map/ppermute | solution.py:369
  5.0 0.1 pad_maximum_fusion
  5.1 3.2 %collective-permute-start.5 = (bf16[208,768]{1,0:T(8,128)(2,1)S(1)}, bf16[208,768]{1,0:T(8,128)(2,1)S(1)}, u32[]{:S(2)}, u32[]{:S(2)}) collective-permute-start(bf16[208,768]{1,0:T(8,128)(2,1)S(1)} %bitcast.62), channel_id=1, source_target_pairs={{0,64},{1,65},{2,66},{3,67},{4,68},{5,69},{6,70},{7,71},{8,72},{9,... | collective-permute-start | bytes 958472 | tf_op jit(solution)/shard_map/ppermute | solution.py:353
  8.3 0.6 collective-permute-start.3
  8.9 2.6 %collective-permute-start.4 = (bf16[208,768]{1,0:T(8,128)(2,1)S(1)}, bf16[208,768]{1,0:T(8,128)(2,1)S(1)}, u32[]{:S(2)}, u32[]{:S(2)}) collective-permute-start(bf16[208,768]{1,0:T(8,128)(2,1)S(1)} %bitcast.60), channel_id=1, source_target_pairs={{0,96},{1,97},{2,98},{3,99},{4,100},{5,101},{6,102},{7,103},{8,104... | collective-permute-start | bytes 958472 | tf_op jit(solution)/shard_map/ppermute | solution.py:353
  11.5 2.2 %collective-permute-done.5.from2_ref = bf16[208,768]{1,0:T(8,128)(2,1)S(1)} collective-permute-done((bf16[208,768]{1,0:T(8,128)(2,1)S(1)}, bf16[208,768]{1,0:T(8,128)(2,1)S(1)}, u32[]{:S(2)}, u32[]{:S(2)}) %collective-permute-start.5) | collective-permute-done | bytes 319520 | tf_op jit(solution)/shard_map/ppermute | solution.py:353
  13.7 3.4 %collective-permute-done.3.from1_ref = bf16[208,768]{1,0:T(8,128)(2,1)S(1)} collective-permute-done((bf16[208,768]{1,0:T(8,128)(2,1)S(1)}, bf16[208,768]{1,0:T(8,128)(2,1)S(1)}, u32[]{:S(2)}, u32[]{:S(2)}) %collective-permute-start.3) | collective-permute-done | bytes 319520 | tf_op jit(solution)/shard_map/ppermute | solution.py:353
  17.1 0.2 collective-permute-done.4.from3_ref
  17.2 1.6 %shard_map.59 = (bf16[640,768]{1,0:T(8,128)(2,1)S(1)}, bf16[320,768]{1,0:T(8,128)(2,1)S(1)}, bf16[320,768]{1,0:T(8,128)(2,1)S(1)}, f32[8,128]{1,0:T(8,128)S(1)}) custom-call(bf16[208,768]{1,0:T(8,128)(2,1)S(1)} %bitcast.51, bf16[208,768]{1,0:T(8,128)(2,1)S(1)} %collective-permute-done.3.from1_ref, bf16[208,768]{1,0:T(8,128)(2,1)S(1)} %collective-permute-done.4.from3_ref, ...), custom_call_target="tpu_custom_call" | custom-call | flops 1000000000 | bytes 2000000 | tf_op jit(solution)/shard_map/pallas_call | solution.py:395
  18.8 3.1 %collective-permute-start.7 = (bf16[640,768]{1,0:T(8,128)(2,1)S(1)}, bf16[640,768]{1,0:T(8,128)(2,1)S(1)}, u32[]{:S(2)}, u32[]{:S(2)}) collective-permute-start(bf16[640,768]{1,0:T(8,128)(2,1)S(1)} %get-tuple-element.120.own), channel_id=1, source_target_pairs={{0,3},{1,0},{2,1},{3,2},{4,7},{5,4},{6,5},{7,6},{8,11},{9,8},{10,9... | collective-permute-start | bytes 2949128 | tf_op jit(solution)/shard_map/ppermute | solution.py:353
  21.9 0.0 collective-permute-start.6
  21.9 4.0 %collective-permute-start.10 = (bf16[320,768]{1,0:T(8,128)(2,1)S(1)}, bf16[320,768]{1,0:T(8,128)(2,1)S(1)}, u32[]{:S(2)}, u32[]{:S(2)}) collective-permute-start(bf16[320,768]{1,0:T(8,128)(2,1)S(1)} %get-tuple-element.121), channel_id=1, source_target_pairs={{0,12},{1,13},{2,14},{3,15},{4,0},{5,1},{6,2},{7,3},{8,4},{9,5},{1... | collective-permute-start | bytes 1474568 | tf_op jit(solution)/shard_map/ppermute | solution.py:353
  25.9 0.4 collective-permute-start.11
  26.3 1.1 %shard_map.60 = (f32[1,8,640]{2,1,0:T(8,128)S(1)}, f32[1,8,640]{2,1,0:T(8,128)S(1)}, bf16[1,640,128]{2,1,0:T(8,128)(2,1)S(1)}) custom-call(bf16[640,768]{1,0:T(8,128)(2,1)S(1)} %get-tuple-element.120.own), custom_call_target="tpu_custom_call" | custom-call | flops 629145600 | bytes 6000000 | tf_op jit(solution)/shard_map/pallas_call | solution.py:415
  27.4 4.8 %collective-permute-done.10.part.z1a = bf16[320,768]{1,0:T(8,128)(2,1)S(1)} collective-permute-done((bf16[320,768]{1,0:T(8,128)(2,1)S(1)}, bf16[320,768]{1,0:T(8,128)(2,1)S(1)}, u32[]{:S(2)}, u32[]{:S(2)}) %collective-permute-start.10) | collective-permute-done | bytes 491552 | tf_op jit(solution)/shard_map/ppermute | solution.py:353
  32.3 3.8 %collective-permute-start.12 = (bf16[320,768]{1,0:T(8,128)(2,1)S(1)}, bf16[320,768]{1,0:T(8,128)(2,1)S(1)}, u32[]{:S(2)}, u32[]{:S(2)}) collective-permute-start(bf16[320,768]{1,0:T(8,128)(2,1)S(1)} %shard_map.61), channel_id=1, source_target_pairs={{0,12},{1,13},{2,14},{3,15},{4,0},{5,1},{6,2},{7,3},{8,4},{9,5},{1... | collective-permute-start | bytes 1474568 | tf_op jit(solution)/shard_map/ppermute | solution.py:353
  36.1 0.0 collective-permute-done.7.m3
  36.1 3.3 %collective-permute-start.9 = (bf16[320,768]{1,0:T(8,128)(2,1)S(1)}, bf16[320,768]{1,0:T(8,128)(2,1)S(1)}, u32[]{:S(2)}, u32[]{:S(2)}) collective-permute-start(bf16[320,768]{1,0:T(8,128)(2,1)S(1)} %slice.35), channel_id=1, source_target_pairs={{0,3},{1,0},{2,1},{3,2},{4,7},{5,4},{6,5},{7,6},{8,11},{9,8},{10,9... | collective-permute-start | bytes 1474568 | tf_op jit(solution)/shard_map/ppermute | solution.py:353
  39.4 0.0 collective-permute-done.6.m1
  39.5 0.1 collective-permute-start.8
  39.5 0.1 collective-permute-start.13
  39.6 0.0 collective-permute-done.11.z1b
  39.6 2.2 %collective-permute-start.14 = (bf16[320,768]{1,0:T(8,128)(2,1)S(1)}, bf16[320,768]{1,0:T(8,128)(2,1)S(1)}, u32[]{:S(2)}, u32[]{:S(2)}) collective-permute-start(bf16[320,768]{1,0:T(8,128)(2,1)S(1)} %collective-permute-done.11.z1b), channel_id=1, source_target_pairs={{0,12},{1,13},{2,14},{3,15},{4,0},{5,1},{6,2},{7,3},{8,4},{9,5},{1... | collective-permute-start | bytes 1474568 | tf_op jit(solution)/shard_map/ppermute | solution.py:353
  41.8 0.0 collective-permute-done.13.over_b
  41.8 1.8 %shard_map.62 = (f32[2,8,640]{2,1,0:T(8,128)S(1)}, f32[2,8,640]{2,1,0:T(8,128)S(1)}, bf16[2,640,128]{2,1,0:T(8,128)(2,1)S(1)}, f32[8,128]{1,0:T(8,128)S(1)}) custom-call(bf16[640,768]{1,0:T(8,128)(2,1)S(1)} %get-tuple-element.120.own, bf16[640,768]{1,0:T(8,128)(2,1)S(1)} %collective-permute-done.6.m1, bf16[640,768]{1,0:T(8,128)(2,1)S(1)} %collective-permute-done.7.m3, ...), custom_call_target="tpu_custom_call" | custom-call | flops 1258291200 | bytes 6000000 | tf_op jit(solution)/shard_map/pallas_call | solution.py:417
  43.6 0.0 collective-permute-done.12.z2a
  43.6 3.9 %shard_map.63 = (bf16[640,768]{1,0:T(8,128)(2,1)S(1)}, f32[3,8,640]{2,1,0:T(8,128)S(1)}, f32[640,128]{1,0:T(8,128)S(1)}, f32[1,8,640]{2,1,0:T(8,128)S(1)}, bf16[1,640,128]{2,1,0:T(8,128)(2,1)S(1)}) custom-call(bf16[640,768]{1,0:T(8,128)(2,1)S(1)} %get-tuple-element.120.own, bf16[640,768]{1,0:T(8,128)(2,1)S(1)} %collective-permute-done.6.m1, ...), custom_call_target="tpu_custom_call" | custom-call | flops 3145728000 | bytes 6000000 | tf_op jit(solution)/shard_map/pallas_call | solution.py:419
  47.5 0.0 collective-permute-done.9.m2b
  47.5 2.1 %collective-permute-done.8.m2a = bf16[320,768]{1,0:T(8,128)(2,1)S(1)} collective-permute-done((bf16[320,768]{1,0:T(8,128)(2,1)S(1)}, bf16[320,768]{1,0:T(8,128)(2,1)S(1)}, u32[]{:S(2)}, u32[]{:S(2)}) %collective-permute-start.8) | collective-permute-done | bytes 491552 | tf_op jit(solution)/shard_map/ppermute | solution.py:353
  49.6 2.3 %shard_map.64 = (bf16[640,768]{1,0:T(8,128)(2,1)S(1)}, f32[1,8,640]{2,1,0:T(8,128)S(1)}, f32[8,128]{1,0:T(8,128)S(1)}, f32[1,8,640]{2,1,0:T(8,128)S(1)}, bf16[1,...) custom-call(bf16[640,768]{1,0:T(8,128)(2,1)S(1)} %get-tuple-element.120.own, ...), custom_call_target="tpu_custom_call" | custom-call | flops 1887436800 | bytes 6000000 | tf_op jit(solution)/shard_map/pallas_call | solution.py:423
  51.9 0.0 collective-permute-done.14.z2b
  51.9 0.0 copy-start
  51.9 0.0 copy-start.2
  51.9 0.0 copy-start.3
  51.9 0.0 copy-start.4
  51.9 2.7 %shard_map.65 = f32[512,128]{1,0:T(8,128)} custom-call(bf16[640,768]{1,0:T(8,128)(2,1)S(1)} %get-tuple-element.120.own, bf16[640,768]{1,0:T(8,128)(2,1)S(1)} %collective-permute-done.6.m1, bf16[640,768]{1,0:T(8,128)(2,1)S(1)} %collective-permute-done.7.m3, bf16[640,768]{1,0:T(8,128)(2,1)S(1)} %get-tuple-element.130.m2, ...), custom_call_target="tpu_custom_call" | custom-call | flops 1258291200 | bytes 6000000 | tf_op jit(solution)/shard_map/pallas_call | solution.py:428
  54.6 7.9 %all-to-all-start.2 = ((f32[64,8,128]{2,1,0:T(8,128)}), f32[64,8,128]{2,1,0:T(8,128)S(1)}, u32[]{:S(2)}, u32[]{:S(2)}) async-start(f32[64,8,128]{2,1,0:T(8,128)} %bitcast.18), calls=%async_computation.2 | async-start | bytes 524288 | tf_op jit(solution)/shard_map/all_to_all | solution.py:434
  62.5 10.4 %all-to-all-done.2 = f32[64,8,128]{2,1,0:T(8,128)S(1)} async-done(((f32[64,8,128]{2,1,0:T(8,128)}), f32[64,8,128]{2,1,0:T(8,128)S(1)}, u32[]{:S(2)}, u32[]{:S(2)}) %all-to-all-start.2) | async-done | bytes 262176 | tf_op jit(solution)/shard_map/all_to_all | solution.py:434
  72.9 0.7 shard_map.66
  74.3 0.0 copy-done
  74.3 0.0 copy-done.2
  74.3 0.0 copy-done.3
  74.3 0.0 copy-done.4
  74.4 0.0 copy-start.5
  74.4 0.6 copy-done.5
  (4 shorter events, 0.1 us)
Async XLA Ops:
  2.8 2.2 %collective-permute-start.2 = (bf16[416,768]{1,0:T(8,128)(2,1)S(1)}, bf16[416,768]{1,0:T(8,128)(2,1)S(1)}, u32[]{:S(2)}, u32[]{:S(2)}) collective-permute-start(bf16[416,768]{1,0:T(8,128)(2,1)S(1)} %get-tuple-element.119), channel_id=1, source_target_pairs={{0,16},{16,0},{1,17},{17,1},{2,18},{18,2},{3,19},{19,3},{4,20},{20... | collective-permute-start | bytes 1916936 | tf_op jit(solution)/shard_map/ppermute | solution.py:369
  5.1 8.6 %collective-permute-start.5 = (bf16[208,768]{1,0:T(8,128)(2,1)S(1)}, bf16[208,768]{1,0:T(8,128)(2,1)S(1)}, u32[]{:S(2)}, u32[]{:S(2)}) collective-permute-start(bf16[208,768]{1,0:T(8,128)(2,1)S(1)} %bitcast.62), channel_id=1, source_target_pairs={{0,64},{1,65},{2,66},{3,67},{4,68},{5,69},{6,70},{7,71},{8,72},{9,... | collective-permute-start | bytes 958472 | tf_op jit(solution)/shard_map/ppermute | solution.py:353
  8.3 8.8 %collective-permute-start.3 = (bf16[208,768]{1,0:T(8,128)(2,1)S(1)}, bf16[208,768]{1,0:T(8,128)(2,1)S(1)}, u32[]{:S(2)}, u32[]{:S(2)}) collective-permute-start(bf16[208,768]{1,0:T(8,128)(2,1)S(1)} %bitcast.61), channel_id=1, source_target_pairs={{0,32},{1,33},{2,34},{3,35},{4,36},{5,37},{6,38},{7,39},{8,40},{9,... | collective-permute-start | bytes 958472 | tf_op jit(solution)/shard_map/ppermute | solution.py:353
  8.9 8.4 %collective-permute-start.4 = (bf16[208,768]{1,0:T(8,128)(2,1)S(1)}, bf16[208,768]{1,0:T(8,128)(2,1)S(1)}, u32[]{:S(2)}, u32[]{:S(2)}) collective-permute-start(bf16[208,768]{1,0:T(8,128)(2,1)S(1)} %bitcast.60), channel_id=1, source_target_pairs={{0,96},{1,97},{2,98},{3,99},{4,100},{5,101},{6,102},{7,103},{8,104... | collective-permute-start | bytes 958472 | tf_op jit(solution)/shard_map/ppermute | solution.py:353
  18.8 17.3 %collective-permute-start.7 = (bf16[640,768]{1,0:T(8,128)(2,1)S(1)}, bf16[640,768]{1,0:T(8,128)(2,1)S(1)}, u32[]{:S(2)}, u32[]{:S(2)}) collective-permute-start(bf16[640,768]{1,0:T(8,128)(2,1)S(1)} %get-tuple-element.120.own), channel_id=1, source_target_pairs={{0,3},{1,0},{2,1},{3,2},{4,7},{5,4},{6,5},{7,6},{8,11},{9,8},{10,9... | collective-permute-start | bytes 2949128 | tf_op jit(solution)/shard_map/ppermute | solution.py:353
  21.9 17.5 %collective-permute-start.6 = (bf16[640,768]{1,0:T(8,128)(2,1)S(1)}, bf16[640,768]{1,0:T(8,128)(2,1)S(1)}, u32[]{:S(2)}, u32[]{:S(2)}) collective-permute-start(bf16[640,768]{1,0:T(8,128)(2,1)S(1)} %get-tuple-element.120.own), channel_id=1, source_target_pairs={{0,1},{1,2},{2,3},{3,0},{4,5},{5,6},{6,7},{7,4},{8,9},{9,10},{10,1... | collective-permute-start | bytes 2949128 | tf_op jit(solution)/shard_map/ppermute | solution.py:353
  21.9 10.4 %collective-permute-start.10 = (bf16[320,768]{1,0:T(8,128)(2,1)S(1)}, bf16[320,768]{1,0:T(8,128)(2,1)S(1)}, u32[]{:S(2)}, u32[]{:S(2)}) collective-permute-start(bf16[320,768]{1,0:T(8,128)(2,1)S(1)} %get-tuple-element.121), channel_id=1, source_target_pairs={{0,12},{1,13},{2,14},{3,15},{4,0},{5,1},{6,2},{7,3},{8,4},{9,5},{1... | collective-permute-start | bytes 1474568 | tf_op jit(solution)/shard_map/ppermute | solution.py:353
  25.9 13.7 %collective-permute-start.11 = (bf16[320,768]{1,0:T(8,128)(2,1)S(1)}, bf16[320,768]{1,0:T(8,128)(2,1)S(1)}, u32[]{:S(2)}, u32[]{:S(2)}) collective-permute-start(bf16[320,768]{1,0:T(8,128)(2,1)S(1)} %get-tuple-element.122), channel_id=1, source_target_pairs={{0,12},{1,13},{2,14},{3,15},{4,0},{5,1},{6,2},{7,3},{8,4},{9,5},{1... | collective-permute-start | bytes 1474568 | tf_op jit(solution)/shard_map/ppermute | solution.py:353
  32.3 11.3 %collective-permute-start.12 = (bf16[320,768]{1,0:T(8,128)(2,1)S(1)}, bf16[320,768]{1,0:T(8,128)(2,1)S(1)}, u32[]{:S(2)}, u32[]{:S(2)}) collective-permute-start(bf16[320,768]{1,0:T(8,128)(2,1)S(1)} %shard_map.61), channel_id=1, source_target_pairs={{0,12},{1,13},{2,14},{3,15},{4,0},{5,1},{6,2},{7,3},{8,4},{9,5},{1... | collective-permute-start | bytes 1474568 | tf_op jit(solution)/shard_map/ppermute | solution.py:353
  36.1 11.4 %collective-permute-start.9 = (bf16[320,768]{1,0:T(8,128)(2,1)S(1)}, bf16[320,768]{1,0:T(8,128)(2,1)S(1)}, u32[]{:S(2)}, u32[]{:S(2)}) collective-permute-start(bf16[320,768]{1,0:T(8,128)(2,1)S(1)} %slice.35), channel_id=1, source_target_pairs={{0,3},{1,0},{2,1},{3,2},{4,7},{5,4},{6,5},{7,6},{8,11},{9,8},{10,9... | collective-permute-start | bytes 1474568 | tf_op jit(solution)/shard_map/ppermute | solution.py:353
  39.5 10.1 %collective-permute-start.8 = (bf16[320,768]{1,0:T(8,128)(2,1)S(1)}, bf16[320,768]{1,0:T(8,128)(2,1)S(1)}, u32[]{:S(2)}, u32[]{:S(2)}) collective-permute-start(bf16[320,768]{1,0:T(8,128)(2,1)S(1)} %slice.34), channel_id=1, source_target_pairs={{0,1},{1,2},{2,3},{3,0},{4,5},{5,6},{6,7},{7,4},{8,9},{9,10},{10,1... | collective-permute-start | bytes 1474568 | tf_op jit(solution)/shard_map/ppermute | solution.py:353
  39.5 2.3 %collective-permute-start.13 = (f32[8,128]{1,0:T(8,128)S(1)}, f32[8,128]{1,0:T(8,128)S(1)}, u32[]{:S(2)}, u32[]{:S(2)}) collective-permute-start(f32[8,128]{1,0:T(8,128)S(1)} %get-tuple-element.124.over_a), channel_id=1, source_target_pairs={{0,16},{16,0},{1,17},{17,1},{2,18},{18,2},{3,19},{19,3},{4,20},{20... | collective-permute-start | bytes 12296 | tf_op jit(solution)/shard_map/ppermute | solution.py:369
  39.6 12.2 %collective-permute-start.14 = (bf16[320,768]{1,0:T(8,128)(2,1)S(1)}, bf16[320,768]{1,0:T(8,128)(2,1)S(1)}, u32[]{:S(2)}, u32[]{:S(2)}) collective-permute-start(bf16[320,768]{1,0:T(8,128)(2,1)S(1)} %collective-permute-done.11.z1b), channel_id=1, source_target_pairs={{0,12},{1,13},{2,14},{3,15},{4,0},{5,1},{6,2},{7,3},{8,4},{9,5},{1... | collective-permute-start | bytes 1474568 | tf_op jit(solution)/shard_map/ppermute | solution.py:353
  51.9 22.4 %copy-start = (bf16[512,768]{1,0:T(8,128)(2,1)S(1)}, bf16[512,768]{1,0:T(8,128)(2,1)}, u32[]{:S(2)}) copy-start(bf16[512,768]{1,0:T(8,128)(2,1)} %emb_ref.1) | copy-start | bytes 2359300
  51.9 22.4 %copy-start.2 = (s32[512]{0:T(512)S(1)}, s32[512]{0:T(512)}, u32[]{:S(2)}) copy-start(s32[512]{0:T(512)} %param.15) | copy-start | bytes 6148
  51.9 22.4 %copy-start.3 = (s32[512]{0:T(512)S(1)}, s32[512]{0:T(512)}, u32[]{:S(2)}) copy-start(s32[512]{0:T(512)} %param.12) | copy-start | bytes 6148
  51.9 22.4 %copy-start.4 = (s32[8]{0:T(128)S(1)}, s32[8]{0:T(128)}, u32[]{:S(2)}) copy-start(s32[8]{0:T(128)} %assign_ref.1) | copy-start | bytes 100
  54.6 18.3 %all-to-all-start.2 = ((f32[64,8,128]{2,1,0:T(8,128)}), f32[64,8,128]{2,1,0:T(8,128)S(1)}, u32[]{:S(2)}, u32[]{:S(2)}) async-start(f32[64,8,128]{2,1,0:T(8,128)} %bitcast.18), calls=%async_computation.2 | async-start | bytes 524288 | tf_op jit(solution)/shard_map/all_to_all | solution.py:434
  74.4 0.6 copy-start.5
